TPU v7x, 512 devices: a whole 4x8x8 slice. The times are simulated.
512 devices in a mesh: visit: 16 (over y, core), patch: 32 (over x, z).
Axes of the slice: x: 4, y: 8, z: 8, core: 2. Of those that a mesh axis runs over, the one named last changes fastest.
Arguments:
- blocks: bfloat16 [16, 512, 128, 128], P('visit', 'patch'), may hold values from -6 to 6
- inv_variance: bfloat16 [16, 512, 128, 128], P('visit', 'patch'), may hold values from 0.0099487305 to 1
- destinations: int32 [16, 512, 2], P('visit', 'patch'), may hold values from 0 to 31, all different within a row; in each aligned block of 16 rows (0 to 15, 16 to 31, ..., all dimensions but the last counted through in order) at most 2 rows name the same one
- offsets: int32 [16, 512, 2, 2], P('visit', 'patch'), may hold values from 0 to 384
- coefficients: float32 [16, 512, 15], P('visit', 'patch'), may hold values from -3 to 3
- basis_rows: bfloat16 [5, 41], replicated, may hold values from -2 to 2
- basis_cols: bfloat16 [5, 41], replicated, may hold values from -2 to 2
Outputs:
- coadd: float32 [32, 512, 512], P('patch', 'visit')
Inputs may be any that keep to these rules, and one draw needn't show every extreme that they name: `destinations`: the two patches of a block differ. Among the 16 blocks of one device no patch is named more than 2 times, a bound that some block reaches.
All inputs are finite; a program needn't handle non-finite values.
Results may differ from a plain program's by a relative error of at most 0.014.
Values may be sent and summed in bfloat16 or wider, within the bound.
No kernel may reach another device: no remote copies, remote signals or barrier semaphores. Data moves between devices by JAX's collectives and lax.ppermute only.
A program may use at most 64 MiB of HBM per device.

v0:
```python
import jax
import jax.numpy as jnp
from jax import lax
from jax.sharding import PartitionSpec as P

P_SIZE = 512


def band_tables(kernel_taps, block_side):
    half_width = (kernel_taps.shape[1] - 1) // 2
    pixels = jnp.arange(block_side, dtype=jnp.int32)
    lag_index = pixels[:, None] - pixels[None, :] + half_width
    which = jnp.arange(kernel_taps.shape[1], dtype=jnp.int32)
    onehot = (lag_index[None, :, :] == which[:, None, None]).astype(jnp.float32)
    return jnp.einsum(
        "kt,tab->kab", kernel_taps.astype(jnp.float32), onehot, precision=lax.Precision.HIGHEST
    )


def match_group(group_blocks, group_coef, row_flat, col_table):
    block_count, block_side = (group_blocks.shape[0], group_blocks.shape[1])
    basis_count = col_table.shape[0]
    across = jnp.einsum("mab,bn->man", group_blocks, row_flat, preferred_element_type=jnp.float32)
    across = across.reshape(block_count, block_side, basis_count, block_side)
    basis_images = jnp.einsum(
        "kab,mbkc->mkac",
        col_table,
        across,
        precision=lax.Precision.HIGHEST,
        preferred_element_type=jnp.float32,
    )
    coords = (jnp.arange(block_side, dtype=jnp.float32) - (block_side - 1) / 2.0) / block_side
    weights_three = group_coef.reshape(block_count, basis_count, 3)
    spatial = (
        weights_three[:, :, 0, None, None]
        + weights_three[:, :, 1, None, None] * coords[:, None]
        + weights_three[:, :, 2, None, None] * coords[None, :]
    )
    return jnp.sum(spatial * basis_images, axis=1).astype(jnp.bfloat16)


def match_blocks(flat_blocks, flat_coef, row_flat, col_table):
    block_count, block_side = (flat_blocks.shape[0], flat_blocks.shape[1])
    group_size = max((d for d in range(1, 9) if block_count % d == 0))
    grouped = (
        flat_blocks.reshape(-1, group_size, block_side, block_side),
        flat_coef.reshape(-1, group_size, flat_coef.shape[-1]),
    )
    matched = lax.map(lambda pair: match_group(pair[0], pair[1], row_flat, col_table), grouped)
    return matched.reshape(block_count, block_side, block_side)


def place_slots(terms, corners, canvas_side):
    slot_total, block_side = (terms.shape[0], terms.shape[-1])
    zero_index = jnp.int32(0)

    def place_one(index, canvas):
        row_start = corners[index, 0]
        col_start = corners[index, 1]
        window = lax.dynamic_slice(
            canvas, (zero_index, row_start, col_start), (2, block_side, block_side)
        )
        return lax.dynamic_update_slice(
            canvas, window + terms[index], (zero_index, row_start, col_start)
        )

    canvas = jnp.zeros((2, canvas_side, canvas_side), jnp.float32)
    return lax.fori_loop(0, slot_total, place_one, canvas)


def body(blocks, inv_variance, destinations, offsets, coefficients, basis_rows, basis_cols):
    block_side = blocks.shape[-1]
    owners = lax.axis_size("patch")
    block_count = blocks.shape[1]
    per_owner = max(2, 4 * block_count // owners)
    row_table = band_tables(basis_rows, block_side)
    row_flat = jnp.transpose(row_table, (1, 0, 2)).reshape(block_side, -1).astype(jnp.bfloat16)
    col_table = jnp.transpose(band_tables(basis_cols, block_side), (0, 2, 1))
    own_blocks = blocks[0]
    own_ivar = inv_variance[0]
    own_coef = coefficients[0]
    pieces = destinations[0].reshape(-1)
    onehot = (pieces[:, None] == jnp.arange(owners, dtype=jnp.int32)[None, :]).astype(jnp.int32)
    before = jnp.cumsum(onehot, axis=0) - onehot
    place = jnp.sum(before * onehot, axis=1)
    target = pieces * per_owner + place
    source = jnp.arange(2 * block_count, dtype=jnp.int32) // 2
    slot_count = owners * per_owner

    def pack_slots(values):
        packed = jnp.zeros((slot_count,) + values.shape[1:], values.dtype).at[target].set(values)
        return packed.reshape((owners, per_owner) + values.shape[1:])

    piece_offsets = pack_slots(offsets[0].reshape(-1, 2))
    got_blocks = lax.all_to_all(
        pack_slots(own_blocks[source]), "patch", split_axis=0, concat_axis=0, tiled=True
    )
    got_ivar = lax.all_to_all(
        pack_slots(own_ivar[source]), "patch", split_axis=0, concat_axis=0, tiled=True
    )
    got_coef = lax.all_to_all(
        pack_slots(own_coef[source]).astype(jnp.bfloat16),
        "patch",
        split_axis=0,
        concat_axis=0,
        tiled=True,
    ).astype(jnp.float32)
    got_off = lax.all_to_all(piece_offsets, "patch", split_axis=0, concat_axis=0, tiled=True)
    leading = got_blocks.shape[:2]
    flat_blocks = got_blocks.reshape((-1, block_side, block_side))
    flat_coef = got_coef.reshape((flat_blocks.shape[0], -1))
    matched_flat = match_blocks(flat_blocks, flat_coef, row_flat, col_table)
    matched = matched_flat.reshape(leading + (block_side, block_side))
    flat_off = got_off.reshape(-1, 2).astype(jnp.int32)
    weight = got_ivar.reshape(-1, block_side, block_side).astype(jnp.float32)
    num_term = matched.reshape(-1, block_side, block_side).astype(jnp.float32) * weight
    stacked_terms = jnp.stack((num_term, weight), axis=1)
    canvas = place_slots(stacked_terms, flat_off, P_SIZE)
    numerator = canvas[0]
    denominator = canvas[1]
    numerator, denominator = lax.psum((numerator, denominator), "visit")
    share_rows = P_SIZE // lax.axis_size("visit")
    first_row = lax.axis_index("visit") * share_rows
    numerator = lax.dynamic_slice_in_dim(numerator, first_row, share_rows, 0)
    denominator = lax.dynamic_slice_in_dim(denominator, first_row, share_rows, 0)
    return (numerator / jnp.maximum(denominator, 1.0))[None]


def solution(mesh):
    return jax.shard_map(
        body,
        mesh=mesh,
        in_specs=(
            P("visit", "patch", None, None),
            P("visit", "patch", None, None),
            P("visit", "patch", None),
            P("visit", "patch", None, None),
            P("visit", "patch", None),
            P(),
            P(),
        ),
        out_specs=P("patch", "visit", None),
        check_vma=False,
    )
```

profile of v0, /device:TPU:1, one launch (start us, length us, event | category | flops | bytes accessed | tf_op | source)
XLA Modules:
  0.0 808.8 jit_solution(9206711526869845402)
XLA Ops:
  11.0 13.7 %all-to-all-start = ((s32[32,2,2]{1,2,0:T(2,128)}), s32[32,2,2]{1,2,0:T(2,128)S(1)}, u32[]{:S(2)}, u32[]{:S(2)}) async-start(s32[32,2,2]{1,2,0:T(2,128)} %copy.46), calls=%async_computation | async-start | bytes 65536 | tf_op jit(solution)/shard_map/all_to_all | solution.py:108
  26.9 6.6 all-to-all-done
  33.5 3.8 all-to-all-start.1
  39.9 4.6 scatter_fusion
  45.9 8.0 all-to-all-start.2
  57.8 3.6 scatter_fusion.1
  61.6 41.1 %all-to-all-done.2 = bf16[32,2,128,128]{3,2,1,0:T(8,128)(2,1)} async-done(((bf16[32,2,128,128]{3,2,1,0:T(8,128)(2,1)}), bf16[32,2,128,128]{3,2,1,0:T(8,128)(2,1)}, u32[]{:S(2)}, u32[]{:S(2)}) %all-to-all-start.2) | async-done | bytes 2097184 | tf_op jit(solution)/shard_map/all_to_all | solution.py:95
  102.7 5.3 all-to-all-start.3
  108.2 39.6 %while.25 = (s32[]{:T(128)}, bf16[8,8,128,128]{2,3,1,0:T(8,128)(2,1)}, f32[8,8,15]{2,1,0:T(8,128)S(1)}, bf16[8,8,128,128]{3,2,1,0:T(8,128)(2,1)}, bf16[128,640]{...) while((s32[]{:T(128)}, bf16[8,8,128,128]{2,3,1,0:T(8,128)(2,1)}, f32[8,8,15]{2,1,0:T(8,128)S(1)}, ...), condition=%wide.region_7.8_spmd, body=%wide.region_5.7_spmd.sunk | while | flops 1176255744 | bytes 6872305 | solution.py:49
  110.0 2.5 fusion.39
  114.9 2.5 fusion.39
  119.8 2.5 fusion.39
  124.8 2.5 fusion.39
  129.7 2.5 fusion.39
  134.7 2.5 fusion.39
  139.6 2.5 fusion.39
  144.6 2.5 fusion.39
  147.9 4.1 copy.52
  151.9 4.3 all-to-all-done.3
  159.1 3.8 pad_maximum_fusion
  163.2 489.1 %while.26 = (s32[]{:T(128)}, f32[2,512,512]{2,1,0:T(8,128)S(1)}, s32[64,2]{0,1:T(2,128)S(1)}, f32[64,2,128,128]{3,2,1,0:T(8,128)}, s32[]{:T(128)}, /*index=5*/s32[]{:T(128)}, s32[]{:T(128)}) while((s32[]{:T(128)}, f32[2,512,512]{2,1,0:T(8,128)S(1)}, s32[64,2]{0,1:T(2,128)S(1)}, f32[64,2,128,128]{3,2,1,0:T(8,128)}, s32[]{:T(128)}, ...), condition=%wide.region_10.11_spmd, body=%wide.region_9.10_spmd.sunk | while | flops 32776 | bytes 655541 | solution.py:68
  581.3 2.5 dynamic_update_slice.18
  612.1 2.5 dynamic_update_slice.18
  653.8 146.6 %all-reduce.3.cloned.1.call-done = (f32[512,512]{1,0:T(8,128)}, f32[512,512]{1,0:T(8,128)}) async-done(((f32[512,512]{1,0:T(8,128)}, f32[512,512]{1,0:T(8,128)}), (f32[512,512]{1,0:T(8,128)}, f32[512,512]{1,0:T(8,128)})) %all-reduce.3.cloned.1.call-update) | async-done | bytes 2097168 | tf_op jit(solution)/shard_map/psum | solution.py:121
  (319 shorter events, 271.7 us)
Async XLA Ops:
  6.5 30.7 %copy-start = (bf16[1,16,128,128]{3,2,1,0:T(8,128)(2,1)S(1)}, bf16[1,16,128,128]{3,2,1,0:T(8,128)(2,1)}, u32[]{:S(2)}) copy-start(bf16[1,16,128,128]{3,2,1,0:T(8,128)(2,1)} %param.11) | copy-start | bytes 1572868
  11.0 22.5 %all-to-all-start = ((s32[32,2,2]{1,2,0:T(2,128)}), s32[32,2,2]{1,2,0:T(2,128)S(1)}, u32[]{:S(2)}, u32[]{:S(2)}) async-start(s32[32,2,2]{1,2,0:T(2,128)} %copy.46), calls=%async_computation | async-start | bytes 65536 | tf_op jit(solution)/shard_map/all_to_all | solution.py:108
  33.5 12.4 %all-to-all-start.1 = ((bf16[32,2,15]{2,1,0:T(2,128)(2,1)}), bf16[32,2,15]{2,1,0:T(2,128)(2,1)S(1)}, u32[]{:S(2)}, u32[]{:S(2)}) async-start(bf16[32,2,15]{2,1,0:T(2,128)(2,1)} %bitcast.25), calls=%async_computation.1 | async-start | bytes 32768 | tf_op jit(solution)/shard_map/all_to_all | solution.py:101
  44.4 9.5 %copy-start.4 = (bf16[5,41]{1,0:T(8,128)(2,1)S(1)}, bf16[5,41]{1,0:T(8,128)(2,1)}, u32[]{:S(2)}) copy-start(bf16[5,41]{1,0:T(8,128)(2,1)} %param.17) | copy-start | bytes 1234
  45.9 8.9 %copy-start.5 = (bf16[5,41]{1,0:T(8,128)(2,1)S(1)}, bf16[5,41]{1,0:T(8,128)(2,1)}, u32[]{:S(2)}) copy-start(bf16[5,41]{1,0:T(8,128)(2,1)} %param.16) | copy-start | bytes 1234
  45.9 9.8 %copy-start.3 = (bf16[1,16,128,128]{3,2,1,0:T(8,128)(2,1)S(1)}, bf16[1,16,128,128]{3,2,1,0:T(8,128)(2,1)}, u32[]{:S(2)}) copy-start(bf16[1,16,128,128]{3,2,1,0:T(8,128)(2,1)} %param.12) | copy-start | bytes 1572868
  45.9 56.7 %all-to-all-start.2 = ((bf16[32,2,128,128]{3,2,1,0:T(8,128)(2,1)}), bf16[32,2,128,128]{3,2,1,0:T(8,128)(2,1)}, u32[]{:S(2)}, u32[]{:S(2)}) async-start(bf16[32,2,128,128]{3,2,1,0:T(8,128)(2,1)} %bitcast.28), calls=%async_computation.2 | async-start | bytes 4194304 | tf_op jit(solution)/shard_map/all_to_all | solution.py:95
  61.4 41.2 %copy-start.2 = (bf16[64,128,128]{2,1,0:T(8,128)(2,1)}, bf16[64,128,128]{2,1,0:T(8,128)(2,1)S(1)}, u32[]{:S(2)}) copy-start(bf16[64,128,128]{2,1,0:T(8,128)(2,1)S(1)} %scatter_fusion.1) | copy-start | bytes 6291460
  102.7 53.6 %all-to-all-start.3 = ((bf16[32,2,128,128]{3,2,1,0:T(8,128)(2,1)}), bf16[32,2,128,128]{3,2,1,0:T(8,128)(2,1)S(1)}, u32[]{:S(2)}, u32[]{:S(2)}) async-start(bf16[32,2,128,128]{3,2,1,0:T(8,128)(2,1)} %bitcast.111), calls=%async_computation.3 | async-start | bytes 4194304 | tf_op jit(solution)/shard_map/all_to_all | solution.py:98
  108.0 692.4 %all-reduce.3.cloned.1.call-start = ((), (), s32[]{:S(2)}) async-start(), calls=%async_computation.4 | async-start | bytes 4194304 | tf_op jit(solution)/shard_map/psum | solution.py:121
  156.3 2.2 copy-start.1
Sparse Core Ops, SparseCore 0:
  653.9 146.4 all-reduce.2
where the time goes:
time: 815 us; the launch traced here: 809 us
  loops' own time  253 us (31%)
  local copies, waits for them, and re-layouts  204 us (25%)
  waiting for transfers between devices  200 us (25%)
  other arithmetic  74 us (9%)
  matrix products  33.1 us (4%)
  starting transfers between devices  31.1 us (4%)
  between operations  13.6 us (2%)
    another operation x1, loops' own time, place_slots(): return lax.fori_loop(0, slot_total, place_one, canvas)  252 us
    psum x1, waiting for transfers between devices, body(): numerator, denominator = lax.psum((numerator, denominator), 'visit')  147 us
    dynamic_update_slice x64, local copies, waits for them, and re-layouts, place_one(): lax.dynamic_update_slice(canvas, window + terms[index], (zero_index, row_...  130 us
    add x64, other arithmetic, place_one(): window + terms[index]  65.1 us
    dynamic_slice x64, local copies, waits for them, and re-layouts, place_one(): col_start = corners[index, 1]  41.6 us
    all_to_all x1, waiting for transfers between devices, body(): lax.all_to_all(pack_slots(own_blocks[source]), 'patch', split_axis=0, con...  41.1 us
    dot_general x8, matrix products, match_group(): jnp.einsum('kab,mbkc->mkac', col_table, across, precision=lax.Precision.H...  20.2 us
  transfers between devices with their start and end apart: 5, of which 5 were waited for; matrix products, arithmetic and copies ran while one was open for 7% of the time, Pallas kernels for 0%

commit v1 on v0

v1 whole, which is shorter than its diff:
```python
import functools

import jax
import jax.numpy as jnp
from jax import lax
from jax.experimental import pallas as pl
from jax.experimental.pallas import tpu as pltpu
from jax.sharding import Mesh
from jax.sharding import PartitionSpec as P

S = 128
P_SIZE = 512
TAPS = 41
HALF = (TAPS - 1) // 2
BASIS = 5
BAND = 32
LANES = 128
META = 16
LEAD = 4
STAGE = 7 * BAND


def match_kernel(coef_ref, taps_ref, blocks_ref, out_ref, rows_tab, cols_tab, stack):
    row_id = lax.broadcasted_iota(jnp.int32, (S, S), 0)
    col_id = lax.broadcasted_iota(jnp.int32, (S, S), 1)
    inside = jnp.abs(row_id - col_id) <= HALF
    for k in range(BASIS):
        for which, table in ((0, rows_tab), (1, cols_tab)):
            taps = jnp.broadcast_to(taps_ref[which * 8 + k : which * 8 + k + 1, :], (8, S))
            band = jnp.concatenate(
                [pltpu.roll(taps, (S - HALF - LEAD + row) % S, 1, stride=1, stride_axis=0) for row in range(0, S, 8)]
            )
            table[:, k * S : (k + 1) * S] = jnp.where(inside, band, 0.0).astype(jnp.bfloat16)
    y = (lax.broadcasted_iota(jnp.int32, (S, 1), 0).astype(jnp.float32) - (S - 1) / 2.0) / S
    x = (lax.broadcasted_iota(jnp.int32, (1, S), 1).astype(jnp.float32) - (S - 1) / 2.0) / S

    def one(i, carry):
        across = jnp.dot(blocks_ref[i], rows_tab[...], preferred_element_type=jnp.float32)
        for k in range(BASIS):
            part = across[:, k * S : (k + 1) * S]
            plain = coef_ref[i, 3 * k] + coef_ref[i, 3 * k + 2] * x
            for at, value in ((0, part * plain), (S, part * coef_ref[i, 3 * k + 1])):
                upper = value.astype(jnp.bfloat16)
                lower = (value - upper.astype(jnp.float32)).astype(jnp.bfloat16)
                stack[k * S : (k + 1) * S, at : at + S] = upper
                stack[k * S : (k + 1) * S, 2 * S + at : 3 * S + at] = lower
        sums = jnp.dot(cols_tab[...], stack[...], preferred_element_type=jnp.float32)
        sums = sums[:, 0 : 2 * S] + sums[:, 2 * S : 4 * S]
        out_ref[i] = (sums[:, 0:S] + y * sums[:, S : 2 * S]).astype(jnp.bfloat16)
        return carry

    lax.fori_loop(0, blocks_ref.shape[0], one, 0)


def match(blocks, coefficients, basis_rows, basis_cols):
    rows = jnp.pad(basis_rows[:, ::-1].astype(jnp.float32), ((0, 8 - BASIS), (LEAD, S - TAPS - LEAD)))
    cols = jnp.pad(basis_cols.astype(jnp.float32), ((0, 8 - BASIS), (LEAD, S - TAPS - LEAD)))
    vmem = pl.BlockSpec(memory_space=pltpu.VMEM)
    return pl.pallas_call(
        match_kernel,
        out_shape=jax.ShapeDtypeStruct(blocks.shape, jnp.bfloat16),
        in_specs=[pl.BlockSpec(memory_space=pltpu.SMEM), vmem, vmem],
        out_specs=vmem,
        scratch_shapes=[
            pltpu.VMEM((S, BASIS * S), jnp.bfloat16),
            pltpu.VMEM((S, BASIS * S), jnp.bfloat16),
            pltpu.VMEM((BASIS * S, 4 * S), jnp.bfloat16),
        ],
        compiler_params=pltpu.CompilerParams(vmem_limit_bytes=32 * 2**20),
        cost_estimate=pl.CostEstimate(flops=2**30, bytes_accessed=2**20, transcendentals=0),
        name="match",
    )(coefficients, jnp.concatenate([rows, cols]), blocks)


def place_kernel(with_matched, meta_ref, where_ref, weight_ref, *refs):
    if with_matched:
        matched_ref, out_ref, canvas, stage = refs
    else:
        out_ref, canvas, stage = refs
    mine, core = where_ref[0], where_ref[1]
    sources = weight_ref.shape[0]
    count = weight_ref.shape[1] // S
    canvas[...] = jnp.zeros_like(canvas)
    stage[...] = jnp.zeros_like(stage)
    lane = lax.broadcasted_iota(jnp.int32, (S, LANES), 1)

    def one(index, carry):
        source, block = index // count, lax.rem(index, count)
        for n in range(2):
            base = index * 10 + 5 * n
            patch = meta_ref[base]

            @pl.when(patch // 8 == mine)
            def add():
                row = meta_ref[base + 1] * LANES + meta_ref[base + 2]
                tile, shift = meta_ref[base + 3], meta_ref[base + 4]
                value = weight_ref[source, pl.ds(pl.multiple_of(block * S, S), S), :].astype(jnp.float32)
                if with_matched:
                    value = value * matched_ref[source, block].astype(jnp.float32)
                value = pltpu.roll(value, shift, 1)
                stage[0, BAND : BAND + S, :] = jnp.where(lane >= shift, value, 0.0)
                stage[1, BAND : BAND + S, :] = jnp.where(lane >= shift, 0.0, value)
                first, within = row // BAND, lax.rem(row, BAND)
                odd = lax.rem(first + core, 2)

                def band(step):
                    start = BAND + BAND * step - within
                    spot = lax.rem(patch, 8) * (P_SIZE // 2) + (first + step) // 2 * BAND
                    spot = pl.multiple_of(spot, BAND)
                    for side in range(2):
                        canvas[tile + side, pl.ds(spot, BAND), :] += stage[side, pl.ds(start, BAND), :]

                band(odd)
                band(odd + 2)

                @pl.when((odd == 0) & (within > 0))
                def last():
                    band(4)

        return carry

    lax.fori_loop(0, sources * count, one, 0)
    for tile in range(P_SIZE // LANES):
        out_ref[:, tile * LANES : (tile + 1) * LANES] = canvas[tile].astype(jnp.bfloat16)


def place(meta, where, weight, matched=None):
    patches, rows = 8, P_SIZE // 2
    vmem = pl.BlockSpec(memory_space=pltpu.VMEM)
    smem = pl.BlockSpec(memory_space=pltpu.SMEM)
    operands = (meta, where, weight) if matched is None else (meta, where, weight, matched)
    out = pl.pallas_call(
        functools.partial(place_kernel, matched is not None),
        out_shape=jax.ShapeDtypeStruct((patches * rows, P_SIZE), jnp.bfloat16),
        in_specs=[smem, smem] + [vmem] * (len(operands) - 2),
        out_specs=vmem,
        scratch_shapes=[
            pltpu.VMEM((P_SIZE // LANES + 1, patches * rows, LANES), jnp.float32),
            pltpu.VMEM((2, STAGE, LANES), jnp.float32),
        ],
        compiler_params=pltpu.CompilerParams(vmem_limit_bytes=40 * 2**20),
        cost_estimate=pl.CostEstimate(flops=2**24, bytes_accessed=2**23, transcendentals=0),
        name="place_num" if matched is not None else "place_den",
    )(*operands)
    return out.reshape(patches, rows, P_SIZE)


def body(blocks, inv_variance, destinations, offsets, coefficients, basis_rows, basis_cols):
    count = blocks.shape[1]
    place_of = jnp.concatenate(
        [destinations[0][:, :, None], jnp.stack([offsets[0] // LANES, offsets[0] % LANES], -1).reshape(count, 2, 4)], -1
    )
    lines = jnp.pad(place_of.reshape(count, 10).astype(jnp.bfloat16), ((0, META - count), (0, S - 10)))
    weight = jnp.concatenate([inv_variance[0].reshape(count * S, S), lines])
    weight = lax.all_gather(weight, ("core", "x"))
    matched = match(blocks[0], coefficients[0], basis_rows, basis_cols)
    matched = lax.all_gather(matched, ("core", "x"))

    meta = weight[:, count * S : count * S + count, :10].astype(jnp.int32).reshape(-1)
    where = jnp.stack([lax.axis_index("x"), lax.axis_index("core")]).astype(jnp.int32)
    den = place(meta, where, weight)
    den = lax.psum_scatter(den, "z", scatter_dimension=0, tiled=True)
    num = place(meta, where, weight, matched)
    num = lax.psum_scatter(num, "z", scatter_dimension=0, tiled=True)

    both = jnp.stack([num.reshape(8, BAND, P_SIZE), den.reshape(8, BAND, P_SIZE)], 1)
    both = lax.all_to_all(both, "y", 0, 0, tiled=True)
    both = jnp.sum(both.astype(jnp.float32), axis=0)
    return (both[0] / jnp.maximum(both[1], 1.0))[None]


def solution(mesh):
    visits = mesh.shape["visit"]
    grid = Mesh(mesh.devices.reshape(visits // 2, 2, 4, mesh.shape["patch"] // 4), ("y", "core", "x", "z"))
    visit, patch = ("y", "core"), ("x", "z")
    return jax.shard_map(
        body,
        mesh=grid,
        in_specs=(
            P(visit, patch, None, None),
            P(visit, patch, None, None),
            P(visit, patch, None),
            P(visit, patch, None, None),
            P(visit, patch, None),
            P(),
            P(),
        ),
        out_specs=P(patch, visit, None),
        check_vma=False,
    )
```

time: 815 us -> 231 us (0.28)
  the two profiles are of different devices: /device:TPU:1 before, /device:TPU:2 now
where the time goes in v1:
time: 231 us
  waiting for transfers between devices  144 us (62%)
  Pallas kernels  37.7 us (16%)
  blocking collectives  19.9 us (9%)
  between operations  13.2 us (6%)
  local copies, waits for them, and re-layouts  9.4 us (4%)
  other arithmetic  6.71 us (3%)
    reduce_scatter x1, waiting for transfers between devices, body(): den = lax.psum_scatter(den, 'z', scatter_dimension=0, tiled=True)  46.4 us
    all_gather x1, waiting for transfers between devices, body(): matched = lax.all_gather(matched, ('core', 'x'))  38.7 us
    reduce_scatter x1, waiting for transfers between devices, body(): num = lax.psum_scatter(num, 'z', scatter_dimension=0, tiled=True)  31.3 us
    all_gather x1, waiting for transfers between devices, body(): weight = lax.all_gather(weight, ('core', 'x'))  27.3 us
    pallas_call x2, Pallas kernels, place(): pl.pallas_call(functools.partial(place_kernel, matched is not None), out_...  27.2 us
    all_to_all x1, blocking collectives, body(): both = lax.all_to_all(both, 'y', 0, 0, tiled=True)  19.9 us
    pallas_call x1, Pallas kernels, match(): pl.pallas_call(match_kernel, out_shape=jax.ShapeDtypeStruct(blocks.shape,...  10.6 us
    unnamed x10, local copies, waits for them, and re-layouts  8.48 us
  transfers between devices with their start and end apart: 4, of which 4 were waited for; matrix products, arithmetic and copies ran while one was open for 1% of the time, Pallas kernels for 10%

profile of v1, /device:TPU:2, one launch (start us, length us, event | category | flops | bytes accessed | tf_op | source)
XLA Modules:
  0.0 230.8 jit_solution(9691634390752631776)
XLA Ops:
  6.5 0.7 convert_bitcast_fusion
  7.2 0.7 fusion.8
  8.0 0.1 copy.20
  8.1 1.9 fusion.1
  10.1 0.8 rev.3
  10.8 0.8 copy.19
  11.6 0.8 fusion.6.taps_ref
  12.4 1.0 copy-done.3
  13.4 10.6 %match.1 = bf16[16,128,128]{2,1,0:T(8,128)(2,1)} custom-call(f32[16,15]{1,0:T(8,128)S(1)} %bitcast.42, f32[16,128]{1,0:T(8,128)S(1)} %fusion.6.taps_ref, bf16[16,128,128]{2,1,0:T(8,128)(2,1)S(1)} %bitcast.43), custom_call_target="tpu_custom_call" | custom-call | flops 1073741824 | bytes 1048576 | tf_op jit(solution)/shard_map/match/pallas_call | solution.py:59
  24.0 0.1 pad_add_fusion.where_ref
  24.1 27.3 %all-gather.5.cloned.1.call-done = bf16[16512,128]{1,0:T(8,128)(2,1)} async-done(((bf16[2064,128]{1,0:T(8,128)(2,1)}), bf16[16512,128]{1,0:T(8,128)(2,1)}) %all-gather.5.cloned.1.call-update) | async-done | bytes 4227088 | tf_op jit(solution)/shard_map/all_gather | solution.py:155
  51.4 0.8 slice_convert_fusion
  52.2 0.1 reshape.125.meta_ref
  52.3 38.7 %all-gather.7.cloned.1.call-done = bf16[128,128,128]{2,1,0:T(8,128)(2,1)} async-done(((bf16[16,128,128]{2,1,0:T(8,128)(2,1)}), bf16[128,128,128]{2,1,0:T(8,128)(2,1)}) %all-gather.7.cloned.1.call-update) | async-done | bytes 4194320 | tf_op jit(solution)/shard_map/all_gather | solution.py:157
  91.0 2.2 copy-done
  93.2 2.2 copy-done.2
  95.4 13.9 %place_num.1 = bf16[2048,512]{1,0:T(8,128)(2,1)} custom-call(s32[1280]{0:T(1024)S(1)} %reshape.125.meta_ref, s32[2]{0:T(128)S(1)} %pad_add_fusion.where_ref, bf16[8,2064,128]{2,1,0:T(8,128)(2,1)S(1)} %bitcast.39, bf16[8,16,128,128]{3,2,1,0:T(8,128)(2,1)S(1)} %bitcast.41), custom_call_target="tpu_custom_call" | custom-call | flops 16777216 | bytes 8388608 | tf_op jit(solution)/shard_map/place_num/pallas_call | solution.py:132
  109.3 2.2 copy-done.1
  111.5 13.3 %place_den.1 = bf16[2048,512]{1,0:T(8,128)(2,1)} custom-call(s32[1280]{0:T(1024)S(1)} %reshape.125.meta_ref, s32[2]{0:T(128)S(1)} %pad_add_fusion.where_ref, bf16[8,2064,128]{2,1,0:T(8,128)(2,1)S(1)} %bitcast.40), custom_call_target="tpu_custom_call" | custom-call | flops 16777216 | bytes 8388608 | tf_op jit(solution)/shard_map/place_den/pallas_call | solution.py:132
  124.9 31.3 %reduce-scatter.3.cloned.1.call-done = bf16[1,256,512]{2,1,0:T(8,128)(2,1)} async-done(((bf16[8,256,512]{2,1,0:T(8,128)(2,1)}), bf16[1,256,512]{2,1,0:T(8,128)(2,1)}) %reduce-scatter.3.cloned.1.call-update) | async-done | bytes 262160 | tf_op jit(solution)/shard_map/reduce_scatter | solution.py:164
  156.2 46.4 %reduce-scatter.5.cloned.1.call-done = bf16[1,256,512]{2,1,0:T(8,128)(2,1)} async-done(((bf16[8,256,512]{2,1,0:T(8,128)(2,1)}), bf16[1,256,512]{2,1,0:T(8,128)(2,1)}) %reduce-scatter.5.cloned.1.call-update) | async-done | bytes 262160 | tf_op jit(solution)/shard_map/reduce_scatter | solution.py:162
  202.6 1.1 pad_maximum_fusion
  203.6 19.9 %all_to_all.5 = bf16[8,2,32,512]{3,2,1,0:T(8,128)(2,1)S(1)} all-to-all(bf16[8,2,32,512]{3,2,1,0:T(8,128)(2,1)S(1)} %pad_maximum_fusion), channel_id=1, replica_groups=mesh['y'=8,'core'=2,'x'=4,'z'=8] {'y'}, dimensions={0} | all-to-all | bytes 1048576 | tf_op jit(solution)/shard_map/all_to_all | solution.py:167
  223.6 0.6 fusion.2
  (18 shorter events, 0.3 us)
Async XLA Ops:
  6.5 44.9 %all-gather.5.cloned.1.call-start = ((), (), s32[]{:S(2)}) async-start(), calls=%async_computation.5 | async-start | bytes 4755456 | tf_op jit(solution)/shard_map/all_gather | solution.py:155
  10.0 81.0 %all-gather.7.cloned.1.call-start = ((), (), s32[]{:S(2)}) async-start(), calls=%async_computation.6 | async-start | bytes 4718592 | tf_op jit(solution)/shard_map/all_gather | solution.py:157
  12.4 1.0 copy-start.3
  24.0 132.2 %reduce-scatter.3.cloned.1.call-start = ((), (), s32[]{:S(2)}) async-start(), calls=%async_computation.3 | async-start | bytes 2359296 | tf_op jit(solution)/shard_map/reduce_scatter | solution.py:164
  91.0 2.2 copy-start
  93.2 2.2 copy-start.2
  109.3 93.3 %reduce-scatter.5.cloned.1.call-start = ((), (), s32[]{:S(2)}) async-start(), calls=%async_computation.4 | async-start | bytes 2359296 | tf_op jit(solution)/shard_map/reduce_scatter | solution.py:162
  109.3 2.2 copy-start.1
Sparse Core Ops, SparseCore 0:
  10.1 41.1 all-gather.4
  53.5 37.4 all-gather.6
  109.4 46.7 reduce-scatter.2
  158.9 43.6 reduce-scatter.4

commit v2 on v1

v2 whole, which is shorter than its diff:
```python
import functools

import jax
import jax.numpy as jnp
from jax import lax
from jax.experimental import pallas as pl
from jax.experimental.pallas import tpu as pltpu
from jax.sharding import Mesh
from jax.sharding import PartitionSpec as P

S = 128
P_SIZE = 512
TAPS = 41
HALF = (TAPS - 1) // 2
BASIS = 5
BAND = 32
LANES = 128
META = 16
LEAD = 4
STAGE = 7 * BAND


def match_kernel(coef_ref, taps_ref, blocks_ref, weight_ref, out_ref, rows_tab, cols_tab, stack):
    row_id = lax.broadcasted_iota(jnp.int32, (S, S), 0)
    col_id = lax.broadcasted_iota(jnp.int32, (S, S), 1)
    inside = jnp.abs(row_id - col_id) <= HALF
    for k in range(BASIS):
        for which, table in ((0, rows_tab), (1, cols_tab)):
            taps = jnp.broadcast_to(taps_ref[which * 8 + k : which * 8 + k + 1, :], (8, S))
            band = jnp.concatenate(
                [pltpu.roll(taps, (S - HALF - LEAD + row) % S, 1, stride=1, stride_axis=0) for row in range(0, S, 8)]
            )
            table[:, k * S : (k + 1) * S] = jnp.where(inside, band, 0.0).astype(jnp.bfloat16)
    y = (lax.broadcasted_iota(jnp.int32, (S, 1), 0).astype(jnp.float32) - (S - 1) / 2.0) / S
    x = (lax.broadcasted_iota(jnp.int32, (1, S), 1).astype(jnp.float32) - (S - 1) / 2.0) / S

    def one(i, carry):
        across = jnp.dot(blocks_ref[i], rows_tab[...], preferred_element_type=jnp.float32)
        for k in range(BASIS):
            part = across[:, k * S : (k + 1) * S]
            plain = coef_ref[i, 3 * k] + coef_ref[i, 3 * k + 2] * x
            for at, value in ((0, part * plain), (S, part * coef_ref[i, 3 * k + 1])):
                upper = value.astype(jnp.bfloat16)
                lower = (value - upper.astype(jnp.float32)).astype(jnp.bfloat16)
                stack[k * S : (k + 1) * S, at : at + S] = upper
                stack[k * S : (k + 1) * S, 2 * S + at : 3 * S + at] = lower
        sums = jnp.dot(cols_tab[...], stack[...], preferred_element_type=jnp.float32)
        sums = sums[:, 0 : 2 * S] + sums[:, 2 * S : 4 * S]
        matched = sums[:, 0:S] + y * sums[:, S : 2 * S]
        term = matched * weight_ref[i].astype(jnp.float32)
        out_ref[pl.ds(pl.multiple_of(i * S, S), S), :] = term.astype(jnp.bfloat16)
        return carry

    lax.fori_loop(0, blocks_ref.shape[0], one, 0)


def match(blocks, weight, coefficients, basis_rows, basis_cols):
    rows = jnp.pad(basis_rows[:, ::-1].astype(jnp.float32), ((0, 8 - BASIS), (LEAD, S - TAPS - LEAD)))
    cols = jnp.pad(basis_cols.astype(jnp.float32), ((0, 8 - BASIS), (LEAD, S - TAPS - LEAD)))
    vmem = pl.BlockSpec(memory_space=pltpu.VMEM)
    return pl.pallas_call(
        match_kernel,
        out_shape=jax.ShapeDtypeStruct((blocks.shape[0] * S, S), jnp.bfloat16),
        in_specs=[pl.BlockSpec(memory_space=pltpu.SMEM), vmem, vmem, vmem],
        out_specs=vmem,
        scratch_shapes=[
            pltpu.VMEM((S, BASIS * S), jnp.bfloat16),
            pltpu.VMEM((S, BASIS * S), jnp.bfloat16),
            pltpu.VMEM((BASIS * S, 4 * S), jnp.bfloat16),
        ],
        compiler_params=pltpu.CompilerParams(vmem_limit_bytes=32 * 2**20),
        cost_estimate=pl.CostEstimate(flops=2**30, bytes_accessed=2**20, transcendentals=0),
        name="match",
    )(coefficients, jnp.concatenate([rows, cols]), blocks, weight)


def pack_kernel(dest_ref, off_ref, weight_ref, out_ref, taken):
    out_ref[...] = jnp.zeros_like(out_ref)
    line = lax.broadcasted_iota(jnp.int32, (META, S), 0)
    lane = lax.broadcasted_iota(jnp.int32, (META, S), 1)

    def clear(patch, carry):
        taken[patch] = 0
        return carry

    lax.fori_loop(0, out_ref.shape[0], clear, 0)

    def one(block, carry):
        value = weight_ref[block]
        for n in range(2):
            patch = dest_ref[2 * block + n]
            slot = taken[patch]
            taken[patch] = slot + 1
            row, col = off_ref[4 * block + 2 * n], off_ref[4 * block + 2 * n + 1]
            out_ref[patch, pl.ds(pl.multiple_of(slot * S, S), S), :] = value
            told = jnp.zeros((META, S), jnp.int32)
            for at, number in enumerate((1, row // LANES, lax.rem(row, LANES), col // LANES, lax.rem(col, LANES))):
                told = jnp.where(lane == at, number, told)
            before = out_ref[patch, 2 * S : 2 * S + META, :].astype(jnp.float32)
            now = jnp.where(line == slot, told.astype(jnp.float32), before)
            out_ref[patch, 2 * S : 2 * S + META, :] = now.astype(jnp.bfloat16)
        return carry

    lax.fori_loop(0, weight_ref.shape[0], one, 0)


def pack(weight, destinations, offsets, owners):
    smem = pl.BlockSpec(memory_space=pltpu.SMEM)
    vmem = pl.BlockSpec(memory_space=pltpu.VMEM)
    return pl.pallas_call(
        pack_kernel,
        out_shape=jax.ShapeDtypeStruct((owners, 2 * S + META, S), jnp.bfloat16),
        in_specs=[smem, smem, vmem],
        out_specs=vmem,
        scratch_shapes=[pltpu.SMEM((owners,), jnp.int32)],
        compiler_params=pltpu.CompilerParams(vmem_limit_bytes=24 * 2**20),
        cost_estimate=pl.CostEstimate(flops=2**20, bytes_accessed=2**21, transcendentals=0),
        name="pack",
    )(destinations.reshape(-1), offsets.reshape(-1), weight)


def whole_kernel(meta_ref, slots_ref, out_ref, canvas):
    canvas[...] = jnp.zeros_like(canvas)
    lane = lax.broadcasted_iota(jnp.int32, (S, LANES), 1)

    def one(index, carry):
        base = 5 * index

        @pl.when(meta_ref[base] > 0)
        def add():
            row = meta_ref[base + 1] * LANES + meta_ref[base + 2]
            tile, shift = meta_ref[base + 3], meta_ref[base + 4]
            source, slot = index // 2, lax.rem(index, 2)
            value = slots_ref[source, pl.ds(pl.multiple_of(slot * S, S), S), :].astype(jnp.float32)
            value = pltpu.roll(value, shift, 1)
            canvas[tile, pl.ds(row, S), :] += jnp.where(lane >= shift, value, 0.0)
            canvas[tile + 1, pl.ds(row, S), :] += jnp.where(lane >= shift, 0.0, value)

        return carry

    lax.fori_loop(0, 2 * slots_ref.shape[0], one, 0)
    for tile in range(P_SIZE // LANES):
        out_ref[:, tile * LANES : (tile + 1) * LANES] = canvas[tile].astype(jnp.bfloat16)


def place_whole(meta, slots):
    return pl.pallas_call(
        whole_kernel,
        out_shape=jax.ShapeDtypeStruct((P_SIZE, P_SIZE), jnp.bfloat16),
        in_specs=[pl.BlockSpec(memory_space=pltpu.SMEM), pl.BlockSpec(memory_space=pltpu.VMEM)],
        out_specs=pl.BlockSpec(memory_space=pltpu.VMEM),
        scratch_shapes=[pltpu.VMEM((P_SIZE // LANES + 1, P_SIZE, LANES), jnp.float32)],
        compiler_params=pltpu.CompilerParams(vmem_limit_bytes=24 * 2**20),
        cost_estimate=pl.CostEstimate(flops=2**23, bytes_accessed=2**22, transcendentals=0),
        name="place_whole",
    )(meta, slots)


def bands_kernel(meta_ref, where_ref, *refs):
    parts, (out_ref, held, canvas, stage, sems) = refs[:8], refs[8:]
    copies = [pltpu.make_async_copy(part, held.at[i], sems.at[i]) for i, part in enumerate(parts)]
    for copy in copies:
        copy.start()
    mine, core = where_ref[0], where_ref[1]
    canvas[...] = jnp.zeros_like(canvas)
    stage[...] = jnp.zeros_like(stage)
    lane = lax.broadcasted_iota(jnp.int32, (S, LANES), 1)
    for copy in copies:
        copy.wait()
    count = held.shape[1] // S

    def one(index, carry):
        source, block = index // count, lax.rem(index, count)
        lag = source // 2
        from_x = lax.rem(mine + 4 - lag, 4)
        from_core = lax.rem(core + lax.rem(source, 2), 2)
        line = (from_core * 4 + from_x) * count + block
        for n in range(2):
            base = line * 6 + 3 * n
            patch = meta_ref[base]

            @pl.when(patch // 8 == mine)
            def add():
                row, col = meta_ref[base + 1], meta_ref[base + 2]
                tile, shift = col // LANES, lax.rem(col, LANES)
                value = held[source, pl.ds(pl.multiple_of(block * S, S), S), :].astype(jnp.float32)
                value = pltpu.roll(value, shift, 1)
                stage[0, BAND : BAND + S, :] = jnp.where(lane >= shift, value, 0.0)
                stage[1, BAND : BAND + S, :] = jnp.where(lane >= shift, 0.0, value)
                first, within = row // BAND, lax.rem(row, BAND)
                odd = lax.rem(first + core, 2)

                def band(step):
                    start = BAND + BAND * step - within
                    spot = (first + step) // 2 * (8 * BAND) + lax.rem(patch, 8) * BAND
                    spot = pl.multiple_of(spot, BAND)
                    for side in range(2):
                        canvas[tile + side, pl.ds(spot, BAND), :] += stage[side, pl.ds(start, BAND), :]

                band(odd)
                band(odd + 2)

                @pl.when((odd == 0) & (within > 0))
                def last():
                    band(4)

        return carry

    lax.fori_loop(0, 8 * count, one, 0)
    for tile in range(P_SIZE // LANES):
        out_ref[:, tile * LANES : (tile + 1) * LANES] = canvas[tile].astype(jnp.bfloat16)


def place_bands(meta, where, parts):
    rows = 8 * P_SIZE // 2
    smem = pl.BlockSpec(memory_space=pltpu.SMEM)
    return pl.pallas_call(
        bands_kernel,
        out_shape=jax.ShapeDtypeStruct((rows, P_SIZE), jnp.bfloat16),
        in_specs=[smem, smem] + [pl.BlockSpec(memory_space=pl.ANY)] * len(parts),
        out_specs=pl.BlockSpec(memory_space=pltpu.VMEM),
        scratch_shapes=[
            pltpu.VMEM((len(parts),) + parts[0].shape, jnp.bfloat16),
            pltpu.VMEM((P_SIZE // LANES + 1, rows, LANES), jnp.float32),
            pltpu.VMEM((2, STAGE, LANES), jnp.float32),
            pltpu.SemaphoreType.DMA((len(parts),)),
        ],
        compiler_params=pltpu.CompilerParams(vmem_limit_bytes=40 * 2**20),
        cost_estimate=pl.CostEstimate(flops=2**24, bytes_accessed=2**23, transcendentals=0),
        name="place_bands",
    )(meta, where, *parts)


def body(blocks, inv_variance, destinations, offsets, coefficients, basis_rows, basis_cols):
    count = blocks.shape[1]
    owners = lax.axis_size("x") * lax.axis_size("z")
    weight = inv_variance[0]
    where = jnp.stack([lax.axis_index("x"), lax.axis_index("core")]).astype(jnp.int32)
    lines = jnp.concatenate([destinations[0][:, :, None], offsets[0]], -1).reshape(count, 6)
    lines = lax.all_gather(lines, ("core", "x")).reshape(-1)

    slots = pack(weight, destinations[0], offsets[0], owners)
    slots = lax.all_to_all(slots, ("x", "z"), 0, 0, tiled=True)

    terms = match(blocks[0], weight, coefficients[0], basis_rows, basis_cols)
    parts = []
    for lag in range(4):
        part = lax.ppermute(terms, "x", [(i, (i + lag) % 4) for i in range(4)]) if lag else terms
        parts += [part, lax.ppermute(part, "core", [(0, 1), (1, 0)])]
    num = place_bands(lines, where, parts).reshape(8, 8, BAND, P_SIZE)
    num = lax.psum_scatter(num, "y", scatter_dimension=0, tiled=True)
    num = lax.all_to_all(num[0], "z", 0, 0, tiled=True)

    told = slots[:, 2 * S : 2 * S + 2, :5].astype(jnp.int32).reshape(-1)
    den = place_whole(told, slots).reshape(16, BAND, P_SIZE)
    den = lax.all_to_all(den, ("y", "core"), 0, 0, tiled=True)

    num = jnp.sum(num.astype(jnp.float32), axis=0)
    den = jnp.sum(den.astype(jnp.float32), axis=0)
    return (num / jnp.maximum(den, 1.0))[None]


def solution(mesh):
    visits = mesh.shape["visit"]
    grid = Mesh(mesh.devices.reshape(visits // 2, 2, 4, mesh.shape["patch"] // 4), ("y", "core", "x", "z"))
    visit, patch = ("y", "core"), ("x", "z")
    return jax.shard_map(
        body,
        mesh=grid,
        in_specs=(
            P(visit, patch, None, None),
            P(visit, patch, None, None),
            P(visit, patch, None),
            P(visit, patch, None, None),
            P(visit, patch, None),
            P(),
            P(),
        ),
        out_specs=P(patch, visit, None),
        check_vma=False,
    )
```

time: 231 us -> 203 us (0.88)
  the two profiles are of different devices: /device:TPU:2 before, /device:TPU:18 now
where the time goes in v2:
time: 203 us; the launch traced here: 202 us
  waiting for transfers between devices  80.6 us (40%)
  starting transfers between devices  46.2 us (23%)
  Pallas kernels  32.3 us (16%)
  blocking collectives  21.2 us (10%)
  between operations  13.6 us (7%)
  local copies, waits for them, and re-layouts  7.07 us (3%)
    reduce_scatter x1, waiting for transfers between devices, body(): num = lax.psum_scatter(num, 'y', scatter_dimension=0, tiled=True)  41.1 us
    ppermute x3, waiting for transfers between devices, body(): lax.ppermute(terms, 'x', [(i, (i + lag) % 4) for i in range(4)])  29.1 us
    all_gather x1, blocking collectives, body(): lines = lax.all_gather(lines, ('core', 'x')).reshape(-1)  21.2 us
    pallas_call x1, Pallas kernels, place_bands(): pl.pallas_call(bands_kernel, out_shape=jax.ShapeDtypeStruct((rows, P_SIZE...  16.3 us
    all_to_all x1, starting transfers between devices, body(): slots = lax.all_to_all(slots, ('x', 'z'), 0, 0, tiled=True)  13.6 us
    ppermute x3, starting transfers between devices, body(): lax.ppermute(terms, 'x', [(i, (i + lag) % 4) for i in range(4)])  10.5 us
    all_to_all x1, waiting for transfers between devices, body(): num = lax.all_to_all(num[0], 'z', 0, 0, tiled=True)  10.4 us
    pallas_call x1, Pallas kernels, match(): pl.pallas_call(match_kernel, out_shape=jax.ShapeDtypeStruct((blocks.shape...  9.77 us
  transfers between devices with their start and end apart: 11, of which 5 were waited for; matrix products, arithmetic and copies ran while one was open for 0% of the time, Pallas kernels for 15%

profile of v2, /device:TPU:18, one launch (start us, length us, event | category | flops | bytes accessed | tf_op | source)
XLA Modules:
  0.0 201.9 jit_solution(2086653849636618087)
XLA Ops:
  8.3 1.0 copy-done.2
  9.3 1.6 pack.1
  10.9 1.4 copy-done
  12.3 13.6 %all-to-all-start.1 = ((bf16[32,272,128]{2,1,0:T(8,128)(2,1)}), bf16[32,272,128]{2,1,0:T(8,128)(2,1)S(1)}, u32[]{:S(2)}, u32[]{:S(2)}) async-start(bf16[32,272,128]{2,1,0:T(8,128)(2,1)} %copy-done), calls=%async_computation.2 | async-start | bytes 4456448 | tf_op jit(solution)/shard_map/all_to_all | solution.py:243
  26.2 1.0 copy-done.4
  27.3 9.8 %match.1.refs_0_ = bf16[2048,128]{1,0:T(8,128)(2,1)S(1)} custom-call(f32[16,15]{1,0:T(8,128)S(1)} %bitcast.19, f32[16,128]{1,0:T(8,128)S(1)} %fusion.3.taps_ref, bf16[16,128,128]{2,1,0:T(8,128)(2,1)S(1)} %bitcast.20, bf16[16,128,128]{2,1,0:T(8,128)(2,1)S(1)} %bitcast.18), custom_call_target="tpu_custom_call" | custom-call | flops 1073741824 | bytes 1048576 | tf_op jit(solution)/shard_map/match/pallas_call | solution.py:61
  37.0 3.4 %collective-permute-start.1 = (bf16[2048,128]{1,0:T(8,128)(2,1)S(1)}, bf16[2048,128]{1,0:T(8,128)(2,1)S(1)}, u32[]{:S(2)}, u32[]{:S(2)}) collective-permute-start(bf16[2048,128]{1,0:T(8,128)(2,1)S(1)} %match.1.refs_0_), channel_id=1, source_target_pairs={{0,8},{8,16},{16,24},{24,0},{1,9},{9,17},{17,25},{25,1},{2,10},{10... | collective-permute-start | bytes 1572872 | tf_op jit(solution)/shard_map/ppermute | solution.py:248
  40.4 2.7 %collective-permute-start.3 = (bf16[2048,128]{1,0:T(8,128)(2,1)S(1)}, bf16[2048,128]{1,0:T(8,128)(2,1)}, u32[]{:S(2)}, u32[]{:S(2)}) collective-permute-start(bf16[2048,128]{1,0:T(8,128)(2,1)S(1)} %match.1.refs_0_), channel_id=1, source_target_pairs={{0,16},{8,24},{16,0},{24,8},{1,17},{9,25},{17,1},{25,9},{2,18},{10... | collective-permute-start | bytes 1572872 | tf_op jit(solution)/shard_map/ppermute | solution.py:248
  43.2 4.3 %collective-permute-start.5 = (bf16[2048,128]{1,0:T(8,128)(2,1)S(1)}, bf16[2048,128]{1,0:T(8,128)(2,1)}, u32[]{:S(2)}, u32[]{:S(2)}) collective-permute-start(bf16[2048,128]{1,0:T(8,128)(2,1)S(1)} %match.1.refs_0_), channel_id=1, source_target_pairs={{0,24},{8,0},{16,8},{24,16},{1,25},{9,1},{17,9},{25,17},{2,26},{10... | collective-permute-start | bytes 1572872 | tf_op jit(solution)/shard_map/ppermute | solution.py:248
  47.5 1.9 collective-permute-start
  49.5 12.8 %collective-permute-done.1.refs_2_ = bf16[2048,128]{1,0:T(8,128)(2,1)S(1)} collective-permute-done((bf16[2048,128]{1,0:T(8,128)(2,1)S(1)}, bf16[2048,128]{1,0:T(8,128)(2,1)S(1)}, u32[]{:S(2)}, u32[]{:S(2)}) %collective-permute-start.1) | collective-permute-done | bytes 524320 | tf_op jit(solution)/shard_map/ppermute | solution.py:248
  62.2 1.9 collective-permute-start.2
  64.1 2.5 %collective-permute-done.3.refs_4_ = bf16[2048,128]{1,0:T(8,128)(2,1)} collective-permute-done((bf16[2048,128]{1,0:T(8,128)(2,1)S(1)}, bf16[2048,128]{1,0:T(8,128)(2,1)}, u32[]{:S(2)}, u32[]{:S(2)}) %collective-permute-start.3) | collective-permute-done | bytes 524320 | tf_op jit(solution)/shard_map/ppermute | solution.py:248
  66.6 1.9 collective-permute-start.4
  68.6 13.8 %collective-permute-done.5.refs_6_ = bf16[2048,128]{1,0:T(8,128)(2,1)} collective-permute-done((bf16[2048,128]{1,0:T(8,128)(2,1)S(1)}, bf16[2048,128]{1,0:T(8,128)(2,1)}, u32[]{:S(2)}, u32[]{:S(2)}) %collective-permute-start.5) | collective-permute-done | bytes 524320 | tf_op jit(solution)/shard_map/ppermute | solution.py:248
  82.4 1.9 collective-permute-start.6
  84.3 21.2 %all_gather.3 = s32[8,16,6]{1,2,0:T(8,128)S(1)} all-gather(s32[1,16,6]{1,2,0:T(8,128)S(1)} %all_gather_reshape.3), channel_id=1, replica_groups=mesh['y'=8,'core'=2,'x'=4,'z'=8] {'core','x'}, dimensions={0}, use_global_device_ids=true | all-gather | bytes 3456 | tf_op jit(solution)/shard_map/all_gather | solution.py:240
  105.9 16.3 %place_bands.1 = bf16[2048,512]{1,0:T(8,128)(2,1)S(1)} custom-call(s32[768]{0:T(1024)S(1)} %reshape.31.meta_ref, s32[2]{0:T(128)S(1)} %pad_add_fusion.1.where_ref, bf16[2048,128]{1,0:T(8,128)(2,1)S(1)} %match.1.refs_0_, bf16[2048,128]{1,0:T(8,128)(2,1)} %collective-permute-done.refs_1_, bf16[2048,128]{1,0:T(8,128)(2,1)S(1)} %collective-permute-done.1.refs_2_, ...), custom_call_target="tpu_custom_call" | custom-call | flops 16777216 | bytes 8388608 | tf_op jit(solution)/shard_map/place_bands/pallas_call | solution.py:217
  122.2 1.3 copy-done.1
  123.7 4.6 %place_whole.1 = bf16[512,512]{1,0:T(8,128)(2,1)} custom-call(s32[320]{0:T(512)S(1)} %reshape.37.meta_ref, bf16[32,272,128]{2,1,0:T(8,128)(2,1)S(1)} %all-to-all-done.1.slots_ref), custom_call_target="tpu_custom_call" | custom-call | flops 8388608 | bytes 4194304 | tf_op jit(solution)/shard_map/place_whole/pallas_call | solution.py:147
  128.3 7.5 %all-to-all-start.2 = ((bf16[16,32,512]{2,1,0:T(8,128)(2,1)}), bf16[16,32,512]{2,1,0:T(8,128)(2,1)S(1)}, u32[]{:S(2)}, u32[]{:S(2)}) async-start(bf16[16,32,512]{2,1,0:T(8,128)(2,1)} %bitcast.10), calls=%async_computation.3 | async-start | bytes 1048576 | tf_op jit(solution)/shard_map/all_to_all | solution.py:256
  135.9 41.1 %reduce-scatter.2.cloned.1.call-done = bf16[1,8,32,512]{3,2,1,0:T(8,128)(2,1)} async-done(((bf16[8,8,32,512]{3,2,1,0:T(8,128)(2,1)}), bf16[1,8,32,512]{3,2,1,0:T(8,128)(2,1)}) %reduce-scatter.2.cloned.1.call-update) | async-done | bytes 262160 | tf_op jit(solution)/shard_map/reduce_scatter | solution.py:251
  177.0 6.9 %all-to-all-start = ((bf16[8,32,512]{2,1,0:T(8,128)(2,1)}), bf16[8,32,512]{2,1,0:T(8,128)(2,1)S(1)}, u32[]{:S(2)}, u32[]{:S(2)}) async-start(bf16[8,32,512]{2,1,0:T(8,128)(2,1)} %bitcast.21), calls=%async_computation.1 | async-start | bytes 524288 | tf_op jit(solution)/shard_map/all_to_all | solution.py:252
  184.0 10.4 %all-to-all-done = bf16[8,32,512]{2,1,0:T(8,128)(2,1)S(1)} async-done(((bf16[8,32,512]{2,1,0:T(8,128)(2,1)}), bf16[8,32,512]{2,1,0:T(8,128)(2,1)S(1)}, u32[]{:S(2)}, u32[]{:S(2)}) %all-to-all-start) | async-done | bytes 262176 | tf_op jit(solution)/shard_map/all_to_all | solution.py:252
  (41 shorter events, 3.4 us)
Async XLA Ops:
  8.3 1.0 copy-start.2
  10.9 1.4 copy-start
  12.3 13.7 %copy-start.8 = (bf16[5,41]{1,0:T(8,128)(2,1)S(1)}, bf16[5,41]{1,0:T(8,128)(2,1)}, u32[]{:S(2)}) copy-start(bf16[5,41]{1,0:T(8,128)(2,1)} %param.12) | copy-start | bytes 1234
  12.3 13.8 %copy-start.6 = (f32[1,16,15]{1,0,2:T(1,128)S(1)}, f32[1,16,15]{1,0,2:T(1,128)}, u32[]{:S(2)}) copy-start(f32[1,16,15]{1,0,2:T(1,128)} %param.11) | copy-start | bytes 2884
  12.3 13.9 %copy-start.9 = (bf16[5,41]{1,0:T(8,128)(2,1)S(1)}, bf16[5,41]{1,0:T(8,128)(2,1)}, u32[]{:S(2)}) copy-start(bf16[5,41]{1,0:T(8,128)(2,1)} %param.13) | copy-start | bytes 1234
  12.3 14.0 %copy-start.3 = (bf16[1,16,128,128]{3,2,1,0:T(8,128)(2,1)S(1)}, bf16[1,16,128,128]{3,2,1,0:T(8,128)(2,1)}, u32[]{:S(2)}) copy-start(bf16[1,16,128,128]{3,2,1,0:T(8,128)(2,1)} %param.8) | copy-start | bytes 1572868
  12.3 111.3 %all-to-all-start.1 = ((bf16[32,272,128]{2,1,0:T(8,128)(2,1)}), bf16[32,272,128]{2,1,0:T(8,128)(2,1)S(1)}, u32[]{:S(2)}, u32[]{:S(2)}) async-start(bf16[32,272,128]{2,1,0:T(8,128)(2,1)} %copy-done), calls=%async_computation.2 | async-start | bytes 4456448 | tf_op jit(solution)/shard_map/all_to_all | solution.py:243
  25.9 58.4 %copy-start.5 = (s32[1,16,2,2]{1,3,2,0:T(2,128)S(1)}, s32[1,16,2,2]{1,3,2,0:T(2,128)}, u32[]{:S(2)}) copy-start(s32[1,16,2,2]{1,3,2,0:T(2,128)} %param.10) | copy-start | bytes 772
  25.9 58.4 %copy-start.7 = (s32[1,16,2]{1,2,0:T(2,128)S(1)}, s32[1,16,2]{1,2,0:T(2,128)}, u32[]{:S(2)}) copy-start(s32[1,16,2]{1,2,0:T(2,128)} %param.9) | copy-start | bytes 388
  25.9 151.0 %reduce-scatter.2.cloned.1.call-start = ((), (), s32[]{:S(2)}) async-start(), calls=%async_computation.4 | async-start | bytes 2359296 | tf_op jit(solution)/shard_map/reduce_scatter | solution.py:251
  26.2 1.0 copy-start.4
  37.0 25.2 %collective-permute-start.1 = (bf16[2048,128]{1,0:T(8,128)(2,1)S(1)}, bf16[2048,128]{1,0:T(8,128)(2,1)S(1)}, u32[]{:S(2)}, u32[]{:S(2)}) collective-permute-start(bf16[2048,128]{1,0:T(8,128)(2,1)S(1)} %match.1.refs_0_), channel_id=1, source_target_pairs={{0,8},{8,16},{16,24},{24,0},{1,9},{9,17},{17,25},{25,1},{2,10},{10... | collective-permute-start | bytes 1572872 | tf_op jit(solution)/shard_map/ppermute | solution.py:248
  40.4 26.2 %collective-permute-start.3 = (bf16[2048,128]{1,0:T(8,128)(2,1)S(1)}, bf16[2048,128]{1,0:T(8,128)(2,1)}, u32[]{:S(2)}, u32[]{:S(2)}) collective-permute-start(bf16[2048,128]{1,0:T(8,128)(2,1)S(1)} %match.1.refs_0_), channel_id=1, source_target_pairs={{0,16},{8,24},{16,0},{24,8},{1,17},{9,25},{17,1},{25,9},{2,18},{10... | collective-permute-start | bytes 1572872 | tf_op jit(solution)/shard_map/ppermute | solution.py:248
  43.2 39.2 %collective-permute-start.5 = (bf16[2048,128]{1,0:T(8,128)(2,1)S(1)}, bf16[2048,128]{1,0:T(8,128)(2,1)}, u32[]{:S(2)}, u32[]{:S(2)}) collective-permute-start(bf16[2048,128]{1,0:T(8,128)(2,1)S(1)} %match.1.refs_0_), channel_id=1, source_target_pairs={{0,24},{8,0},{16,8},{24,16},{1,25},{9,1},{17,9},{25,17},{2,26},{10... | collective-permute-start | bytes 1572872 | tf_op jit(solution)/shard_map/ppermute | solution.py:248
  47.5 58.3 %collective-permute-start = (bf16[2048,128]{1,0:T(8,128)(2,1)S(1)}, bf16[2048,128]{1,0:T(8,128)(2,1)}, u32[]{:S(2)}, u32[]{:S(2)}) collective-permute-start(bf16[2048,128]{1,0:T(8,128)(2,1)S(1)} %match.1.refs_0_), channel_id=1, source_target_pairs={{0,32},{32,0},{1,33},{33,1},{2,34},{34,2},{3,35},{35,3},{4,36},{36... | collective-permute-start | bytes 1572872 | tf_op jit(solution)/shard_map/ppermute | solution.py:249
  62.2 43.7 %collective-permute-start.2 = (bf16[2048,128]{1,0:T(8,128)(2,1)S(1)}, bf16[2048,128]{1,0:T(8,128)(2,1)}, u32[]{:S(2)}, u32[]{:S(2)}) collective-permute-start(bf16[2048,128]{1,0:T(8,128)(2,1)S(1)} %collective-permute-done.1.refs_2_), channel_id=1, source_target_pairs={{0,32},{32,0},{1,33},{33,1},{2,34},{34,2},{3,35},{35,3},{4,36},{36... | collective-permute-start | bytes 1572872 | tf_op jit(solution)/shard_map/ppermute | solution.py:249
  66.6 39.2 %collective-permute-start.4 = (bf16[2048,128]{1,0:T(8,128)(2,1)}, bf16[2048,128]{1,0:T(8,128)(2,1)}, u32[]{:S(2)}, u32[]{:S(2)}) collective-permute-start(bf16[2048,128]{1,0:T(8,128)(2,1)} %collective-permute-done.3.refs_4_), channel_id=1, source_target_pairs={{0,32},{32,0},{1,33},{33,1},{2,34},{34,2},{3,35},{35,3},{4,36},{36... | collective-permute-start | bytes 1572872 | tf_op jit(solution)/shard_map/ppermute | solution.py:249
  82.4 23.5 %collective-permute-start.6 = (bf16[2048,128]{1,0:T(8,128)(2,1)}, bf16[2048,128]{1,0:T(8,128)(2,1)}, u32[]{:S(2)}, u32[]{:S(2)}) collective-permute-start(bf16[2048,128]{1,0:T(8,128)(2,1)} %collective-permute-done.5.refs_6_), channel_id=1, source_target_pairs={{0,32},{32,0},{1,33},{33,1},{2,34},{34,2},{3,35},{35,3},{4,36},{36... | collective-permute-start | bytes 1572872 | tf_op jit(solution)/shard_map/ppermute | solution.py:249
  122.2 1.3 copy-start.1
  128.3 48.6 %all-to-all-start.2 = ((bf16[16,32,512]{2,1,0:T(8,128)(2,1)}), bf16[16,32,512]{2,1,0:T(8,128)(2,1)S(1)}, u32[]{:S(2)}, u32[]{:S(2)}) async-start(bf16[16,32,512]{2,1,0:T(8,128)(2,1)} %bitcast.10), calls=%async_computation.3 | async-start | bytes 1048576 | tf_op jit(solution)/shard_map/all_to_all | solution.py:256
  177.0 17.4 %all-to-all-start = ((bf16[8,32,512]{2,1,0:T(8,128)(2,1)}), bf16[8,32,512]{2,1,0:T(8,128)(2,1)S(1)}, u32[]{:S(2)}, u32[]{:S(2)}) async-start(bf16[8,32,512]{2,1,0:T(8,128)(2,1)} %bitcast.21), calls=%async_computation.1 | async-start | bytes 524288 | tf_op jit(solution)/shard_map/all_to_all | solution.py:252
Sparse Core Ops, SparseCore 0:
  123.7 53.2 reduce-scatter.1

commit v3 on v2

v3 whole, which is shorter than its diff:
```python
import functools

import jax
import jax.numpy as jnp
from jax import lax
from jax.experimental import pallas as pl
from jax.experimental.pallas import tpu as pltpu
from jax.sharding import Mesh
from jax.sharding import PartitionSpec as P

S = 128
P_SIZE = 512
TAPS = 41
HALF = (TAPS - 1) // 2
BASIS = 5
BAND = 32
LANES = 128
META = 16
LEAD = 4
GROUP = 4


def match_kernel(coef_ref, dest_ref, off_ref, taps_ref, blocks_ref, weight_ref, out_ref, rows_tab, cols_tab, stack):
    count = blocks_ref.shape[0]
    row_id = lax.broadcasted_iota(jnp.int32, (S, S), 0)
    col_id = lax.broadcasted_iota(jnp.int32, (S, S), 1)
    inside = jnp.abs(row_id - col_id) <= HALF
    for k in range(BASIS):
        for which, table in ((0, rows_tab), (1, cols_tab)):
            taps = jnp.broadcast_to(taps_ref[which * 8 + k : which * 8 + k + 1, :], (8, S))
            band = jnp.concatenate(
                [pltpu.roll(taps, (S - HALF - LEAD + row) % S, 1, stride=1, stride_axis=0) for row in range(0, S, 8)]
            )
            table[:, k * S : (k + 1) * S] = jnp.where(inside, band, 0.0).astype(jnp.bfloat16)
    y = (lax.broadcasted_iota(jnp.int32, (S, 1), 0).astype(jnp.float32) - (S - 1) / 2.0) / S
    x = (lax.broadcasted_iota(jnp.int32, (1, S), 1).astype(jnp.float32) - (S - 1) / 2.0) / S

    def some(step, carry):
        for part in range(GROUP):
            i = step * GROUP + part
            across = jnp.dot(blocks_ref[i], rows_tab[...], preferred_element_type=jnp.float32)
            for k in range(BASIS):
                image = across[:, k * S : (k + 1) * S]
                plain = coef_ref[i, 3 * k] + coef_ref[i, 3 * k + 2] * x
                stack[part, k * S : (k + 1) * S, 0:S] = (image * plain).astype(jnp.bfloat16)
                stack[part, k * S : (k + 1) * S, S : 2 * S] = (image * coef_ref[i, 3 * k + 1]).astype(jnp.bfloat16)
        for part in range(GROUP):
            i = step * GROUP + part
            sums = jnp.dot(cols_tab[...], stack[part], preferred_element_type=jnp.float32)
            term = (sums[:, 0:S] + y * sums[:, S : 2 * S]) * weight_ref[i].astype(jnp.float32)
            out_ref[pl.ds(pl.multiple_of(i * S, S), S), :] = term.astype(jnp.bfloat16)
        return carry

    lax.fori_loop(0, count // GROUP, some, 0)

    line = lax.broadcasted_iota(jnp.int32, (META, S), 0)
    lane = lax.broadcasted_iota(jnp.int32, (META, S), 1)

    def tell(i, told):
        for n in range(2):
            row, col = off_ref[4 * i + 2 * n], off_ref[4 * i + 2 * n + 1]
            numbers = (dest_ref[2 * i + n], row // LANES, lax.rem(row, LANES), col // LANES, lax.rem(col, LANES))
            for at, number in enumerate(numbers):
                told = jnp.where((line == i) & (lane == 5 * n + at), number, told)
        return told

    told = lax.fori_loop(0, count, tell, jnp.zeros((META, S), jnp.int32))
    out_ref[count * S : count * S + META, :] = told.astype(jnp.float32).astype(jnp.bfloat16)


def match(blocks, weight, destinations, offsets, coefficients, basis_rows, basis_cols):
    rows = jnp.pad(basis_rows[:, ::-1].astype(jnp.float32), ((0, 8 - BASIS), (LEAD, S - TAPS - LEAD)))
    cols = jnp.pad(basis_cols.astype(jnp.float32), ((0, 8 - BASIS), (LEAD, S - TAPS - LEAD)))
    vmem = pl.BlockSpec(memory_space=pltpu.VMEM)
    smem = pl.BlockSpec(memory_space=pltpu.SMEM)
    return pl.pallas_call(
        match_kernel,
        out_shape=jax.ShapeDtypeStruct((blocks.shape[0] * S + META, S), jnp.bfloat16),
        in_specs=[smem, smem, smem, vmem, vmem, vmem],
        out_specs=vmem,
        scratch_shapes=[
            pltpu.VMEM((S, BASIS * S), jnp.bfloat16),
            pltpu.VMEM((S, BASIS * S), jnp.bfloat16),
            pltpu.VMEM((GROUP, BASIS * S, 2 * S), jnp.bfloat16),
        ],
        compiler_params=pltpu.CompilerParams(vmem_limit_bytes=32 * 2**20),
        cost_estimate=pl.CostEstimate(flops=2**30, bytes_accessed=16 * 2**20, transcendentals=0),
        name="match",
    )(coefficients, destinations.reshape(-1), offsets.reshape(-1), jnp.concatenate([rows, cols]), blocks, weight)


def pack_kernel(dest_ref, off_ref, weight_ref, after_ref, out_ref, taken):
    out_ref[...] = jnp.zeros_like(out_ref)
    line = lax.broadcasted_iota(jnp.int32, (META, S), 0)
    lane = lax.broadcasted_iota(jnp.int32, (META, S), 1)

    def clear(patch, carry):
        taken[patch] = 0
        return carry

    lax.fori_loop(0, out_ref.shape[0], clear, 0)

    def one(block, carry):
        value = weight_ref[block]
        for n in range(2):
            patch = dest_ref[2 * block + n]
            slot = taken[patch]
            taken[patch] = slot + 1
            row, col = off_ref[4 * block + 2 * n], off_ref[4 * block + 2 * n + 1]
            out_ref[patch, pl.ds(pl.multiple_of(slot * S, S), S), :] = value
            told = jnp.zeros((META, S), jnp.int32)
            for at, number in enumerate((1, row // LANES, lax.rem(row, LANES), col // LANES, lax.rem(col, LANES))):
                told = jnp.where(lane == at, number, told)
            before = out_ref[patch, 2 * S : 2 * S + META, :].astype(jnp.float32)
            now = jnp.where(line == slot, told.astype(jnp.float32), before)
            out_ref[patch, 2 * S : 2 * S + META, :] = now.astype(jnp.bfloat16)
        return carry

    lax.fori_loop(0, weight_ref.shape[0], one, 0)


def pack(weight, destinations, offsets, owners, after):
    smem = pl.BlockSpec(memory_space=pltpu.SMEM)
    vmem = pl.BlockSpec(memory_space=pltpu.VMEM)
    return pl.pallas_call(
        pack_kernel,
        out_shape=jax.ShapeDtypeStruct((owners, 2 * S + META, S), jnp.bfloat16),
        in_specs=[smem, smem, vmem, pl.BlockSpec(memory_space=pl.ANY)],
        out_specs=vmem,
        scratch_shapes=[pltpu.SMEM((owners,), jnp.int32)],
        compiler_params=pltpu.CompilerParams(vmem_limit_bytes=24 * 2**20),
        cost_estimate=pl.CostEstimate(flops=2**20, bytes_accessed=6 * 2**20, transcendentals=0),
        name="pack",
    )(destinations.reshape(-1), offsets.reshape(-1), weight, after)


def whole_kernel(meta_ref, slots_ref, out_ref, canvas):
    canvas[...] = jnp.zeros_like(canvas)
    lane = lax.broadcasted_iota(jnp.int32, (S, LANES), 1)

    def one(index, carry):
        base = 5 * index

        @pl.when(meta_ref[base] > 0)
        def add():
            row = meta_ref[base + 1] * LANES + meta_ref[base + 2]
            tile, shift = meta_ref[base + 3], meta_ref[base + 4]
            source, slot = index // 2, lax.rem(index, 2)
            value = slots_ref[source, pl.ds(pl.multiple_of(slot * S, S), S), :].astype(jnp.float32)
            value = pltpu.roll(value, shift, 1)
            canvas[tile, pl.ds(row, S), :] += jnp.where(lane >= shift, value, 0.0)
            canvas[tile + 1, pl.ds(row, S), :] += jnp.where(lane >= shift, 0.0, value)

        return carry

    lax.fori_loop(0, 2 * slots_ref.shape[0], one, 0)
    for tile in range(P_SIZE // LANES):
        out_ref[:, tile * LANES : (tile + 1) * LANES] = canvas[tile].astype(jnp.bfloat16)


def place_whole(meta, slots):
    return pl.pallas_call(
        whole_kernel,
        out_shape=jax.ShapeDtypeStruct((P_SIZE, P_SIZE), jnp.bfloat16),
        in_specs=[pl.BlockSpec(memory_space=pltpu.SMEM), pl.BlockSpec(memory_space=pltpu.VMEM)],
        out_specs=pl.BlockSpec(memory_space=pltpu.VMEM),
        scratch_shapes=[pltpu.VMEM((P_SIZE // LANES + 1, P_SIZE, LANES), jnp.float32)],
        compiler_params=pltpu.CompilerParams(vmem_limit_bytes=24 * 2**20),
        cost_estimate=pl.CostEstimate(flops=2**23, bytes_accessed=16 * 2**20, transcendentals=0),
        name="place_whole",
    )(meta, slots)


def halves_kernel(where_ref, *refs):
    parts, (out_ref, held, canvas, told, lines, sems) = refs[:8], refs[8:]
    copies = [pltpu.make_async_copy(part, held.at[i], sems.at[i]) for i, part in enumerate(parts)]
    for copy in copies:
        copy.start()
    mine, core = where_ref[0], where_ref[1]
    count = held.shape[1] // S
    canvas[...] = jnp.zeros_like(canvas)
    for copy in copies:
        copy.wait()
    told[...] = held[:, count * S : count * S + META, :].astype(jnp.float32).astype(jnp.int32)
    tell = pltpu.make_async_copy(told, lines, sems.at[len(parts)])
    tell.start()
    tell.wait()
    lane = lax.broadcasted_iota(jnp.int32, (S, LANES), 1)

    def one(index, carry):
        source, block = index // count, lax.rem(index, count)
        for n in range(2):
            patch, tile = lines[source, block, 5 * n], lines[source, block, 5 * n + 3]
            left, right = tile - 2 * core, tile + 1 - 2 * core

            @pl.when((patch // 8 == mine) & (right >= 0) & (left < 2))
            def add():
                row = lines[source, block, 5 * n + 1] * LANES + lines[source, block, 5 * n + 2]
                shift = lines[source, block, 5 * n + 4]
                spot = pl.ds(lax.rem(patch, 8) * P_SIZE + row, S)
                value = held[source, pl.ds(pl.multiple_of(block * S, S), S), :].astype(jnp.float32)
                value = pltpu.roll(value, shift, 1)

                @pl.when(left >= 0)
                def first():
                    canvas[left, spot, :] += jnp.where(lane >= shift, value, 0.0)

                @pl.when(right < 2)
                def second():
                    canvas[right, spot, :] += jnp.where(lane >= shift, 0.0, value)

        return carry

    lax.fori_loop(0, len(parts) * count, one, 0)
    for tile in range(2):
        out_ref[:, tile * LANES : (tile + 1) * LANES] = canvas[tile].astype(jnp.bfloat16)


def place_halves(where, parts):
    rows, lines = 8 * P_SIZE, (len(parts), META, S)
    return pl.pallas_call(
        halves_kernel,
        out_shape=jax.ShapeDtypeStruct((rows, 2 * LANES), jnp.bfloat16),
        in_specs=[pl.BlockSpec(memory_space=pltpu.SMEM)] + [pl.BlockSpec(memory_space=pl.ANY)] * len(parts),
        out_specs=pl.BlockSpec(memory_space=pltpu.VMEM),
        scratch_shapes=[
            pltpu.VMEM((len(parts),) + parts[0].shape, jnp.bfloat16),
            pltpu.VMEM((2, rows, LANES), jnp.float32),
            pltpu.VMEM(lines, jnp.int32),
            pltpu.SMEM(lines, jnp.int32),
            pltpu.SemaphoreType.DMA((len(parts) + 1,)),
        ],
        compiler_params=pltpu.CompilerParams(vmem_limit_bytes=40 * 2**20),
        cost_estimate=pl.CostEstimate(flops=2**24, bytes_accessed=24 * 2**20, transcendentals=0),
        name="place_halves",
    )(where, *parts)


def body(blocks, inv_variance, destinations, offsets, coefficients, basis_rows, basis_cols):
    count = blocks.shape[1]
    owners = lax.axis_size("x") * lax.axis_size("z")
    weight = inv_variance[0]
    where = jnp.stack([lax.axis_index("x"), lax.axis_index("core")]).astype(jnp.int32)
    terms = match(blocks[0], weight, destinations[0], offsets[0], coefficients[0], basis_rows, basis_cols)
    parts = []
    for lag in range(4):
        part = lax.ppermute(terms, "x", [(i, (i + lag) % 4) for i in range(4)]) if lag else terms
        parts += [part, lax.ppermute(part, "core", [(0, 1), (1, 0)])]

    slots = pack(weight, destinations[0], offsets[0], owners, parts[1])
    slots = lax.all_to_all(slots, ("x", "z"), 0, 0, tiled=True)
    told = slots[:, 2 * S : 2 * S + 2, :5].astype(jnp.int32).reshape(-1)
    den = place_whole(told, slots).reshape(16, BAND, P_SIZE)
    den = lax.all_to_all(den, ("y", "core"), 0, 0, tiled=True)

    num = place_halves(where, parts).reshape(8, P_SIZE, 2 * LANES)
    num = lax.psum_scatter(num, "z", scatter_dimension=0, tiled=True)
    num = lax.all_to_all(num.reshape(16, BAND, 2 * LANES), ("y", "core"), 0, 0, tiled=True)

    num = jnp.sum(num.reshape(8, 2, BAND, 2 * LANES).astype(jnp.float32), axis=0)
    num = jnp.concatenate([num[0], num[1]], axis=-1)
    den = jnp.sum(den.astype(jnp.float32), axis=0)
    return (num / jnp.maximum(den, 1.0))[None]


def solution(mesh):
    visits = mesh.shape["visit"]
    grid = Mesh(mesh.devices.reshape(visits // 2, 2, 4, mesh.shape["patch"] // 4), ("y", "core", "x", "z"))
    visit, patch = ("y", "core"), ("x", "z")
    return jax.shard_map(
        body,
        mesh=grid,
        in_specs=(
            P(visit, patch, None, None),
            P(visit, patch, None, None),
            P(visit, patch, None),
            P(visit, patch, None, None),
            P(visit, patch, None),
            P(),
            P(),
        ),
        out_specs=P(patch, visit, None),
        check_vma=False,
    )
```

time: 203 us -> 191 us (0.941)
  the two profiles are of different devices: /device:TPU:18 before, /device:TPU:1 now
where the time goes in v3:
time: 191 us
  waiting for transfers between devices  84.8 us (44%)
  starting transfers between devices  59.9 us (31%)
  Pallas kernels  22.5 us (12%)
  between operations  13.6 us (7%)
  local copies, waits for them, and re-layouts  8.16 us (4%)
    all_to_all x1, waiting for transfers between devices, body(): slots = lax.all_to_all(slots, ('x', 'z'), 0, 0, tiled=True)  42.5 us
    ppermute x4, starting transfers between devices, body(): parts += [part, lax.ppermute(part, 'core', [(0, 1), (1, 0)])]  24.2 us
    all_to_all x1, waiting for transfers between devices, body(): den = lax.all_to_all(den, ('y', 'core'), 0, 0, tiled=True)  16.7 us
    reduce_scatter x1, waiting for transfers between devices, body(): num = lax.psum_scatter(num, 'z', scatter_dimension=0, tiled=True)  16.5 us
    pallas_call x1, Pallas kernels, place_halves(): pl.pallas_call(halves_kernel, out_shape=jax.ShapeDtypeStruct((rows, 2 * L...  12.7 us
    all_to_all x1, starting transfers between devices, body(): slots = lax.all_to_all(slots, ('x', 'z'), 0, 0, tiled=True)  12.3 us
    ppermute x3, starting transfers between devices, body(): lax.ppermute(terms, 'x', [(i, (i + lag) % 4) for i in range(4)])  10.2 us
    all_to_all x1, starting transfers between devices, body(): lax.all_to_all(num.reshape(16, BAND, 2 * LANES), ('y', 'core'), 0, 0, til...  9.82 us
  transfers between devices with their start and end apart: 11, of which 6 were waited for; matrix products, arithmetic and copies ran while one was open for 0% of the time, Pallas kernels for 10%

profile of v3, /device:TPU:1, one launch (start us, length us, event | category | flops | bytes accessed | tf_op | source)
XLA Modules:
  0.0 190.5 jit_solution(15843147378359747363)
XLA Ops:
  8.1 0.8 copy.11
  10.6 1.0 copy-done.2
  11.6 1.0 copy-done.3
  12.6 3.7 %match.1.refs_0_ = bf16[2064,128]{1,0:T(8,128)(2,1)S(1)} custom-call(f32[16,15]{1,0:T(8,128)S(1)} %bitcast.15, s32[32]{0:T(128)S(1)} %reshape_squeeze.8.dest_ref, s32[64]{0:T(128)S(1)} %reshape_squeeze.9.off_ref, f32[16,128]{1,0:T(8,128)S(1)} %fusion.3.taps_ref, bf16[16,128,128]{2,1,0:T(8,128)(2,1)S(1)} %bitcast.16, bf16[16,128,128]{2,1,0:T(8,128)(2,1)S(1)} %bitcast.13), custom_call_target="tpu_custom_call" | custom-call | flops 1073741824 | bytes 16777216 | tf_op jit(solution)/shard_map/match/pallas_call | solution.py:76
  16.4 5.2 %collective-permute-start.5 = (bf16[2064,128]{1,0:T(8,128)(2,1)S(1)}, bf16[2064,128]{1,0:T(8,128)(2,1)}, u32[]{:S(2)}, u32[]{:S(2)}) collective-permute-start(bf16[2064,128]{1,0:T(8,128)(2,1)S(1)} %match.1.refs_0_), channel_id=1, source_target_pairs={{0,24},{8,0},{16,8},{24,16},{1,25},{9,1},{17,9},{25,17},{2,26},{10... | collective-permute-start | bytes 1585160 | tf_op jit(solution)/shard_map/ppermute | solution.py:247
  21.6 2.4 %collective-permute-start.3 = (bf16[2064,128]{1,0:T(8,128)(2,1)S(1)}, bf16[2064,128]{1,0:T(8,128)(2,1)}, u32[]{:S(2)}, u32[]{:S(2)}) collective-permute-start(bf16[2064,128]{1,0:T(8,128)(2,1)S(1)} %match.1.refs_0_), channel_id=1, source_target_pairs={{0,16},{8,24},{16,0},{24,8},{1,17},{9,25},{17,1},{25,9},{2,18},{10... | collective-permute-start | bytes 1585160 | tf_op jit(solution)/shard_map/ppermute | solution.py:247
  24.0 2.5 %collective-permute-start.1 = (bf16[2064,128]{1,0:T(8,128)(2,1)S(1)}, bf16[2064,128]{1,0:T(8,128)(2,1)}, u32[]{:S(2)}, u32[]{:S(2)}) collective-permute-start(bf16[2064,128]{1,0:T(8,128)(2,1)S(1)} %match.1.refs_0_), channel_id=1, source_target_pairs={{0,8},{8,16},{16,24},{24,0},{1,9},{9,17},{17,25},{25,1},{2,10},{10... | collective-permute-start | bytes 1585160 | tf_op jit(solution)/shard_map/ppermute | solution.py:247
  26.5 6.4 %collective-permute-start = (bf16[2064,128]{1,0:T(8,128)(2,1)S(1)}, bf16[2064,128]{1,0:T(8,128)(2,1)S(1)}, u32[]{:S(2)}, u32[]{:S(2)}) collective-permute-start(bf16[2064,128]{1,0:T(8,128)(2,1)S(1)} %match.1.refs_0_), channel_id=1, source_target_pairs={{0,32},{32,0},{1,33},{33,1},{2,34},{34,2},{3,35},{35,3},{4,36},{36... | collective-permute-start | bytes 1585160 | tf_op jit(solution)/shard_map/ppermute | solution.py:248
  33.5 13.5 %collective-permute-start.6 = (bf16[2064,128]{1,0:T(8,128)(2,1)}, bf16[2064,128]{1,0:T(8,128)(2,1)}, u32[]{:S(2)}, u32[]{:S(2)}) collective-permute-start(bf16[2064,128]{1,0:T(8,128)(2,1)} %collective-permute-done.5.refs_6_), channel_id=1, source_target_pairs={{0,32},{32,0},{1,33},{33,1},{2,34},{34,2},{3,35},{35,3},{4,36},{36... | collective-permute-start | bytes 1585160 | tf_op jit(solution)/shard_map/ppermute | solution.py:248
  47.0 1.9 %collective-permute-start.4 = (bf16[2064,128]{1,0:T(8,128)(2,1)}, bf16[2064,128]{1,0:T(8,128)(2,1)}, u32[]{:S(2)}, u32[]{:S(2)}) collective-permute-start(bf16[2064,128]{1,0:T(8,128)(2,1)} %collective-permute-done.3.refs_4_), channel_id=1, source_target_pairs={{0,32},{32,0},{1,33},{33,1},{2,34},{34,2},{3,35},{35,3},{4,36},{36... | collective-permute-start | bytes 1585160 | tf_op jit(solution)/shard_map/ppermute | solution.py:248
  49.0 1.4 collective-permute-done.1.refs_2_
  50.3 2.4 %collective-permute-start.2 = (bf16[2064,128]{1,0:T(8,128)(2,1)}, bf16[2064,128]{1,0:T(8,128)(2,1)}, u32[]{:S(2)}, u32[]{:S(2)}) collective-permute-start(bf16[2064,128]{1,0:T(8,128)(2,1)} %collective-permute-done.1.refs_2_), channel_id=1, source_target_pairs={{0,32},{32,0},{1,33},{33,1},{2,34},{34,2},{3,35},{35,3},{4,36},{36... | collective-permute-start | bytes 1585160 | tf_op jit(solution)/shard_map/ppermute | solution.py:248
  52.8 1.6 pack.1
  54.3 1.4 copy-done
  55.7 12.3 %all-to-all-start.1 = ((bf16[32,272,128]{2,1,0:T(8,128)(2,1)}), bf16[32,272,128]{2,1,0:T(8,128)(2,1)S(1)}, u32[]{:S(2)}, u32[]{:S(2)}) async-start(bf16[32,272,128]{2,1,0:T(8,128)(2,1)} %copy-done), calls=%async_computation.2 | async-start | bytes 4456448 | tf_op jit(solution)/shard_map/all_to_all | solution.py:251
  68.1 12.7 %place_halves.1 = bf16[4096,256]{1,0:T(8,128)(2,1)S(1)} custom-call(s32[2]{0:T(128)S(1)} %pad_add_fusion.where_ref, bf16[2064,128]{1,0:T(8,128)(2,1)S(1)} %match.1.refs_0_, bf16[2064,128]{1,0:T(8,128)(2,1)S(1)} %collective-permute-done.refs_1_.after_ref, bf16[2064,128]{1,0:T(8,128)(2,1)} %collective-permute-done.1.refs_2_, ...), custom_call_target="tpu_custom_call" | custom-call | flops 16777216 | bytes 25165824 | tf_op jit(solution)/shard_map/place_halves/pallas_call | solution.py:221
  80.9 1.3 copy-done.1
  82.2 42.5 %all-to-all-done.1.slots_ref = bf16[32,272,128]{2,1,0:T(8,128)(2,1)S(1)} async-done(((bf16[32,272,128]{2,1,0:T(8,128)(2,1)}), bf16[32,272,128]{2,1,0:T(8,128)(2,1)S(1)}, u32[]{:S(2)}, u32[]{:S(2)}) %all-to-all-start.1) | async-done | bytes 2228256 | tf_op jit(solution)/shard_map/all_to_all | solution.py:251
  124.7 16.5 %reduce-scatter.2.cloned.1.call-done = bf16[1,512,256]{2,1,0:T(8,128)(2,1)} async-done(((bf16[8,512,256]{2,1,0:T(8,128)(2,1)}), bf16[1,512,256]{2,1,0:T(8,128)(2,1)}) %reduce-scatter.2.cloned.1.call-update) | async-done | bytes 262160 | tf_op jit(solution)/shard_map/reduce_scatter | solution.py:257
  141.2 9.8 %all-to-all-start = ((bf16[16,32,256]{2,1,0:T(8,128)(2,1)}), bf16[16,32,256]{2,1,0:T(8,128)(2,1)S(1)}, u32[]{:S(2)}, u32[]{:S(2)}) async-start(bf16[16,32,256]{2,1,0:T(8,128)(2,1)} %bitcast.18), calls=%async_computation.1 | async-start | bytes 524288 | tf_op jit(solution)/shard_map/all_to_all | solution.py:258
  151.2 4.5 %place_whole.1 = bf16[512,512]{1,0:T(8,128)(2,1)} custom-call(s32[320]{0:T(512)S(1)} %reshape.58.meta_ref, bf16[32,272,128]{2,1,0:T(8,128)(2,1)S(1)} %all-to-all-done.1.slots_ref), custom_call_target="tpu_custom_call" | custom-call | flops 8388608 | bytes 16777216 | tf_op jit(solution)/shard_map/place_whole/pallas_call | solution.py:162
  155.7 7.0 %all-to-all-done = bf16[16,32,256]{2,1,0:T(8,128)(2,1)S(1)} async-done(((bf16[16,32,256]{2,1,0:T(8,128)(2,1)}), bf16[16,32,256]{2,1,0:T(8,128)(2,1)S(1)}, u32[]{:S(2)}, u32[]{:S(2)}) %all-to-all-start) | async-done | bytes 262176 | tf_op jit(solution)/shard_map/all_to_all | solution.py:258
  162.7 3.5 %all-to-all-start.2 = ((bf16[16,32,512]{2,1,0:T(8,128)(2,1)}), bf16[16,32,512]{2,1,0:T(8,128)(2,1)S(1)}, u32[]{:S(2)}, u32[]{:S(2)}) async-start(bf16[16,32,512]{2,1,0:T(8,128)(2,1)} %bitcast.8), calls=%async_computation.3 | async-start | bytes 1048576 | tf_op jit(solution)/shard_map/all_to_all | solution.py:254
  166.3 16.7 %all-to-all-done.2 = bf16[16,32,512]{2,1,0:T(8,128)(2,1)S(1)} async-done(((bf16[16,32,512]{2,1,0:T(8,128)(2,1)}), bf16[16,32,512]{2,1,0:T(8,128)(2,1)S(1)}, u32[]{:S(2)}, u32[]{:S(2)}) %all-to-all-start.2) | async-done | bytes 524320 | tf_op jit(solution)/shard_map/all_to_all | solution.py:254
  (25 shorter events, 4.9 us)
Async XLA Ops:
  10.6 1.0 copy-start.2
  11.6 1.0 copy-start.3
  16.4 17.2 %collective-permute-start.5 = (bf16[2064,128]{1,0:T(8,128)(2,1)S(1)}, bf16[2064,128]{1,0:T(8,128)(2,1)}, u32[]{:S(2)}, u32[]{:S(2)}) collective-permute-start(bf16[2064,128]{1,0:T(8,128)(2,1)S(1)} %match.1.refs_0_), channel_id=1, source_target_pairs={{0,24},{8,0},{16,8},{24,16},{1,25},{9,1},{17,9},{25,17},{2,26},{10... | collective-permute-start | bytes 1585160 | tf_op jit(solution)/shard_map/ppermute | solution.py:247
  21.6 25.4 %collective-permute-start.3 = (bf16[2064,128]{1,0:T(8,128)(2,1)S(1)}, bf16[2064,128]{1,0:T(8,128)(2,1)}, u32[]{:S(2)}, u32[]{:S(2)}) collective-permute-start(bf16[2064,128]{1,0:T(8,128)(2,1)S(1)} %match.1.refs_0_), channel_id=1, source_target_pairs={{0,16},{8,24},{16,0},{24,8},{1,17},{9,25},{17,1},{25,9},{2,18},{10... | collective-permute-start | bytes 1585160 | tf_op jit(solution)/shard_map/ppermute | solution.py:247
  24.0 26.3 %collective-permute-start.1 = (bf16[2064,128]{1,0:T(8,128)(2,1)S(1)}, bf16[2064,128]{1,0:T(8,128)(2,1)}, u32[]{:S(2)}, u32[]{:S(2)}) collective-permute-start(bf16[2064,128]{1,0:T(8,128)(2,1)S(1)} %match.1.refs_0_), channel_id=1, source_target_pairs={{0,8},{8,16},{16,24},{24,0},{1,9},{9,17},{17,25},{25,1},{2,10},{10... | collective-permute-start | bytes 1585160 | tf_op jit(solution)/shard_map/ppermute | solution.py:247
  26.5 26.2 %collective-permute-start = (bf16[2064,128]{1,0:T(8,128)(2,1)S(1)}, bf16[2064,128]{1,0:T(8,128)(2,1)S(1)}, u32[]{:S(2)}, u32[]{:S(2)}) collective-permute-start(bf16[2064,128]{1,0:T(8,128)(2,1)S(1)} %match.1.refs_0_), channel_id=1, source_target_pairs={{0,32},{32,0},{1,33},{33,1},{2,34},{34,2},{3,35},{35,3},{4,36},{36... | collective-permute-start | bytes 1585160 | tf_op jit(solution)/shard_map/ppermute | solution.py:248
  33.5 34.6 %collective-permute-start.6 = (bf16[2064,128]{1,0:T(8,128)(2,1)}, bf16[2064,128]{1,0:T(8,128)(2,1)}, u32[]{:S(2)}, u32[]{:S(2)}) collective-permute-start(bf16[2064,128]{1,0:T(8,128)(2,1)} %collective-permute-done.5.refs_6_), channel_id=1, source_target_pairs={{0,32},{32,0},{1,33},{33,1},{2,34},{34,2},{3,35},{35,3},{4,36},{36... | collective-permute-start | bytes 1585160 | tf_op jit(solution)/shard_map/ppermute | solution.py:248
  47.0 21.1 %collective-permute-start.4 = (bf16[2064,128]{1,0:T(8,128)(2,1)}, bf16[2064,128]{1,0:T(8,128)(2,1)}, u32[]{:S(2)}, u32[]{:S(2)}) collective-permute-start(bf16[2064,128]{1,0:T(8,128)(2,1)} %collective-permute-done.3.refs_4_), channel_id=1, source_target_pairs={{0,32},{32,0},{1,33},{33,1},{2,34},{34,2},{3,35},{35,3},{4,36},{36... | collective-permute-start | bytes 1585160 | tf_op jit(solution)/shard_map/ppermute | solution.py:248
  50.3 17.8 %collective-permute-start.2 = (bf16[2064,128]{1,0:T(8,128)(2,1)}, bf16[2064,128]{1,0:T(8,128)(2,1)}, u32[]{:S(2)}, u32[]{:S(2)}) collective-permute-start(bf16[2064,128]{1,0:T(8,128)(2,1)} %collective-permute-done.1.refs_2_), channel_id=1, source_target_pairs={{0,32},{32,0},{1,33},{33,1},{2,34},{34,2},{3,35},{35,3},{4,36},{36... | collective-permute-start | bytes 1585160 | tf_op jit(solution)/shard_map/ppermute | solution.py:248
  54.3 1.4 copy-start
  55.7 69.0 %all-to-all-start.1 = ((bf16[32,272,128]{2,1,0:T(8,128)(2,1)}), bf16[32,272,128]{2,1,0:T(8,128)(2,1)S(1)}, u32[]{:S(2)}, u32[]{:S(2)}) async-start(bf16[32,272,128]{2,1,0:T(8,128)(2,1)} %copy-done), calls=%async_computation.2 | async-start | bytes 4456448 | tf_op jit(solution)/shard_map/all_to_all | solution.py:251
  68.0 73.2 %reduce-scatter.2.cloned.1.call-start = ((), (), s32[]{:S(2)}) async-start(), calls=%async_computation.4 | async-start | bytes 2359296 | tf_op jit(solution)/shard_map/reduce_scatter | solution.py:257
  80.8 1.3 copy-start.1
  141.2 21.5 %all-to-all-start = ((bf16[16,32,256]{2,1,0:T(8,128)(2,1)}), bf16[16,32,256]{2,1,0:T(8,128)(2,1)S(1)}, u32[]{:S(2)}, u32[]{:S(2)}) async-start(bf16[16,32,256]{2,1,0:T(8,128)(2,1)} %bitcast.18), calls=%async_computation.1 | async-start | bytes 524288 | tf_op jit(solution)/shard_map/all_to_all | solution.py:258
  162.7 20.2 %all-to-all-start.2 = ((bf16[16,32,512]{2,1,0:T(8,128)(2,1)}), bf16[16,32,512]{2,1,0:T(8,128)(2,1)S(1)}, u32[]{:S(2)}, u32[]{:S(2)}) async-start(bf16[16,32,512]{2,1,0:T(8,128)(2,1)} %bitcast.8), calls=%async_computation.3 | async-start | bytes 1048576 | tf_op jit(solution)/shard_map/all_to_all | solution.py:254
Sparse Core Ops, SparseCore 0:
  82.3 58.8 reduce-scatter.1

commit v4 on v3

v4 whole, which is shorter than its diff:
```python
import functools

import jax
import jax.numpy as jnp
from jax import lax
from jax.experimental import pallas as pl
from jax.experimental.pallas import tpu as pltpu
from jax.sharding import Mesh
from jax.sharding import PartitionSpec as P

S = 128
P_SIZE = 512
TAPS = 41
HALF = (TAPS - 1) // 2
BASIS = 5
BAND = 32
LANES = 128
META = 16
LEAD = 4
GROUP = 4


def places(dest_ref, off_ref, block, n):
    row, col = off_ref[block, n, 0], off_ref[block, n, 1]
    return dest_ref[block, n], row // LANES, lax.rem(row, LANES), col // LANES, lax.rem(col, LANES)


def match_kernel(
    coef_ref, dest_ref, off_ref, taps_ref, blocks_ref, weight_ref, out_ref, rows_tab, cols_tab, stack, taken
):
    row_id = lax.broadcasted_iota(jnp.int32, (S, S), 0)
    col_id = lax.broadcasted_iota(jnp.int32, (S, S), 1)
    inside = jnp.abs(row_id - col_id) <= HALF
    for k in range(BASIS):
        for which, table in ((0, rows_tab), (1, cols_tab)):
            taps = jnp.broadcast_to(taps_ref[which * 8 + k : which * 8 + k + 1, :], (8, S))
            band = jnp.concatenate(
                [pltpu.roll(taps, (S - HALF - LEAD + row) % S, 1, stride=1, stride_axis=0) for row in range(0, S, 8)]
            )
            table[:, k * S : (k + 1) * S] = jnp.where(inside, band, 0.0).astype(jnp.bfloat16)
    y = (lax.broadcasted_iota(jnp.int32, (S, 1), 0).astype(jnp.float32) - (S - 1) / 2.0) / S
    x = (lax.broadcasted_iota(jnp.int32, (1, S), 1).astype(jnp.float32) - (S - 1) / 2.0) / S
    line = lax.broadcasted_iota(jnp.int32, (META, S), 0)
    lane = lax.broadcasted_iota(jnp.int32, (META, S), 1)

    def clear(patch, carry):
        taken[patch] = 0
        out_ref[patch, 2 * S : 2 * S + META, :] = jnp.zeros((META, S), jnp.bfloat16)
        return carry

    lax.fori_loop(0, out_ref.shape[0], clear, 0)

    def some(step, carry):
        for part in range(GROUP):
            i = step * GROUP + part
            across = jnp.dot(blocks_ref[i], rows_tab[...], preferred_element_type=jnp.float32)
            for k in range(BASIS):
                image = across[:, k * S : (k + 1) * S]
                plain = coef_ref[i, 3 * k] + coef_ref[i, 3 * k + 2] * x
                stack[part, k * S : (k + 1) * S, 0:S] = (image * plain).astype(jnp.bfloat16)
                stack[part, k * S : (k + 1) * S, S : 2 * S] = (image * coef_ref[i, 3 * k + 1]).astype(jnp.bfloat16)
        for part in range(GROUP):
            i = step * GROUP + part
            sums = jnp.dot(cols_tab[...], stack[part], preferred_element_type=jnp.float32)
            term = (sums[:, 0:S] + y * sums[:, S : 2 * S]) * weight_ref[i].astype(jnp.float32)
            term = term.astype(jnp.bfloat16)
            for n in range(2):
                patch, *numbers = places(dest_ref, off_ref, i, n)
                slot = taken[patch]
                taken[patch] = slot + 1
                out_ref[patch, pl.ds(pl.multiple_of(slot * S, S), S), :] = term
                told = out_ref[patch, 2 * S : 2 * S + META, :].astype(jnp.float32).astype(jnp.int32)
                for at, number in enumerate([1] + numbers):
                    told = jnp.where((line == slot) & (lane == at), number, told)
                out_ref[patch, 2 * S : 2 * S + META, :] = told.astype(jnp.float32).astype(jnp.bfloat16)
        return carry

    lax.fori_loop(0, blocks_ref.shape[0] // GROUP, some, 0)


def match(blocks, weight, destinations, offsets, coefficients, basis_rows, basis_cols, owners):
    rows = jnp.pad(basis_rows[:, ::-1].astype(jnp.float32), ((0, 8 - BASIS), (LEAD, S - TAPS - LEAD)))
    cols = jnp.pad(basis_cols.astype(jnp.float32), ((0, 8 - BASIS), (LEAD, S - TAPS - LEAD)))
    vmem = pl.BlockSpec(memory_space=pltpu.VMEM)
    smem = pl.BlockSpec(memory_space=pltpu.SMEM)
    return pl.pallas_call(
        match_kernel,
        out_shape=jax.ShapeDtypeStruct((owners, 2 * S + META, S), jnp.bfloat16),
        in_specs=[smem, smem, smem, vmem, vmem, vmem],
        out_specs=vmem,
        scratch_shapes=[
            pltpu.VMEM((S, BASIS * S), jnp.bfloat16),
            pltpu.VMEM((S, BASIS * S), jnp.bfloat16),
            pltpu.VMEM((GROUP, BASIS * S, 2 * S), jnp.bfloat16),
            pltpu.SMEM((owners,), jnp.int32),
        ],
        compiler_params=pltpu.CompilerParams(vmem_limit_bytes=32 * 2**20),
        cost_estimate=pl.CostEstimate(flops=2**30, bytes_accessed=16 * 2**20, transcendentals=0),
        name="match",
    )(coefficients, destinations, offsets, jnp.concatenate([rows, cols]), blocks, weight)


def lines_kernel(dest_ref, off_ref, weight_ref, out_ref, told, sems):
    count = dest_ref.shape[0]
    body = pltpu.make_async_copy(weight_ref, out_ref.at[pl.ds(0, count * S)], sems.at[0])
    body.start()
    line = lax.broadcasted_iota(jnp.int32, (META, S), 0)
    lane = lax.broadcasted_iota(jnp.int32, (META, S), 1)
    words = jnp.zeros((META, S), jnp.int32)
    for block in range(count):
        for n in range(2):
            for at, number in enumerate(places(dest_ref, off_ref, block, n)):
                words = jnp.where((line == n) & (lane == 8 * block + at), number, words)
    told[...] = words.astype(jnp.float32).astype(jnp.bfloat16)
    tail = pltpu.make_async_copy(told, out_ref.at[pl.ds(count * S, META)], sems.at[1])
    tail.start()
    body.wait()
    tail.wait()


def with_lines(weight, destinations, offsets):
    smem = pl.BlockSpec(memory_space=pltpu.SMEM)
    rows = weight.shape[0] * S
    return pl.pallas_call(
        lines_kernel,
        out_shape=jax.ShapeDtypeStruct((rows + META, S), jnp.bfloat16),
        in_specs=[smem, smem, pl.BlockSpec(memory_space=pl.ANY)],
        out_specs=pl.BlockSpec(memory_space=pl.ANY),
        scratch_shapes=[pltpu.VMEM((META, S), jnp.bfloat16), pltpu.SemaphoreType.DMA((2,))],
        compiler_params=pltpu.CompilerParams(vmem_limit_bytes=4 * 2**20),
        cost_estimate=pl.CostEstimate(flops=2**16, bytes_accessed=2**20, transcendentals=0),
        name="lines",
    )(destinations, offsets, weight.reshape(rows, S))


def whole_kernel(meta_ref, slots_ref, out_ref, canvas):
    canvas[...] = jnp.zeros_like(canvas)
    lane = lax.broadcasted_iota(jnp.int32, (S, LANES), 1)

    def one(index, carry):
        base = 5 * index

        @pl.when(meta_ref[base] > 0)
        def add():
            row = meta_ref[base + 1] * LANES + meta_ref[base + 2]
            tile, shift = meta_ref[base + 3], meta_ref[base + 4]
            source, slot = index // 2, lax.rem(index, 2)
            value = slots_ref[source, pl.ds(pl.multiple_of(slot * S, S), S), :].astype(jnp.float32)
            value = pltpu.roll(value, shift, 1)
            canvas[tile, pl.ds(row, S), :] += jnp.where(lane >= shift, value, 0.0)
            canvas[tile + 1, pl.ds(row, S), :] += jnp.where(lane >= shift, 0.0, value)

        return carry

    lax.fori_loop(0, 2 * slots_ref.shape[0], one, 0)
    for tile in range(P_SIZE // LANES):
        out_ref[:, tile * LANES : (tile + 1) * LANES] = canvas[tile].astype(jnp.bfloat16)


def place_whole(meta, slots):
    return pl.pallas_call(
        whole_kernel,
        out_shape=jax.ShapeDtypeStruct((P_SIZE, P_SIZE), jnp.bfloat16),
        in_specs=[pl.BlockSpec(memory_space=pltpu.SMEM), pl.BlockSpec(memory_space=pltpu.VMEM)],
        out_specs=pl.BlockSpec(memory_space=pltpu.VMEM),
        scratch_shapes=[pltpu.VMEM((P_SIZE // LANES + 1, P_SIZE, LANES), jnp.float32)],
        compiler_params=pltpu.CompilerParams(vmem_limit_bytes=24 * 2**20),
        cost_estimate=pl.CostEstimate(flops=2**23, bytes_accessed=16 * 2**20, transcendentals=0),
        name="place_whole",
    )(meta, slots)


def halves_kernel(where_ref, parts_ref, out_ref, held, canvas, told, lines, sems):
    count = parts_ref.shape[1] // S
    fetch = pltpu.make_async_copy(parts_ref, held, sems.at[0])
    fetch.start()
    mine, core = where_ref[0], where_ref[1]
    canvas[...] = jnp.zeros_like(canvas)
    fetch.wait()
    words = held[:, count * S : count * S + META, :].astype(jnp.float32).astype(jnp.int32)
    told[...] = words[:, 0:8, :]
    tell = pltpu.make_async_copy(told, lines, sems.at[1])
    tell.start()
    tell.wait()
    lane = lax.broadcasted_iota(jnp.int32, (S, LANES), 1)

    def one(index, carry):
        source, block = index // count, lax.rem(index, count)
        for n in range(2):
            patch, tile = lines[source, n, 8 * block], lines[source, n, 8 * block + 3]
            left, right = tile - 2 * core, tile + 1 - 2 * core

            @pl.when((patch // 8 == mine) & (right >= 0) & (left < 2))
            def add():
                row = lines[source, n, 8 * block + 1] * LANES + lines[source, n, 8 * block + 2]
                shift = lines[source, n, 8 * block + 4]
                spot = pl.ds(lax.rem(patch, 8) * P_SIZE + row, S)
                value = held[source, pl.ds(pl.multiple_of(block * S, S), S), :].astype(jnp.float32)
                value = pltpu.roll(value, shift, 1)

                @pl.when(left >= 0)
                def first():
                    canvas[left, spot, :] += jnp.where(lane >= shift, value, 0.0)

                @pl.when(right < 2)
                def second():
                    canvas[right, spot, :] += jnp.where(lane >= shift, 0.0, value)

        return carry

    lax.fori_loop(0, parts_ref.shape[0] * count, one, 0)
    for band in range(out_ref.shape[0]):
        for patch in range(8):
            start = patch * P_SIZE + band * 2 * BAND
            for tile in range(2):
                rows = canvas[tile, start : start + 2 * BAND, :]
                out_ref[band, patch, :, tile * LANES : (tile + 1) * LANES] = rows.astype(jnp.bfloat16)


def place_halves(where, parts):
    sources = parts.shape[0]
    return pl.pallas_call(
        halves_kernel,
        out_shape=jax.ShapeDtypeStruct((P_SIZE // (2 * BAND), 8, 2 * BAND, 2 * LANES), jnp.bfloat16),
        in_specs=[pl.BlockSpec(memory_space=pltpu.SMEM), pl.BlockSpec(memory_space=pl.ANY)],
        out_specs=pl.BlockSpec(memory_space=pltpu.VMEM),
        scratch_shapes=[
            pltpu.VMEM(parts.shape, jnp.bfloat16),
            pltpu.VMEM((2, 8 * P_SIZE, LANES), jnp.float32),
            pltpu.VMEM((sources, 8, S), jnp.int32),
            pltpu.SMEM((sources, 8, S), jnp.int32),
            pltpu.SemaphoreType.DMA((2,)),
        ],
        compiler_params=pltpu.CompilerParams(vmem_limit_bytes=40 * 2**20),
        cost_estimate=pl.CostEstimate(flops=2**24, bytes_accessed=24 * 2**20, transcendentals=0),
        name="place_halves",
    )(where, parts)


def body(blocks, inv_variance, destinations, offsets, coefficients, basis_rows, basis_cols):
    owners = lax.axis_size("x") * lax.axis_size("z")
    weight = inv_variance[0]
    where = jnp.stack([lax.axis_index("x"), lax.axis_index("core")]).astype(jnp.int32)

    near = lax.all_gather(with_lines(weight, destinations[0], offsets[0]), ("core", "x"))
    den = place_halves(where, near)
    den = lax.psum_scatter(den, "y", scatter_dimension=0, tiled=True)
    den = lax.all_to_all(den.reshape(16, BAND, 2 * LANES), ("z", "core"), 0, 0, tiled=True)

    slots = match(blocks[0], weight, destinations[0], offsets[0], coefficients[0], basis_rows, basis_cols, owners)
    slots = lax.all_to_all(slots, ("x", "z"), 0, 0, tiled=True)
    told = slots[:, 2 * S : 2 * S + 2, :5].astype(jnp.int32).reshape(-1)
    num = place_whole(told, slots).reshape(16, BAND, P_SIZE)
    num = lax.all_to_all(num, ("y", "core"), 0, 0, tiled=True)

    num = jnp.sum(num.astype(jnp.float32), axis=0)
    den = jnp.sum(den.reshape(8, 2, BAND, 2 * LANES).astype(jnp.float32), axis=0)
    den = jnp.concatenate([den[0], den[1]], axis=-1)
    return (num / jnp.maximum(den, 1.0))[None]


def solution(mesh):
    visits = mesh.shape["visit"]
    grid = Mesh(mesh.devices.reshape(visits // 2, 2, 4, mesh.shape["patch"] // 4), ("y", "core", "x", "z"))
    visit, patch = ("y", "core"), ("x", "z")
    return jax.shard_map(
        body,
        mesh=grid,
        in_specs=(
            P(visit, patch, None, None),
            P(visit, patch, None, None),
            P(visit, patch, None),
            P(visit, patch, None, None),
            P(visit, patch, None),
            P(),
            P(),
        ),
        out_specs=P(patch, visit, None),
        check_vma=False,
    )
```

time: 191 us -> 171 us (0.90)
  starting transfers between devices: 59.9 us -> 28.2 us
  blocking collectives: 0 us -> 29.4 us
  waiting for transfers between devices: 84.8 us -> 65.3 us
  local copies, waits for them, and re-layouts: 8.16 us -> 11.3 us
    all_to_all x1, waiting for transfers between devices: 42.5 us -> 0.01 us  [body(): slots = lax.all_to_all(slots, ('x', 'z'), 0, 0, tiled=True)]
    all_gather x0 -> x1, waiting for transfers between devices: none -> 36.2 us  [body(): lax.all_gather(with_lines(weight, destinations[0], offsets[0]), ('core',...]
    ppermute x7 -> x0, starting transfers between devices: 34.3 us -> none  [the longest x4 24.2 us: body(): parts += [part, lax.ppermute(part, 'core', [(0, 1), (1, 0)])]]
    all_to_all x0 -> x1, blocking collectives: none -> 29.4 us  [body(): num = lax.all_to_all(num, ('y', 'core'), 0, 0, tiled=True)]
    all_to_all x2 -> x1, waiting for transfers between devices: 23.7 us -> 11.6 us  [body(): lax.all_to_all(den.reshape(16, BAND, 2 * LANES), ('z', 'core'), 0, 0, til...]
    ppermute x7 -> x0, waiting for transfers between devices: 2.01 us -> none  [the longest x3 2 us: body(): lax.ppermute(terms, 'x', [(i, (i + lag) % 4) for i in range(4)])]
    unnamed x11 -> x13, local copies, waits for them, and re-layouts: 7.05 us -> 8.82 us
    all_to_all x2 -> x1, starting transfers between devices: 13.3 us -> 14.5 us  [body(): lax.all_to_all(den.reshape(16, BAND, 2 * LANES), ('z', 'core'), 0, 0, til...]
  transfers between devices with their start and end apart: 11 -> 4, of which waited for: 6 -> 3; matrix products, arithmetic and copies ran while one was open for 0% -> 2% of each run, Pallas kernels for 10% -> 12%
where the time goes in v4:
time: 171 us
  waiting for transfers between devices  65.3 us (38%)
  blocking collectives  29.4 us (17%)
  starting transfers between devices  28.2 us (16%)
  Pallas kernels  21.6 us (13%)
  between operations  13.5 us (8%)
  local copies, waits for them, and re-layouts  11.3 us (7%)
    all_gather x1, waiting for transfers between devices, body(): lax.all_gather(with_lines(weight, destinations[0], offsets[0]), ('core',...  36.2 us
    all_to_all x1, blocking collectives, body(): num = lax.all_to_all(num, ('y', 'core'), 0, 0, tiled=True)  29.4 us
    reduce_scatter x1, waiting for transfers between devices, body(): den = lax.psum_scatter(den, 'y', scatter_dimension=0, tiled=True)  17.4 us
    all_to_all x1, starting transfers between devices, body(): lax.all_to_all(den.reshape(16, BAND, 2 * LANES), ('z', 'core'), 0, 0, til...  14.5 us
    all_to_all x1, starting transfers between devices, body(): slots = lax.all_to_all(slots, ('x', 'z'), 0, 0, tiled=True)  13.7 us
    pallas_call x1, Pallas kernels, place_halves(): pl.pallas_call(halves_kernel, out_shape=jax.ShapeDtypeStruct((P_SIZE // (...  12 us
    all_to_all x1, waiting for transfers between devices, body(): lax.all_to_all(den.reshape(16, BAND, 2 * LANES), ('z', 'core'), 0, 0, til...  11.6 us
    unnamed x13, local copies, waits for them, and re-layouts  8.82 us
  transfers between devices with their start and end apart: 4, of which 3 were waited for; matrix products, arithmetic and copies ran while one was open for 2% of the time, Pallas kernels for 12%

profile of v4, /device:TPU:1, one launch (start us, length us, event | category | flops | bytes accessed | tf_op | source)
XLA Modules:
  0.0 170.8 jit_solution(4672430760529762588)
XLA Ops:
  6.5 0.8 copy.14.dest_ref
  7.3 0.8 copy.15.off_ref
  8.1 1.0 copy-done.3
  9.1 1.8 %lines.1 = bf16[2064,128]{1,0:T(8,128)(2,1)} custom-call(s32[16,2]{1,0:T(8,128)S(1)} %copy.14.dest_ref, s32[16,2,2]{2,1,0:T(2,128)S(1)} %copy.15.off_ref, bf16[2048,128]{1,0:T(8,128)(2,1)S(1)} %bitcast.17), custom_call_target="tpu_custom_call" | custom-call | flops 65536 | bytes 1048576 | tf_op jit(solution)/shard_map/lines/pallas_call | solution.py:124
  11.0 0.8 copy.13
  11.8 0.8 rev.3
  12.5 0.8 fusion.4.taps_ref
  13.3 1.0 copy-done.4
  14.3 1.0 copy-done.5
  15.4 4.1 %match.1 = bf16[32,272,128]{2,1,0:T(8,128)(2,1)S(1)} custom-call(f32[16,15]{1,0:T(8,128)S(1)} %bitcast.19, s32[16,2]{1,0:T(8,128)S(1)} %copy.14.dest_ref, s32[16,2,2]{2,1,0:T(2,128)S(1)} %copy.15.off_ref, f32[16,128]{1,0:T(8,128)S(1)} %fusion.4.taps_ref, bf16[16,128,128]{2,1,0:T(8,128)(2,1)S(1)} %bitcast.20, bf16[16,128,128]{2,1,0:T(8,128)(2,1)S(1)} %bitcast.18), custom_call_target="tpu_custom_call" | custom-call | flops 1073741824 | bytes 16777216 | tf_op jit(solution)/shard_map/match/pallas_call | solution.py:86
  19.5 1.4 copy-done.2
  20.9 13.7 %all-to-all-start = ((bf16[32,272,128]{2,1,0:T(8,128)(2,1)}), bf16[32,272,128]{2,1,0:T(8,128)(2,1)S(1)}, u32[]{:S(2)}, u32[]{:S(2)}) async-start(bf16[32,272,128]{2,1,0:T(8,128)(2,1)} %copy-done.2), calls=%async_computation | async-start | bytes 4456448 | tf_op jit(solution)/shard_map/all_to_all | solution.py:251
  34.7 0.1 pad_add_fusion.where_ref
  34.7 36.2 %all-gather.3.cloned.1.call-done = bf16[16512,128]{1,0:T(8,128)(2,1)} async-done(((bf16[2064,128]{1,0:T(8,128)(2,1)}), bf16[16512,128]{1,0:T(8,128)(2,1)}) %all-gather.3.cloned.1.call-update) | async-done | bytes 4227088 | tf_op jit(solution)/shard_map/all_gather | solution.py:245
  70.9 2.2 %copy-done.1 = bf16[16512,128]{1,0:T(8,128)(2,1)S(1)} copy-done((bf16[16512,128]{1,0:T(8,128)(2,1)S(1)}, bf16[16512,128]{1,0:T(8,128)(2,1)}, u32[]{:S(2)}) %copy-start.1) | copy-done | bytes 4227096
  73.1 12.0 %place_halves.1 = bf16[8,8,64,256]{3,2,1,0:T(8,128)(2,1)S(1)} custom-call(s32[2]{0:T(128)S(1)} %pad_add_fusion.where_ref, bf16[8,2064,128]{2,1,0:T(8,128)(2,1)S(1)} %bitcast.15), custom_call_target="tpu_custom_call" | custom-call | flops 16777216 | bytes 25165824 | tf_op jit(solution)/shard_map/place_halves/pallas_call | solution.py:222
  85.2 1.3 copy-done
  86.6 0.1 reshape.51.meta_ref
  86.7 3.6 %place_whole.1 = bf16[512,512]{1,0:T(8,128)(2,1)S(1)} custom-call(s32[320]{0:T(512)S(1)} %reshape.51.meta_ref, bf16[32,272,128]{2,1,0:T(8,128)(2,1)S(1)} %all-to-all-done.slots_ref), custom_call_target="tpu_custom_call" | custom-call | flops 8388608 | bytes 16777216 | tf_op jit(solution)/shard_map/place_whole/pallas_call | solution.py:161
  90.3 29.4 %all_to_all.15 = bf16[16,32,512]{2,1,0:T(8,128)(2,1)S(1)} all-to-all(bf16[16,32,512]{2,1,0:T(8,128)(2,1)S(1)} %bitcast.16), channel_id=1, replica_groups=mesh['y'=8,'core'=2,'x'=4,'z'=8] {'y','core'}, dimensions={0} | all-to-all | bytes 1048576 | tf_op jit(solution)/shard_map/all_to_all | solution.py:254
  119.7 17.4 %reduce-scatter.2.cloned.1.call-done = bf16[1,8,64,256]{3,2,1,0:T(8,128)(2,1)} async-done(((bf16[8,8,64,256]{3,2,1,0:T(8,128)(2,1)}), bf16[1,8,64,256]{3,2,1,0:T(8,128)(2,1)}) %reduce-scatter.2.cloned.1.call-update) | async-done | bytes 262160 | tf_op jit(solution)/shard_map/reduce_scatter | solution.py:247
  137.1 14.5 %all-to-all-start.2 = ((bf16[16,32,256]{2,1,0:T(8,128)(2,1)}), bf16[16,32,256]{2,1,0:T(8,128)(2,1)S(1)}, u32[]{:S(2)}, u32[]{:S(2)}) async-start(bf16[16,32,256]{2,1,0:T(8,128)(2,1)} %bitcast.22), calls=%async_computation.3 | async-start | bytes 524288 | tf_op jit(solution)/shard_map/all_to_all | solution.py:248
  151.6 11.6 %all-to-all-done.2 = bf16[16,32,256]{2,1,0:T(8,128)(2,1)S(1)} async-done(((bf16[16,32,256]{2,1,0:T(8,128)(2,1)}), bf16[16,32,256]{2,1,0:T(8,128)(2,1)S(1)}, u32[]{:S(2)}, u32[]{:S(2)}) %all-to-all-start.2) | async-done | bytes 262176 | tf_op jit(solution)/shard_map/all_to_all | solution.py:248
  163.3 0.6 fusion
  (15 shorter events, 0.2 us)
Async XLA Ops:
  6.5 64.4 %all-gather.3.cloned.1.call-start = ((), (), s32[]{:S(2)}) async-start(), calls=%async_computation.5 | async-start | bytes 4755456 | tf_op jit(solution)/shard_map/all_gather | solution.py:245
  8.1 1.0 copy-start.3
  13.3 1.0 copy-start.4
  14.3 1.0 copy-start.5
  19.5 1.4 copy-start.2
  20.9 65.7 %all-to-all-start = ((bf16[32,272,128]{2,1,0:T(8,128)(2,1)}), bf16[32,272,128]{2,1,0:T(8,128)(2,1)S(1)}, u32[]{:S(2)}, u32[]{:S(2)}) async-start(bf16[32,272,128]{2,1,0:T(8,128)(2,1)} %copy-done.2), calls=%async_computation | async-start | bytes 4456448 | tf_op jit(solution)/shard_map/all_to_all | solution.py:251
  34.6 102.5 %reduce-scatter.2.cloned.1.call-start = ((), (), s32[]{:S(2)}) async-start(), calls=%async_computation.4 | async-start | bytes 2359296 | tf_op jit(solution)/shard_map/reduce_scatter | solution.py:247
  70.9 2.2 %copy-start.1 = (bf16[16512,128]{1,0:T(8,128)(2,1)S(1)}, bf16[16512,128]{1,0:T(8,128)(2,1)}, u32[]{:S(2)}) copy-start(bf16[16512,128]{1,0:T(8,128)(2,1)} %all-gather.3.cloned.1.call-done) | copy-start | bytes 12681220
  85.2 1.3 copy-start
  137.1 26.2 %all-to-all-start.2 = ((bf16[16,32,256]{2,1,0:T(8,128)(2,1)}), bf16[16,32,256]{2,1,0:T(8,128)(2,1)S(1)}, u32[]{:S(2)}, u32[]{:S(2)}) async-start(bf16[16,32,256]{2,1,0:T(8,128)(2,1)} %bitcast.22), calls=%async_computation.3 | async-start | bytes 524288 | tf_op jit(solution)/shard_map/all_to_all | solution.py:248
Sparse Core Ops, SparseCore 0:
  11.1 59.7 all-gather.2
  86.7 50.4 reduce-scatter.1

commit v5 on v4

v5 whole, which is shorter than its diff:
```python
import functools

import jax
import jax.numpy as jnp
from jax import lax
from jax.experimental import pallas as pl
from jax.experimental.pallas import tpu as pltpu
from jax.sharding import Mesh
from jax.sharding import PartitionSpec as P

S = 128
P_SIZE = 512
TAPS = 41
HALF = (TAPS - 1) // 2
BASIS = 5
BAND = 32
LANES = 128
META = 16
LEAD = 4
GROUP = 4


def places(dest_ref, off_ref, block, n):
    row, col = off_ref[n, 0, block], off_ref[n, 1, block]
    return dest_ref[n, block], row // LANES, lax.rem(row, LANES), col // LANES, lax.rem(col, LANES)


def match_kernel(
    coef_ref, dest_ref, off_ref, rows_ref, cols_ref, blocks_ref, weight_ref,
    out_ref, near_ref, wide, rows_tab, cols_tab, stack, told, taken, sems,
):
    count = blocks_ref.shape[0]
    body = pltpu.make_async_copy(weight_ref, near_ref.at[pl.ds(0, count * S)], sems.at[0])
    body.start()
    line = lax.broadcasted_iota(jnp.int32, (META, S), 0)
    lane = lax.broadcasted_iota(jnp.int32, (META, S), 1)
    words = jnp.zeros((META, S), jnp.int32)
    for block in range(count):
        for n in range(2):
            for at, number in enumerate(places(dest_ref, off_ref, block, n)):
                words = jnp.where((line == n) & (lane == 8 * block + at), number, words)
    told[...] = words.astype(jnp.float32).astype(jnp.bfloat16)
    tail = pltpu.make_async_copy(told, near_ref.at[pl.ds(count * S, META)], sems.at[1])
    tail.start()

    row_id = lax.broadcasted_iota(jnp.int32, (S, S), 0)
    col_id = lax.broadcasted_iota(jnp.int32, (S, S), 1)
    inside = jnp.abs(row_id - col_id) <= HALF
    wide[...] = jnp.zeros_like(wide)
    wide[0:BASIS, LEAD : LEAD + TAPS] = rows_ref[...].astype(jnp.float32)
    wide[8 : 8 + BASIS, LEAD : LEAD + TAPS] = cols_ref[...].astype(jnp.float32)
    for which in range(2):
        for k in range(BASIS):
            taps = jnp.broadcast_to(wide[which * 8 + k : which * 8 + k + 1, :], (8, S))
            band = jnp.concatenate(
                [pltpu.roll(taps, (S - HALF - LEAD + row) % S, 1, stride=1, stride_axis=0) for row in range(0, S, 8)]
            )
            band = jnp.where(inside, band, 0.0).astype(jnp.bfloat16)
            if which:
                cols_tab[:, k * S : (k + 1) * S] = band
            else:
                rows_tab[k * S : (k + 1) * S, :] = band
    y = (lax.broadcasted_iota(jnp.int32, (S, 1), 0).astype(jnp.float32) - (S - 1) / 2.0) / S
    x = (lax.broadcasted_iota(jnp.int32, (1, S), 1).astype(jnp.float32) - (S - 1) / 2.0) / S

    def clear(patch, carry):
        taken[patch] = 0
        out_ref[patch, 2 * S : 2 * S + META, :] = jnp.zeros((META, S), jnp.bfloat16)
        return carry

    lax.fori_loop(0, out_ref.shape[0], clear, 0)

    def some(step, carry):
        for part in range(GROUP):
            i = step * GROUP + part
            across = lax.dot_general(
                blocks_ref[i], rows_tab[...], (((1,), (1,)), ((), ())), preferred_element_type=jnp.float32
            )
            for k in range(BASIS):
                image = across[:, k * S : (k + 1) * S]
                plain = coef_ref[3 * k, i] + coef_ref[3 * k + 2, i] * x
                stack[part, k * S : (k + 1) * S, 0:S] = (image * plain).astype(jnp.bfloat16)
                stack[part, k * S : (k + 1) * S, S : 2 * S] = (image * coef_ref[3 * k + 1, i]).astype(jnp.bfloat16)
        for part in range(GROUP):
            i = step * GROUP + part
            sums = jnp.dot(cols_tab[...], stack[part], preferred_element_type=jnp.float32)
            weight = weight_ref[pl.ds(pl.multiple_of(i * S, S), S), :].astype(jnp.float32)
            term = ((sums[:, 0:S] + y * sums[:, S : 2 * S]) * weight).astype(jnp.bfloat16)
            for n in range(2):
                patch, *numbers = places(dest_ref, off_ref, i, n)
                slot = taken[patch]
                taken[patch] = slot + 1
                out_ref[patch, pl.ds(pl.multiple_of(slot * S, S), S), :] = term
                notes = out_ref[patch, 2 * S : 2 * S + META, :].astype(jnp.float32).astype(jnp.int32)
                for at, number in enumerate([1] + numbers):
                    notes = jnp.where((line == slot) & (lane == at), number, notes)
                out_ref[patch, 2 * S : 2 * S + META, :] = notes.astype(jnp.float32).astype(jnp.bfloat16)
        return carry

    lax.fori_loop(0, count // GROUP, some, 0)
    body.wait()
    tail.wait()


def match(blocks, weight, destinations, offsets, coefficients, basis_rows, basis_cols, owners):
    vmem = pl.BlockSpec(memory_space=pltpu.VMEM)
    smem = pl.BlockSpec(memory_space=pltpu.SMEM)
    rows = weight.shape[0] * S
    return pl.pallas_call(
        match_kernel,
        out_shape=[
            jax.ShapeDtypeStruct((owners, 2 * S + META, S), jnp.bfloat16),
            jax.ShapeDtypeStruct((rows + META, S), jnp.bfloat16),
        ],
        in_specs=[smem, smem, smem, vmem, vmem, vmem, vmem],
        out_specs=[vmem, vmem],
        scratch_shapes=[
            pltpu.VMEM((16, S), jnp.float32),
            pltpu.VMEM((BASIS * S, S), jnp.bfloat16),
            pltpu.VMEM((S, BASIS * S), jnp.bfloat16),
            pltpu.VMEM((GROUP, BASIS * S, 2 * S), jnp.bfloat16),
            pltpu.VMEM((META, S), jnp.bfloat16),
            pltpu.SMEM((owners,), jnp.int32),
            pltpu.SemaphoreType.DMA((2,)),
        ],
        compiler_params=pltpu.CompilerParams(vmem_limit_bytes=32 * 2**20),
        cost_estimate=pl.CostEstimate(flops=2**30, bytes_accessed=16 * 2**20, transcendentals=0),
        name="match",
    )(
        coefficients.T,
        destinations.T,
        jnp.transpose(offsets, (1, 2, 0)),
        basis_rows,
        basis_cols,
        blocks,
        weight.reshape(rows, S),
    )


def listed(codes, total, queue, idle):
    def one(i, found):
        code = codes(i)
        queue[found] = code
        return found + jnp.where(code >= 0, 1, 0)

    found = lax.fori_loop(0, total, one, jnp.int32(0), unroll=8)
    queue[found] = idle
    queue[found + 1] = idle
    return found


def add_pieces(queue, found, blocks, canvas):
    lane = lax.broadcasted_iota(jnp.int32, (S, LANES), 1)

    def pair(step, carry):
        values = []
        for part in range(2):
            code = queue[2 * step + part]
            shift = code & 127
            value = pltpu.roll(blocks((code >> 7) & 127).astype(jnp.float32), shift, 1)
            values.append((code >> 17, (code >> 14) & 7, value, lane >= shift))
        for row, tile, value, here in values:
            canvas[tile, pl.ds(row, S), :] += jnp.where(here, value, 0.0)
            canvas[tile + 1, pl.ds(row, S), :] += jnp.where(here, 0.0, value)
        return carry

    lax.fori_loop(0, (found + 1) // 2, pair, 0)


def whole_kernel(slots_ref, out_ref, canvas, told, codes, queue, sem):
    sources = slots_ref.shape[0]
    notes = slots_ref[:, 2 * S : 2 * S + META, :].astype(jnp.float32).astype(jnp.int32)[:, 0:8, :]
    notes = notes.reshape(sources * 8, S)
    at = [notes] + [pltpu.roll(notes, S - i, 1) for i in range(1, 5)]
    place = lax.broadcasted_iota(jnp.int32, notes.shape, 0)
    place = (place >> 3) * 2 + (place & 7)
    code = ((at[1] * LANES + at[2]) << 17) + (at[3] << 14) + (place << 7) + at[4]
    code = jnp.where(at[0] > 0, code, -1)[:, 0:1].reshape(sources, 8, 1)
    lane = lax.broadcasted_iota(jnp.int32, (sources, 8, S), 2)
    source = lax.broadcasted_iota(jnp.int32, (sources, 8, S), 0)
    told[...] = jnp.sum(jnp.where(lane == source, code, 0), axis=0)
    tell = pltpu.make_async_copy(told, codes, sem)
    tell.start()
    for tile in range(P_SIZE // LANES):
        canvas[tile] = jnp.zeros((P_SIZE, LANES), jnp.float32)
    tell.wait()
    found = listed(lambda i: codes[i & 1, i >> 1], 2 * sources, queue, (P_SIZE // LANES) << 14)

    def block(i):
        return slots_ref[i >> 1, pl.ds(pl.multiple_of((i & 1) * S, S), S), :]

    add_pieces(queue, found, block, canvas)
    for tile in range(P_SIZE // LANES):
        out_ref[:, tile * LANES : (tile + 1) * LANES] = canvas[tile].astype(jnp.bfloat16)


def place_whole(slots):
    sources = slots.shape[0]
    return pl.pallas_call(
        whole_kernel,
        out_shape=jax.ShapeDtypeStruct((P_SIZE, P_SIZE), jnp.bfloat16),
        in_specs=[pl.BlockSpec(memory_space=pltpu.VMEM)],
        out_specs=pl.BlockSpec(memory_space=pltpu.VMEM),
        scratch_shapes=[
            pltpu.VMEM((P_SIZE // LANES + 2, P_SIZE, LANES), jnp.float32),
            pltpu.VMEM((8, S), jnp.int32),
            pltpu.SMEM((8, S), jnp.int32),
            pltpu.SMEM((2 * sources + 2,), jnp.int32),
            pltpu.SemaphoreType.DMA,
        ],
        compiler_params=pltpu.CompilerParams(vmem_limit_bytes=24 * 2**20),
        cost_estimate=pl.CostEstimate(flops=2**23, bytes_accessed=16 * 2**20, transcendentals=0),
        name="place_whole",
    )(slots)


def halves_kernel(where_ref, *refs):
    parts, (out_ref, held, canvas, told, codes, queue, sems) = refs[:8], refs[8:]
    count, sources = held.shape[1] // S, len(parts)
    copies = [pltpu.make_async_copy(part, held.at[i], sems.at[i]) for i, part in enumerate(parts)]
    for copy in copies:
        copy.start()
    mine, core = where_ref[0], where_ref[1]
    for tile in (1, 2):
        canvas[tile] = jnp.zeros((8 * P_SIZE, LANES), jnp.float32)
    for copy in copies:
        copy.wait()
    notes = held[:, count * S : count * S + META, :].astype(jnp.float32).astype(jnp.int32)[:, 0:8, :]
    notes = notes.reshape(sources * 8, S)
    at = [notes] + [pltpu.roll(notes, S - i, 1) for i in range(1, 5)]
    place = lax.broadcasted_iota(jnp.int32, notes.shape, 0) >> 3
    place = place * count + (lax.broadcasted_iota(jnp.int32, notes.shape, 1) >> 3)
    tile = at[3] - 2 * core + 1
    row = (at[0] & 7) * P_SIZE + at[1] * LANES + at[2]
    code = (row << 17) + (tile << 14) + (place << 7) + at[4]
    code = jnp.where(((at[0] >> 3) == mine) & (tile >= 0) & (tile <= 2), code, -1)
    first = (lax.broadcasted_iota(jnp.int32, (8, S), 1) & 7) == 0
    words = jnp.zeros((8, S), jnp.int32)
    for i in range(sources):
        words += pltpu.roll(jnp.where(first, code[8 * i : 8 * i + 8, :], 0), i, 1)
    told[...] = words
    tell = pltpu.make_async_copy(told, codes, sems.at[sources])
    tell.start()
    tell.wait()

    found = listed(lambda i: codes[i // S, lax.rem(i, S)], 2 * sources * count, queue, 3 << 14)

    def block(i):
        return held[lax.div(i, count), pl.ds(pl.multiple_of(lax.rem(i, count) * S, S), S), :]

    add_pieces(queue, found, block, canvas)
    for band in range(out_ref.shape[0]):
        for patch in range(8):
            start = patch * P_SIZE + band * 2 * BAND
            for half in range(2):
                rows = canvas[half + 1, start : start + 2 * BAND, :]
                out_ref[band, patch, :, half * LANES : (half + 1) * LANES] = rows.astype(jnp.bfloat16)


def place_halves(where, parts):
    sources = len(parts)
    pieces = 2 * sources * (parts[0].shape[0] // S)
    return pl.pallas_call(
        halves_kernel,
        out_shape=jax.ShapeDtypeStruct((P_SIZE // (2 * BAND), 8, 2 * BAND, 2 * LANES), jnp.bfloat16),
        in_specs=[pl.BlockSpec(memory_space=pltpu.SMEM)] + [pl.BlockSpec(memory_space=pl.ANY)] * sources,
        out_specs=pl.BlockSpec(memory_space=pltpu.VMEM),
        scratch_shapes=[
            pltpu.VMEM((sources,) + parts[0].shape, jnp.bfloat16),
            pltpu.VMEM((5, 8 * P_SIZE, LANES), jnp.float32),
            pltpu.VMEM((8, S), jnp.int32),
            pltpu.SMEM((8, S), jnp.int32),
            pltpu.SMEM((pieces + 2,), jnp.int32),
            pltpu.SemaphoreType.DMA((sources + 1,)),
        ],
        compiler_params=pltpu.CompilerParams(vmem_limit_bytes=40 * 2**20),
        cost_estimate=pl.CostEstimate(flops=2**24, bytes_accessed=24 * 2**20, transcendentals=0),
        name="place_halves",
    )(where, *parts)


def body(blocks, inv_variance, destinations, offsets, coefficients, basis_rows, basis_cols):
    owners = lax.axis_size("x") * lax.axis_size("z")
    where = jnp.stack([lax.axis_index("x"), lax.axis_index("core")]).astype(jnp.int32)
    slots, near = match(
        blocks[0], inv_variance[0], destinations[0], offsets[0], coefficients[0], basis_rows, basis_cols, owners
    )

    parts = []
    for lag in range(4):
        part = lax.ppermute(near, "x", [(i, (i + lag) % 4) for i in range(4)]) if lag else near
        parts += [part, lax.ppermute(part, "core", [(0, 1), (1, 0)])]
    den = place_halves(where, parts)
    den = lax.psum_scatter(den, "y", scatter_dimension=0, tiled=True)
    den = lax.all_to_all(den.reshape(16, BAND, 2 * LANES), ("z", "core"), 0, 0, tiled=True)

    slots = lax.all_to_all(slots, ("x", "z"), 0, 0, tiled=True)
    num = place_whole(slots).reshape(16, BAND, P_SIZE)
    num = lax.all_to_all(num, ("y", "core"), 0, 0, tiled=True)

    num = jnp.sum(num.astype(jnp.float32), axis=0)
    den = jnp.sum(den.reshape(8, 2, BAND, 2 * LANES).astype(jnp.float32), axis=0)
    den = jnp.concatenate([den[0], den[1]], axis=-1)
    return (num / jnp.maximum(den, 1.0))[None]


def solution(mesh):
    visits = mesh.shape["visit"]
    grid = Mesh(mesh.devices.reshape(visits // 2, 2, 4, mesh.shape["patch"] // 4), ("y", "core", "x", "z"))
    visit, patch = ("y", "core"), ("x", "z")
    return jax.shard_map(
        body,
        mesh=grid,
        in_specs=(
            P(visit, patch, None, None),
            P(visit, patch, None, None),
            P(visit, patch, None),
            P(visit, patch, None, None),
            P(visit, patch, None),
            P(),
            P(),
        ),
        out_specs=P(patch, visit, None),
        check_vma=False,
    )
```

time: 171 us -> 178 us (1.041); the launches traced: 171 us -> 175 us
  starting transfers between devices: 28.2 us -> 72.5 us
  blocking collectives: 29.4 us -> 0 us
  Pallas kernels: 21.6 us -> 16.3 us
  local copies, waits for them, and re-layouts: 11.3 us -> 8.17 us
    ppermute x0 -> x7, starting transfers between devices: none -> 42.3 us  [the longest x4 33 us: body(): parts += [part, lax.ppermute(part, 'core', [(0, 1), (1, 0)])]]
    all_gather x1 -> x0, waiting for transfers between devices: 36.2 us -> none  [body(): lax.all_gather(with_lines(weight, destinations[0], offsets[0]), ('core',...]
    all_to_all x1 -> x0, blocking collectives: 29.4 us -> none  [body(): num = lax.all_to_all(num, ('y', 'core'), 0, 0, tiled=True)]
    reduce_scatter x1, waiting for transfers between devices: 17.4 us -> 37.9 us  [body(): den = lax.psum_scatter(den, 'y', scatter_dimension=0, tiled=True)]
    ppermute x0 -> x7, waiting for transfers between devices: none -> 14.6 us  [the longest x3 12.9 us: body(): lax.ppermute(near, 'x', [(i, (i + lag) % 4) for i in range(4)])]
    all_to_all x0 -> x1, starting transfers between devices: none -> 7.4 us  [body(): num = lax.all_to_all(num, ('y', 'core'), 0, 0, tiled=True)]
    all_to_all x1, starting transfers between devices: 14.5 us -> 8.97 us  [body(): lax.all_to_all(den.reshape(16, BAND, 2 * LANES), ('z', 'core'), 0, 0, til...]
    pallas_call x1, Pallas kernels: 12 us -> 8.38 us  [place_halves(): pl.pallas_call(halves_kernel, out_shape=jax.ShapeDtypeStruct((P_SIZE // (...]
  transfers between devices with their start and end apart: 4 -> 11, of which waited for: 3 -> 4; matrix products, arithmetic and copies ran while one was open for 2% -> 0% of each run, Pallas kernels for 12% -> 7%
where the time goes in v5:
time: 178 us; the launch traced here: 175 us
  starting transfers between devices  72.5 us (41%)
  waiting for transfers between devices  64.1 us (36%)
  Pallas kernels  16.3 us (9%)
  between operations  13.6 us (8%)
  local copies, waits for them, and re-layouts  8.17 us (5%)
    reduce_scatter x1, waiting for transfers between devices, body(): den = lax.psum_scatter(den, 'y', scatter_dimension=0, tiled=True)  37.9 us
    ppermute x4, starting transfers between devices, body(): parts += [part, lax.ppermute(part, 'core', [(0, 1), (1, 0)])]  33 us
    all_to_all x1, starting transfers between devices, body(): slots = lax.all_to_all(slots, ('x', 'z'), 0, 0, tiled=True)  13.7 us
    ppermute x3, waiting for transfers between devices, body(): lax.ppermute(near, 'x', [(i, (i + lag) % 4) for i in range(4)])  12.9 us
    all_to_all x1, waiting for transfers between devices, body(): lax.all_to_all(den.reshape(16, BAND, 2 * LANES), ('z', 'core'), 0, 0, til...  11.6 us
    ppermute x3, starting transfers between devices, body(): lax.ppermute(near, 'x', [(i, (i + lag) % 4) for i in range(4)])  9.33 us
    all_to_all x1, starting transfers between devices, body(): lax.all_to_all(den.reshape(16, BAND, 2 * LANES), ('z', 'core'), 0, 0, til...  8.97 us
    pallas_call x1, Pallas kernels, place_halves(): pl.pallas_call(halves_kernel, out_shape=jax.ShapeDtypeStruct((P_SIZE // (...  8.38 us
  transfers between devices with their start and end apart: 11, of which 4 were waited for; matrix products, arithmetic and copies ran while one was open for 0% of the time, Pallas kernels for 7%

profile of v5, /device:TPU:1, one launch (start us, length us, event | category | flops | bytes accessed | tf_op | source)
XLA Modules:
  0.0 175.5 jit_solution(1538771330414760888)
XLA Ops:
  6.5 0.7 copy.10
  7.2 1.0 copy-done.2
  8.3 1.0 copy-done.3
  9.3 0.7 copy-done.4
  10.0 0.7 copy-done.5
  12.0 4.3 %match.1 = (bf16[32,272,128]{2,1,0:T(8,128)(2,1)S(1)}, bf16[2064,128]{1,0:T(8,128)(2,1)S(1)}) custom-call(f32[15,16]{1,0:T(8,128)S(1)} %bitcast.21, s32[2,16]{1,0:T(2,128)S(1)} %bitcast.25, s32[2,2,16]{2,1,0:T(2,128)S(1)} %bitcast.24, bf16[5,41]{1,0:T(8,128)(2,1)S(1)} %copy-done.5, bf16[5,41]{1,0:T(8,128)(2,1)S(1)} %copy-done.6, ...), custom_call_target="tpu_custom_call" | custom-call | flops 1073741824 | bytes 16777216 | tf_op jit(solution)/shard_map/match/pallas_call | solution.py:109
  16.3 1.4 copy-done.1
  17.7 13.7 %all-to-all-start = ((bf16[32,272,128]{2,1,0:T(8,128)(2,1)}), bf16[32,272,128]{2,1,0:T(8,128)(2,1)S(1)}, u32[]{:S(2)}, u32[]{:S(2)}) async-start(bf16[32,272,128]{2,1,0:T(8,128)(2,1)} %copy-done.1), calls=%async_computation | async-start | bytes 4456448 | tf_op jit(solution)/shard_map/all_to_all | solution.py:297
  31.5 4.4 %collective-permute-start.5 = (bf16[2064,128]{1,0:T(8,128)(2,1)S(1)}, bf16[2064,128]{1,0:T(8,128)(2,1)S(1)}, u32[]{:S(2)}, u32[]{:S(2)}) collective-permute-start(bf16[2064,128]{1,0:T(8,128)(2,1)S(1)} %get-tuple-element.8.refs_0_), channel_id=1, source_target_pairs={{0,24},{8,0},{16,8},{24,16},{1,25},{9,1},{17,9},{25,17},{2,26},{10... | collective-permute-start | bytes 1585160 | tf_op jit(solution)/shard_map/ppermute | solution.py:291
  35.9 2.4 %collective-permute-start.3 = (bf16[2064,128]{1,0:T(8,128)(2,1)S(1)}, bf16[2064,128]{1,0:T(8,128)(2,1)}, u32[]{:S(2)}, u32[]{:S(2)}) collective-permute-start(bf16[2064,128]{1,0:T(8,128)(2,1)S(1)} %get-tuple-element.8.refs_0_), channel_id=1, source_target_pairs={{0,16},{8,24},{16,0},{24,8},{1,17},{9,25},{17,1},{25,9},{2,18},{10... | collective-permute-start | bytes 1585160 | tf_op jit(solution)/shard_map/ppermute | solution.py:291
  38.3 2.5 %collective-permute-start.1 = (bf16[2064,128]{1,0:T(8,128)(2,1)S(1)}, bf16[2064,128]{1,0:T(8,128)(2,1)}, u32[]{:S(2)}, u32[]{:S(2)}) collective-permute-start(bf16[2064,128]{1,0:T(8,128)(2,1)S(1)} %get-tuple-element.8.refs_0_), channel_id=1, source_target_pairs={{0,8},{8,16},{16,24},{24,0},{1,9},{9,17},{17,25},{25,1},{2,10},{10... | collective-permute-start | bytes 1585160 | tf_op jit(solution)/shard_map/ppermute | solution.py:291
  40.8 4.0 %collective-permute-start = (bf16[2064,128]{1,0:T(8,128)(2,1)S(1)}, bf16[2064,128]{1,0:T(8,128)(2,1)}, u32[]{:S(2)}, u32[]{:S(2)}) collective-permute-start(bf16[2064,128]{1,0:T(8,128)(2,1)S(1)} %get-tuple-element.8.refs_0_), channel_id=1, source_target_pairs={{0,32},{32,0},{1,33},{33,1},{2,34},{34,2},{3,35},{35,3},{4,36},{36... | collective-permute-start | bytes 1585160 | tf_op jit(solution)/shard_map/ppermute | solution.py:292
  44.8 12.9 %collective-permute-done.5.refs_6_ = bf16[2064,128]{1,0:T(8,128)(2,1)S(1)} collective-permute-done((bf16[2064,128]{1,0:T(8,128)(2,1)S(1)}, bf16[2064,128]{1,0:T(8,128)(2,1)S(1)}, u32[]{:S(2)}, u32[]{:S(2)}) %collective-permute-start.5) | collective-permute-done | bytes 528416 | tf_op jit(solution)/shard_map/ppermute | solution.py:291
  57.7 24.7 %collective-permute-start.6 = (bf16[2064,128]{1,0:T(8,128)(2,1)S(1)}, bf16[2064,128]{1,0:T(8,128)(2,1)}, u32[]{:S(2)}, u32[]{:S(2)}) collective-permute-start(bf16[2064,128]{1,0:T(8,128)(2,1)S(1)} %collective-permute-done.5.refs_6_), channel_id=1, source_target_pairs={{0,32},{32,0},{1,33},{33,1},{2,34},{34,2},{3,35},{35,3},{4,36},{36... | collective-permute-start | bytes 1585160 | tf_op jit(solution)/shard_map/ppermute | solution.py:292
  82.4 1.9 %collective-permute-start.4 = (bf16[2064,128]{1,0:T(8,128)(2,1)}, bf16[2064,128]{1,0:T(8,128)(2,1)}, u32[]{:S(2)}, u32[]{:S(2)}) collective-permute-start(bf16[2064,128]{1,0:T(8,128)(2,1)} %collective-permute-done.3.refs_4_), channel_id=1, source_target_pairs={{0,32},{32,0},{1,33},{33,1},{2,34},{34,2},{3,35},{35,3},{4,36},{36... | collective-permute-start | bytes 1585160 | tf_op jit(solution)/shard_map/ppermute | solution.py:292
  84.3 2.4 %collective-permute-start.2 = (bf16[2064,128]{1,0:T(8,128)(2,1)}, bf16[2064,128]{1,0:T(8,128)(2,1)}, u32[]{:S(2)}, u32[]{:S(2)}) collective-permute-start(bf16[2064,128]{1,0:T(8,128)(2,1)} %collective-permute-done.1.refs_2_), channel_id=1, source_target_pairs={{0,32},{32,0},{1,33},{33,1},{2,34},{34,2},{3,35},{35,3},{4,36},{36... | collective-permute-start | bytes 1585160 | tf_op jit(solution)/shard_map/ppermute | solution.py:292
  86.8 1.8 %collective-permute-done.2.refs_3_ = bf16[2064,128]{1,0:T(8,128)(2,1)} collective-permute-done((bf16[2064,128]{1,0:T(8,128)(2,1)}, bf16[2064,128]{1,0:T(8,128)(2,1)}, u32[]{:S(2)}, u32[]{:S(2)}) %collective-permute-start.2) | collective-permute-done | bytes 528416 | tf_op jit(solution)/shard_map/ppermute | solution.py:292
  88.6 8.4 %place_halves.1 = bf16[8,8,64,256]{3,2,1,0:T(8,128)(2,1)S(1)} custom-call(s32[2]{0:T(128)S(1)} %pad_add_fusion.where_ref, bf16[2064,128]{1,0:T(8,128)(2,1)S(1)} %get-tuple-element.8.refs_0_, bf16[2064,128]{1,0:T(8,128)(2,1)} %collective-permute-done.refs_1_, bf16[2064,128]{1,0:T(8,128)(2,1)} %collective-permute-done.1.refs_2_, ...), custom_call_target="tpu_custom_call" | custom-call | flops 16777216 | bytes 25165824 | tf_op jit(solution)/shard_map/place_halves/pallas_call | solution.py:263
  97.0 1.3 copy-done
  98.3 3.6 %place_whole.1 = bf16[512,512]{1,0:T(8,128)(2,1)} custom-call(bf16[32,272,128]{2,1,0:T(8,128)(2,1)S(1)} %all-to-all-done.slots_ref), custom_call_target="tpu_custom_call" | custom-call | flops 8388608 | bytes 16777216 | tf_op jit(solution)/shard_map/place_whole/pallas_call | solution.py:199
  102.0 7.4 %all-to-all-start.1 = ((bf16[16,32,512]{2,1,0:T(8,128)(2,1)}), bf16[16,32,512]{2,1,0:T(8,128)(2,1)S(1)}, u32[]{:S(2)}, u32[]{:S(2)}) async-start(bf16[16,32,512]{2,1,0:T(8,128)(2,1)} %bitcast.7), calls=%async_computation.1 | async-start | bytes 1048576 | tf_op jit(solution)/shard_map/all_to_all | solution.py:299
  109.4 37.9 %reduce-scatter.2.cloned.1.call-done = bf16[1,8,64,256]{3,2,1,0:T(8,128)(2,1)} async-done(((bf16[8,8,64,256]{3,2,1,0:T(8,128)(2,1)}), bf16[1,8,64,256]{3,2,1,0:T(8,128)(2,1)}) %reduce-scatter.2.cloned.1.call-update) | async-done | bytes 262160 | tf_op jit(solution)/shard_map/reduce_scatter | solution.py:294
  147.2 9.0 %all-to-all-start.2 = ((bf16[16,32,256]{2,1,0:T(8,128)(2,1)}), bf16[16,32,256]{2,1,0:T(8,128)(2,1)S(1)}, u32[]{:S(2)}, u32[]{:S(2)}) async-start(bf16[16,32,256]{2,1,0:T(8,128)(2,1)} %bitcast.27), calls=%async_computation.3 | async-start | bytes 524288 | tf_op jit(solution)/shard_map/all_to_all | solution.py:295
  156.3 11.6 %all-to-all-done.2 = bf16[16,32,256]{2,1,0:T(8,128)(2,1)S(1)} async-done(((bf16[16,32,256]{2,1,0:T(8,128)(2,1)}), bf16[16,32,256]{2,1,0:T(8,128)(2,1)S(1)}, u32[]{:S(2)}, u32[]{:S(2)}) %all-to-all-start.2) | async-done | bytes 262176 | tf_op jit(solution)/shard_map/all_to_all | solution.py:295
  (24 shorter events, 2.3 us)
Async XLA Ops:
  7.2 1.0 copy-start.2
  8.3 1.0 copy-start.3
  9.3 0.7 copy-start.4
  10.0 0.7 copy-start.5
  10.7 0.7 copy-start.6
  11.4 0.7 copy-start.7
  16.3 1.4 copy-start.1
  17.7 80.6 %all-to-all-start = ((bf16[32,272,128]{2,1,0:T(8,128)(2,1)}), bf16[32,272,128]{2,1,0:T(8,128)(2,1)S(1)}, u32[]{:S(2)}, u32[]{:S(2)}) async-start(bf16[32,272,128]{2,1,0:T(8,128)(2,1)} %copy-done.1), calls=%async_computation | async-start | bytes 4456448 | tf_op jit(solution)/shard_map/all_to_all | solution.py:297
  31.4 115.8 %reduce-scatter.2.cloned.1.call-start = ((), (), s32[]{:S(2)}) async-start(), calls=%async_computation.4 | async-start | bytes 2359296 | tf_op jit(solution)/shard_map/reduce_scatter | solution.py:294
  31.5 26.2 %collective-permute-start.5 = (bf16[2064,128]{1,0:T(8,128)(2,1)S(1)}, bf16[2064,128]{1,0:T(8,128)(2,1)S(1)}, u32[]{:S(2)}, u32[]{:S(2)}) collective-permute-start(bf16[2064,128]{1,0:T(8,128)(2,1)S(1)} %get-tuple-element.8.refs_0_), channel_id=1, source_target_pairs={{0,24},{8,0},{16,8},{24,16},{1,25},{9,1},{17,9},{25,17},{2,26},{10... | collective-permute-start | bytes 1585160 | tf_op jit(solution)/shard_map/ppermute | solution.py:291
  35.9 46.5 %collective-permute-start.3 = (bf16[2064,128]{1,0:T(8,128)(2,1)S(1)}, bf16[2064,128]{1,0:T(8,128)(2,1)}, u32[]{:S(2)}, u32[]{:S(2)}) collective-permute-start(bf16[2064,128]{1,0:T(8,128)(2,1)S(1)} %get-tuple-element.8.refs_0_), channel_id=1, source_target_pairs={{0,16},{8,24},{16,0},{24,8},{1,17},{9,25},{17,1},{25,9},{2,18},{10... | collective-permute-start | bytes 1585160 | tf_op jit(solution)/shard_map/ppermute | solution.py:291
  38.3 46.0 %collective-permute-start.1 = (bf16[2064,128]{1,0:T(8,128)(2,1)S(1)}, bf16[2064,128]{1,0:T(8,128)(2,1)}, u32[]{:S(2)}, u32[]{:S(2)}) collective-permute-start(bf16[2064,128]{1,0:T(8,128)(2,1)S(1)} %get-tuple-element.8.refs_0_), channel_id=1, source_target_pairs={{0,8},{8,16},{16,24},{24,0},{1,9},{9,17},{17,25},{25,1},{2,10},{10... | collective-permute-start | bytes 1585160 | tf_op jit(solution)/shard_map/ppermute | solution.py:291
  40.8 46.0 %collective-permute-start = (bf16[2064,128]{1,0:T(8,128)(2,1)S(1)}, bf16[2064,128]{1,0:T(8,128)(2,1)}, u32[]{:S(2)}, u32[]{:S(2)}) collective-permute-start(bf16[2064,128]{1,0:T(8,128)(2,1)S(1)} %get-tuple-element.8.refs_0_), channel_id=1, source_target_pairs={{0,32},{32,0},{1,33},{33,1},{2,34},{34,2},{3,35},{35,3},{4,36},{36... | collective-permute-start | bytes 1585160 | tf_op jit(solution)/shard_map/ppermute | solution.py:292
  57.7 29.2 %collective-permute-start.6 = (bf16[2064,128]{1,0:T(8,128)(2,1)S(1)}, bf16[2064,128]{1,0:T(8,128)(2,1)}, u32[]{:S(2)}, u32[]{:S(2)}) collective-permute-start(bf16[2064,128]{1,0:T(8,128)(2,1)S(1)} %collective-permute-done.5.refs_6_), channel_id=1, source_target_pairs={{0,32},{32,0},{1,33},{33,1},{2,34},{34,2},{3,35},{35,3},{4,36},{36... | collective-permute-start | bytes 1585160 | tf_op jit(solution)/shard_map/ppermute | solution.py:292
  82.4 4.4 %collective-permute-start.4 = (bf16[2064,128]{1,0:T(8,128)(2,1)}, bf16[2064,128]{1,0:T(8,128)(2,1)}, u32[]{:S(2)}, u32[]{:S(2)}) collective-permute-start(bf16[2064,128]{1,0:T(8,128)(2,1)} %collective-permute-done.3.refs_4_), channel_id=1, source_target_pairs={{0,32},{32,0},{1,33},{33,1},{2,34},{34,2},{3,35},{35,3},{4,36},{36... | collective-permute-start | bytes 1585160 | tf_op jit(solution)/shard_map/ppermute | solution.py:292
  84.3 4.3 %collective-permute-start.2 = (bf16[2064,128]{1,0:T(8,128)(2,1)}, bf16[2064,128]{1,0:T(8,128)(2,1)}, u32[]{:S(2)}, u32[]{:S(2)}) collective-permute-start(bf16[2064,128]{1,0:T(8,128)(2,1)} %collective-permute-done.1.refs_2_), channel_id=1, source_target_pairs={{0,32},{32,0},{1,33},{33,1},{2,34},{34,2},{3,35},{35,3},{4,36},{36... | collective-permute-start | bytes 1585160 | tf_op jit(solution)/shard_map/ppermute | solution.py:292
  97.0 1.3 copy-start
  102.0 45.3 %all-to-all-start.1 = ((bf16[16,32,512]{2,1,0:T(8,128)(2,1)}), bf16[16,32,512]{2,1,0:T(8,128)(2,1)S(1)}, u32[]{:S(2)}, u32[]{:S(2)}) async-start(bf16[16,32,512]{2,1,0:T(8,128)(2,1)} %bitcast.7), calls=%async_computation.1 | async-start | bytes 1048576 | tf_op jit(solution)/shard_map/all_to_all | solution.py:299
  147.2 20.7 %all-to-all-start.2 = ((bf16[16,32,256]{2,1,0:T(8,128)(2,1)}), bf16[16,32,256]{2,1,0:T(8,128)(2,1)S(1)}, u32[]{:S(2)}, u32[]{:S(2)}) async-start(bf16[16,32,256]{2,1,0:T(8,128)(2,1)} %bitcast.27), calls=%async_computation.3 | async-start | bytes 524288 | tf_op jit(solution)/shard_map/all_to_all | solution.py:295
Sparse Core Ops, SparseCore 0:
  98.4 48.7 reduce-scatter.1

commit v6 on v5

--- a/solution.py
+++ b/solution.py
@@ -26,23 +26,11 @@
 
 
 def match_kernel(
-    coef_ref, dest_ref, off_ref, rows_ref, cols_ref, blocks_ref, weight_ref,
-    out_ref, near_ref, wide, rows_tab, cols_tab, stack, told, taken, sems,
+    coef_ref, dest_ref, off_ref, rows_ref, cols_ref, blocks_ref, weight_ref, out_ref, wide, rows_tab, cols_tab, stack, taken
 ):
     count = blocks_ref.shape[0]
-    body = pltpu.make_async_copy(weight_ref, near_ref.at[pl.ds(0, count * S)], sems.at[0])
-    body.start()
     line = lax.broadcasted_iota(jnp.int32, (META, S), 0)
     lane = lax.broadcasted_iota(jnp.int32, (META, S), 1)
-    words = jnp.zeros((META, S), jnp.int32)
-    for block in range(count):
-        for n in range(2):
-            for at, number in enumerate(places(dest_ref, off_ref, block, n)):
-                words = jnp.where((line == n) & (lane == 8 * block + at), number, words)
-    told[...] = words.astype(jnp.float32).astype(jnp.bfloat16)
-    tail = pltpu.make_async_copy(told, near_ref.at[pl.ds(count * S, META)], sems.at[1])
-    tail.start()
-
     row_id = lax.broadcasted_iota(jnp.int32, (S, S), 0)
     col_id = lax.broadcasted_iota(jnp.int32, (S, S), 1)
     inside = jnp.abs(row_id - col_id) <= HALF
@@ -84,7 +72,7 @@
         for part in range(GROUP):
             i = step * GROUP + part
             sums = jnp.dot(cols_tab[...], stack[part], preferred_element_type=jnp.float32)
-            weight = weight_ref[pl.ds(pl.multiple_of(i * S, S), S), :].astype(jnp.float32)
+            weight = weight_ref[i].astype(jnp.float32)
             term = ((sums[:, 0:S] + y * sums[:, S : 2 * S]) * weight).astype(jnp.bfloat16)
             for n in range(2):
                 patch, *numbers = places(dest_ref, off_ref, i, n)
@@ -98,30 +86,22 @@
         return carry
 
     lax.fori_loop(0, count // GROUP, some, 0)
-    body.wait()
-    tail.wait()
 
 
 def match(blocks, weight, destinations, offsets, coefficients, basis_rows, basis_cols, owners):
     vmem = pl.BlockSpec(memory_space=pltpu.VMEM)
     smem = pl.BlockSpec(memory_space=pltpu.SMEM)
-    rows = weight.shape[0] * S
     return pl.pallas_call(
         match_kernel,
-        out_shape=[
-            jax.ShapeDtypeStruct((owners, 2 * S + META, S), jnp.bfloat16),
-            jax.ShapeDtypeStruct((rows + META, S), jnp.bfloat16),
-        ],
+        out_shape=jax.ShapeDtypeStruct((owners, 2 * S + META, S), jnp.bfloat16),
         in_specs=[smem, smem, smem, vmem, vmem, vmem, vmem],
-        out_specs=[vmem, vmem],
+        out_specs=vmem,
         scratch_shapes=[
             pltpu.VMEM((16, S), jnp.float32),
             pltpu.VMEM((BASIS * S, S), jnp.bfloat16),
             pltpu.VMEM((S, BASIS * S), jnp.bfloat16),
             pltpu.VMEM((GROUP, BASIS * S, 2 * S), jnp.bfloat16),
-            pltpu.VMEM((META, S), jnp.bfloat16),
             pltpu.SMEM((owners,), jnp.int32),
-            pltpu.SemaphoreType.DMA((2,)),
         ],
         compiler_params=pltpu.CompilerParams(vmem_limit_bytes=32 * 2**20),
         cost_estimate=pl.CostEstimate(flops=2**30, bytes_accessed=16 * 2**20, transcendentals=0),
@@ -133,8 +113,58 @@
         basis_rows,
         basis_cols,
         blocks,
-        weight.reshape(rows, S),
+        weight,
     )
+
+
+def lines_kernel(dest_ref, off_ref, weight_ref, near_ref):
+    rows = weight_ref.shape[0]
+    for copy in range(near_ref.shape[0]):
+        near_ref[copy, 0:rows, :] = weight_ref[...]
+    line = lax.broadcasted_iota(jnp.int32, (META, S), 0)
+    lane = lax.broadcasted_iota(jnp.int32, (META, S), 1)
+    words = jnp.zeros((META, S), jnp.int32)
+    for block in range(rows // S):
+        for n in range(2):
+            for at, number in enumerate(places(dest_ref, off_ref, block, n)):
+                words = jnp.where((line == n) & (lane == 8 * block + at), number, words)
+    words = words.astype(jnp.float32).astype(jnp.bfloat16)
+    for copy in range(near_ref.shape[0]):
+        near_ref[copy, rows : rows + META, :] = words
+
+
+def with_lines(weight, destinations, offsets, copies):
+    smem = pl.BlockSpec(memory_space=pltpu.SMEM)
+    vmem = pl.BlockSpec(memory_space=pltpu.VMEM)
+    rows = weight.shape[0] * S
+    return pl.pallas_call(
+        lines_kernel,
+        out_shape=jax.ShapeDtypeStruct((copies, rows + META, S), jnp.bfloat16),
+        in_specs=[smem, smem, vmem],
+        out_specs=vmem,
+        compiler_params=pltpu.CompilerParams(vmem_limit_bytes=8 * 2**20),
+        cost_estimate=pl.CostEstimate(flops=2**16, bytes_accessed=2**22, transcendentals=0),
+        name="lines",
+    )(destinations.T, jnp.transpose(offsets, (1, 2, 0)), weight.reshape(rows, S))
+
+
+def together_kernel(large_ref, small_ref, large_out, small_out):
+    small_out[...] = small_ref[...]
+
+
+def together(large, small):
+    hbm = pl.BlockSpec(memory_space=pltpu.HBM)
+    vmem = pl.BlockSpec(memory_space=pltpu.VMEM)
+    return pl.pallas_call(
+        together_kernel,
+        out_shape=[jax.ShapeDtypeStruct(array.shape, array.dtype) for array in (large, small)],
+        in_specs=[hbm, vmem],
+        out_specs=[hbm, vmem],
+        input_output_aliases={0: 0},
+        compiler_params=pltpu.CompilerParams(vmem_limit_bytes=12 * 2**20),
+        cost_estimate=pl.CostEstimate(flops=2**16, bytes_accessed=2**22, transcendentals=0),
+        name="together",
+    )(large, small)
 
 
 def listed(codes, total, queue, idle):
@@ -215,9 +245,12 @@
 
 
 def halves_kernel(where_ref, *refs):
-    parts, (out_ref, held, canvas, told, codes, queue, sems) = refs[:8], refs[8:]
-    count, sources = held.shape[1] // S, len(parts)
-    copies = [pltpu.make_async_copy(part, held.at[i], sems.at[i]) for i, part in enumerate(parts)]
+    parts, (out_ref, held, canvas, told, codes, queue, sems) = refs[:2], refs[2:]
+    sources, count = held.shape[0], held.shape[1] // S
+    copies = [
+        pltpu.make_async_copy(part, held.at[pl.ds(i * sources // 2, sources // 2)], sems.at[i])
+        for i, part in enumerate(parts)
+    ]
     for copy in copies:
         copy.start()
     mine, core = where_ref[0], where_ref[1]
@@ -239,7 +272,7 @@
     for i in range(sources):
         words += pltpu.roll(jnp.where(first, code[8 * i : 8 * i + 8, :], 0), i, 1)
     told[...] = words
-    tell = pltpu.make_async_copy(told, codes, sems.at[sources])
+    tell = pltpu.make_async_copy(told, codes, sems.at[len(parts)])
     tell.start()
     tell.wait()
 
@@ -258,20 +291,19 @@
 
 
 def place_halves(where, parts):
-    sources = len(parts)
-    pieces = 2 * sources * (parts[0].shape[0] // S)
+    sources, rows = 2 * parts[0].shape[0], parts[0].shape[1]
     return pl.pallas_call(
         halves_kernel,
         out_shape=jax.ShapeDtypeStruct((P_SIZE // (2 * BAND), 8, 2 * BAND, 2 * LANES), jnp.bfloat16),
-        in_specs=[pl.BlockSpec(memory_space=pltpu.SMEM)] + [pl.BlockSpec(memory_space=pl.ANY)] * sources,
+        in_specs=[pl.BlockSpec(memory_space=pltpu.SMEM)] + [pl.BlockSpec(memory_space=pl.ANY)] * len(parts),
         out_specs=pl.BlockSpec(memory_space=pltpu.VMEM),
         scratch_shapes=[
-            pltpu.VMEM((sources,) + parts[0].shape, jnp.bfloat16),
+            pltpu.VMEM((sources, rows, S), jnp.bfloat16),
             pltpu.VMEM((5, 8 * P_SIZE, LANES), jnp.float32),
             pltpu.VMEM((8, S), jnp.int32),
             pltpu.SMEM((8, S), jnp.int32),
-            pltpu.SMEM((pieces + 2,), jnp.int32),
-            pltpu.SemaphoreType.DMA((sources + 1,)),
+            pltpu.SMEM((2 * sources * (rows // S) + 2,), jnp.int32),
+            pltpu.SemaphoreType.DMA((len(parts) + 1,)),
         ],
         compiler_params=pltpu.CompilerParams(vmem_limit_bytes=40 * 2**20),
         cost_estimate=pl.CostEstimate(flops=2**24, bytes_accessed=24 * 2**20, transcendentals=0),
@@ -282,14 +314,13 @@
 def body(blocks, inv_variance, destinations, offsets, coefficients, basis_rows, basis_cols):
     owners = lax.axis_size("x") * lax.axis_size("z")
     where = jnp.stack([lax.axis_index("x"), lax.axis_index("core")]).astype(jnp.int32)
-    slots, near = match(
-        blocks[0], inv_variance[0], destinations[0], offsets[0], coefficients[0], basis_rows, basis_cols, owners
-    )
-
-    parts = []
-    for lag in range(4):
-        part = lax.ppermute(near, "x", [(i, (i + lag) % 4) for i in range(4)]) if lag else near
-        parts += [part, lax.ppermute(part, "core", [(0, 1), (1, 0)])]
+    weight = inv_variance[0]
+    near = with_lines(weight, destinations[0], offsets[0], lax.axis_size("x"))
+    near = lax.all_to_all(near, "x", 0, 0, tiled=True)
+    slots = match(blocks[0], weight, destinations[0], offsets[0], coefficients[0], basis_rows, basis_cols, owners)
+    slots, near = together(slots, near)
+
+    parts = [near, lax.ppermute(near, "core", [(0, 1), (1, 0)])]
     den = place_halves(where, parts)
     den = lax.psum_scatter(den, "y", scatter_dimension=0, tiled=True)
     den = lax.all_to_all(den.reshape(16, BAND, 2 * LANES), ("z", "core"), 0, 0, tiled=True)

time: 178 us -> 167 us (0.938)
  starting transfers between devices: 72.5 us -> 30.4 us
  blocking collectives: 0 us -> 25.5 us
  waiting for transfers between devices: 64.1 us -> 70.1 us
  Pallas kernels: 16.3 us -> 20.6 us
  local copies, waits for them, and re-layouts: 8.17 us -> 5.09 us
    all_to_all x1, waiting for transfers between devices: 0.01 us -> 42.1 us  [body(): slots = lax.all_to_all(slots, ('x', 'z'), 0, 0, tiled=True)]
    reduce_scatter x1, waiting for transfers between devices: 37.9 us -> 0.01 us  [body(): den = lax.psum_scatter(den, 'y', scatter_dimension=0, tiled=True)]
    ppermute x7 -> x1, starting transfers between devices: 42.3 us -> 9.35 us  [body(): parts = [near, lax.ppermute(near, 'core', [(0, 1), (1, 0)])]]
    all_to_all x0 -> x1, blocking collectives: none -> 25.5 us  [body(): num = lax.all_to_all(num, ('y', 'core'), 0, 0, tiled=True)]
    all_to_all x1, waiting for transfers between devices: 0.01 us -> 16.4 us  [body(): near = lax.all_to_all(near, 'x', 0, 0, tiled=True)]
    ppermute x7 -> x1, waiting for transfers between devices: 14.6 us -> 0.01 us  [body(): parts = [near, lax.ppermute(near, 'core', [(0, 1), (1, 0)])]]
    pallas_call x1 -> x3, Pallas kernels: 4.27 us -> 9.41 us  [the longest x1 3.89 us: match(): pl.pallas_call(match_kernel, out_shape=jax.ShapeDtypeStruct((owners, 2 *...]
    all_to_all x1, starting transfers between devices: 8.97 us -> 4.83 us  [body(): lax.all_to_all(den.reshape(16, BAND, 2 * LANES), ('z', 'core'), 0, 0, til...]
  transfers between devices with their start and end apart: 11 -> 5, of which waited for: 4 -> 3; matrix products, arithmetic and copies ran while one was open for 0% -> 0% of each run, Pallas kernels for 7% -> 9%
where the time goes in v6:
time: 167 us; the launch traced here: 166 us
  waiting for transfers between devices  70.1 us (42%)
  starting transfers between devices  30.4 us (18%)
  blocking collectives  25.5 us (15%)
  Pallas kernels  20.6 us (12%)
  between operations  13.5 us (8%)
  local copies, waits for them, and re-layouts  5.09 us (3%)
    all_to_all x1, waiting for transfers between devices, body(): slots = lax.all_to_all(slots, ('x', 'z'), 0, 0, tiled=True)  42.1 us
    all_to_all x1, blocking collectives, body(): num = lax.all_to_all(num, ('y', 'core'), 0, 0, tiled=True)  25.5 us
    all_to_all x1, waiting for transfers between devices, body(): near = lax.all_to_all(near, 'x', 0, 0, tiled=True)  16.4 us
    all_to_all x1, waiting for transfers between devices, body(): lax.all_to_all(den.reshape(16, BAND, 2 * LANES), ('z', 'core'), 0, 0, til...  11.6 us
    all_to_all x1, starting transfers between devices, body(): slots = lax.all_to_all(slots, ('x', 'z'), 0, 0, tiled=True)  11.2 us
    ppermute x1, starting transfers between devices, body(): parts = [near, lax.ppermute(near, 'core', [(0, 1), (1, 0)])]  9.35 us
    pallas_call x1, Pallas kernels, place_halves(): pl.pallas_call(halves_kernel, out_shape=jax.ShapeDtypeStruct((P_SIZE // (...  8.57 us
    unnamed x25, local copies, waits for them, and re-layouts  5.09 us
  transfers between devices with their start and end apart: 5, of which 3 were waited for; matrix products, arithmetic and copies ran while one was open for 0% of the time, Pallas kernels for 9%

profile of v6, /device:TPU:1, one launch (start us, length us, event | category | flops | bytes accessed | tf_op | source)
XLA Modules:
  0.0 166.1 jit_solution(9990862395343822422)
XLA Ops:
  6.5 1.0 copy-done.2
  7.6 0.7 copy-done.4
  8.3 0.7 copy-done.6
  8.9 2.5 %lines.1 = bf16[4,2064,128]{2,1,0:T(8,128)(2,1)} custom-call(s32[2,16]{1,0:T(2,128)S(1)} %bitcast.28, s32[2,2,16]{2,1,0:T(2,128)S(1)} %bitcast.26, bf16[2048,128]{1,0:T(8,128)(2,1)S(1)} %bitcast.23), custom_call_target="tpu_custom_call" | custom-call | flops 65536 | bytes 4194304 | tf_op jit(solution)/shard_map/lines/pallas_call | solution.py:140
  11.4 0.0 copy-start.9
  11.5 5.0 %all-to-all-start = ((bf16[4,2064,128]{2,1,0:T(8,128)(2,1)}), bf16[4,2064,128]{2,1,0:T(8,128)(2,1)}, u32[]{:S(2)}, u32[]{:S(2)}) async-start(bf16[4,2064,128]{2,1,0:T(8,128)(2,1)} %lines.1), calls=%async_computation | async-start | bytes 4227072 | tf_op jit(solution)/shard_map/all_to_all | solution.py:319
  16.5 3.9 %match.1.large_ref = bf16[32,272,128]{2,1,0:T(8,128)(2,1)S(1)} custom-call(f32[15,16]{1,0:T(8,128)S(1)} %bitcast.25, s32[2,16]{1,0:T(2,128)S(1)} %bitcast.29, s32[2,2,16]{2,1,0:T(2,128)S(1)} %bitcast.27, bf16[5,41]{1,0:T(8,128)(2,1)S(1)} %copy-done.9, bf16[5,41]{1,0:T(8,128)(2,1)S(1)} %copy-done.10, bf16[16,128,128]{2,1,0:T(8,128)(2,1)S(1)} %bitcast.30, ...), custom_call_target="tpu_custom_call" | custom-call | flops 1073741824 | bytes 16777216 | tf_op jit(solution)/shard_map/match/pallas_call | solution.py:94
  20.4 16.4 %all-to-all-done.small_ref = bf16[4,2064,128]{2,1,0:T(8,128)(2,1)} async-done(((bf16[4,2064,128]{2,1,0:T(8,128)(2,1)}), bf16[4,2064,128]{2,1,0:T(8,128)(2,1)}, u32[]{:S(2)}, u32[]{:S(2)}) %all-to-all-start) | async-done | bytes 2113568 | tf_op jit(solution)/shard_map/all_to_all | solution.py:319
  36.8 3.0 %together.1 = (bf16[32,272,128]{2,1,0:T(8,128)(2,1)S(1)}, bf16[4,2064,128]{2,1,0:T(8,128)(2,1)}) custom-call(bf16[32,272,128]{2,1,0:T(8,128)(2,1)S(1)} %match.1.large_ref, bf16[4,2064,128]{2,1,0:T(8,128)(2,1)} %all-to-all-done.small_ref), custom_call_target="tpu_custom_call", output_to_operand_aliasing={{0}: (0, {})} | custom-call | flops 65536 | bytes 4194304 | tf_op jit(solution)/shard_map/together/pallas_call | solution.py:158
  39.8 1.4 copy-done
  41.2 9.3 %collective-permute-start = (bf16[4,2064,128]{2,1,0:T(8,128)(2,1)}, bf16[4,2064,128]{2,1,0:T(8,128)(2,1)}, u32[]{:S(2)}, u32[]{:S(2)}) collective-permute-start(bf16[4,2064,128]{2,1,0:T(8,128)(2,1)} %get-tuple-element.8.refs_0_), channel_id=1, source_target_pairs={{0,32},{32,0},{1,33},{33,1},{2,34},{34,2},{3,35},{35,3},{4,36},{36... | collective-permute-start | bytes 6340616 | tf_op jit(solution)/shard_map/ppermute | solution.py:323
  50.5 11.2 %all-to-all-start.1 = ((bf16[32,272,128]{2,1,0:T(8,128)(2,1)}), bf16[32,272,128]{2,1,0:T(8,128)(2,1)S(1)}, u32[]{:S(2)}, u32[]{:S(2)}) async-start(bf16[32,272,128]{2,1,0:T(8,128)(2,1)} %copy-done), calls=%async_computation.1 | async-start | bytes 4456448 | tf_op jit(solution)/shard_map/all_to_all | solution.py:328
  61.8 0.0 reduce-scatter.2.cloned.1.call-start
  61.8 0.1 pad_add_fusion.where_ref
  61.9 8.6 %place_halves.1 = bf16[8,8,64,256]{3,2,1,0:T(8,128)(2,1)S(1)} custom-call(s32[2]{0:T(128)S(1)} %pad_add_fusion.where_ref, bf16[4,2064,128]{2,1,0:T(8,128)(2,1)} %get-tuple-element.8.refs_0_, bf16[4,2064,128]{2,1,0:T(8,128)(2,1)} %collective-permute-done.refs_1_), custom_call_target="tpu_custom_call" | custom-call | flops 16777216 | bytes 25165824 | tf_op jit(solution)/shard_map/place_halves/pallas_call | solution.py:295
  70.5 1.3 copy-done.1
  71.8 0.0 reduce-scatter.2.cloned.1.call-update
  71.8 42.1 %all-to-all-done.1.slots_ref = bf16[32,272,128]{2,1,0:T(8,128)(2,1)S(1)} async-done(((bf16[32,272,128]{2,1,0:T(8,128)(2,1)}), bf16[32,272,128]{2,1,0:T(8,128)(2,1)S(1)}, u32[]{:S(2)}, u32[]{:S(2)}) %all-to-all-start.1) | async-done | bytes 2228256 | tf_op jit(solution)/shard_map/all_to_all | solution.py:328
  113.9 2.7 %place_whole.1 = bf16[512,512]{1,0:T(8,128)(2,1)S(1)} custom-call(bf16[32,272,128]{2,1,0:T(8,128)(2,1)S(1)} %all-to-all-done.1.slots_ref), custom_call_target="tpu_custom_call" | custom-call | flops 8388608 | bytes 16777216 | tf_op jit(solution)/shard_map/place_whole/pallas_call | solution.py:229
  116.6 25.5 %all_to_all.20 = bf16[16,32,512]{2,1,0:T(8,128)(2,1)S(1)} all-to-all(bf16[16,32,512]{2,1,0:T(8,128)(2,1)S(1)} %bitcast.22), channel_id=1, replica_groups=mesh['y'=8,'core'=2,'x'=4,'z'=8] {'y','core'}, dimensions={0} | all-to-all | bytes 1048576 | tf_op jit(solution)/shard_map/all_to_all | solution.py:330
  142.1 4.8 %all-to-all-start.3 = ((bf16[16,32,256]{2,1,0:T(8,128)(2,1)}), bf16[16,32,256]{2,1,0:T(8,128)(2,1)S(1)}, u32[]{:S(2)}, u32[]{:S(2)}) async-start(bf16[16,32,256]{2,1,0:T(8,128)(2,1)} %bitcast.32), calls=%async_computation.4 | async-start | bytes 524288 | tf_op jit(solution)/shard_map/all_to_all | solution.py:326
  146.9 0.1 convert_reduce_fusion
  147.0 11.6 %all-to-all-done.3 = bf16[16,32,256]{2,1,0:T(8,128)(2,1)S(1)} async-done(((bf16[16,32,256]{2,1,0:T(8,128)(2,1)}), bf16[16,32,256]{2,1,0:T(8,128)(2,1)S(1)}, u32[]{:S(2)}, u32[]{:S(2)}) %all-to-all-start.3) | async-done | bytes 262176 | tf_op jit(solution)/shard_map/all_to_all | solution.py:326
  158.6 0.6 fusion
  (23 shorter events, 0.1 us)
Async XLA Ops:
  6.5 1.0 copy-start.2
  7.6 0.7 copy-start.4
  8.3 0.7 copy-start.6
  11.4 5.0 %copy-start.11 = (f32[1,16,15]{1,0,2:T(1,128)S(1)}, f32[1,16,15]{1,0,2:T(1,128)}, u32[]{:S(2)}) copy-start(f32[1,16,15]{1,0,2:T(1,128)} %param.11) | copy-start | bytes 2884
  11.4 5.0 %copy-start.3 = (bf16[1,16,128,128]{3,2,1,0:T(8,128)(2,1)S(1)}, bf16[1,16,128,128]{3,2,1,0:T(8,128)(2,1)}, u32[]{:S(2)}) copy-start(bf16[1,16,128,128]{3,2,1,0:T(8,128)(2,1)} %param.8) | copy-start | bytes 1572868
  11.4 5.0 %copy-start.5 = (s32[1,16,2,2]{1,3,2,0:T(2,128)S(1)}, s32[1,16,2,2]{1,3,2,0:T(2,128)}, u32[]{:S(2)}) copy-start(s32[1,16,2,2]{1,3,2,0:T(2,128)} %param.10) | copy-start | bytes 772
  11.4 5.1 %copy-start.7 = (s32[1,16,2]{1,2,0:T(2,128)S(1)}, s32[1,16,2]{1,2,0:T(2,128)}, u32[]{:S(2)}) copy-start(s32[1,16,2]{1,2,0:T(2,128)} %param.9) | copy-start | bytes 388
  11.4 5.1 %copy-start.8 = (bf16[1,16,128,128]{3,2,1,0:T(8,128)(2,1)S(1)}, bf16[1,16,128,128]{3,2,1,0:T(8,128)(2,1)}, u32[]{:S(2)}) copy-start(bf16[1,16,128,128]{3,2,1,0:T(8,128)(2,1)} %param.7) | copy-start | bytes 1572868
  11.4 5.1 %copy-start.9 = (bf16[5,41]{1,0:T(8,128)(2,1)S(1)}, bf16[5,41]{1,0:T(8,128)(2,1)}, u32[]{:S(2)}) copy-start(bf16[5,41]{1,0:T(8,128)(2,1)} %rows_ref.1) | copy-start | bytes 1234
  11.5 5.1 %copy-start.10 = (bf16[5,41]{1,0:T(8,128)(2,1)S(1)}, bf16[5,41]{1,0:T(8,128)(2,1)}, u32[]{:S(2)}) copy-start(bf16[5,41]{1,0:T(8,128)(2,1)} %cols_ref.1) | copy-start | bytes 1234
  11.5 25.3 %all-to-all-start = ((bf16[4,2064,128]{2,1,0:T(8,128)(2,1)}), bf16[4,2064,128]{2,1,0:T(8,128)(2,1)}, u32[]{:S(2)}, u32[]{:S(2)}) async-start(bf16[4,2064,128]{2,1,0:T(8,128)(2,1)} %lines.1), calls=%async_computation | async-start | bytes 4227072 | tf_op jit(solution)/shard_map/all_to_all | solution.py:319
  39.8 1.4 copy-start
  41.2 20.7 %collective-permute-start = (bf16[4,2064,128]{2,1,0:T(8,128)(2,1)}, bf16[4,2064,128]{2,1,0:T(8,128)(2,1)}, u32[]{:S(2)}, u32[]{:S(2)}) collective-permute-start(bf16[4,2064,128]{2,1,0:T(8,128)(2,1)} %get-tuple-element.8.refs_0_), channel_id=1, source_target_pairs={{0,32},{32,0},{1,33},{33,1},{2,34},{34,2},{3,35},{35,3},{4,36},{36... | collective-permute-start | bytes 6340616 | tf_op jit(solution)/shard_map/ppermute | solution.py:323
  50.5 63.4 %all-to-all-start.1 = ((bf16[32,272,128]{2,1,0:T(8,128)(2,1)}), bf16[32,272,128]{2,1,0:T(8,128)(2,1)S(1)}, u32[]{:S(2)}, u32[]{:S(2)}) async-start(bf16[32,272,128]{2,1,0:T(8,128)(2,1)} %copy-done), calls=%async_computation.1 | async-start | bytes 4456448 | tf_op jit(solution)/shard_map/all_to_all | solution.py:328
  61.8 80.3 %reduce-scatter.2.cloned.1.call-start = ((), (), s32[]{:S(2)}) async-start(), calls=%async_computation.5 | async-start | bytes 2359296 | tf_op jit(solution)/shard_map/reduce_scatter | solution.py:325
  70.5 1.3 copy-start.1
  142.1 16.5 %all-to-all-start.3 = ((bf16[16,32,256]{2,1,0:T(8,128)(2,1)}), bf16[16,32,256]{2,1,0:T(8,128)(2,1)S(1)}, u32[]{:S(2)}, u32[]{:S(2)}) async-start(bf16[16,32,256]{2,1,0:T(8,128)(2,1)} %bitcast.32), calls=%async_computation.4 | async-start | bytes 524288 | tf_op jit(solution)/shard_map/all_to_all | solution.py:326
Sparse Core Ops, SparseCore 0:
  71.9 40.6 reduce-scatter.1

commit v7 on v6

--- a/solution.py
+++ b/solution.py
@@ -103,7 +103,7 @@
             pltpu.VMEM((GROUP, BASIS * S, 2 * S), jnp.bfloat16),
             pltpu.SMEM((owners,), jnp.int32),
         ],
-        compiler_params=pltpu.CompilerParams(vmem_limit_bytes=32 * 2**20),
+        compiler_params=pltpu.CompilerParams(vmem_limit_bytes=12 * 2**20),
         cost_estimate=pl.CostEstimate(flops=2**30, bytes_accessed=16 * 2**20, transcendentals=0),
         name="match",
     )(
@@ -119,8 +119,7 @@
 
 def lines_kernel(dest_ref, off_ref, weight_ref, near_ref):
     rows = weight_ref.shape[0]
-    for copy in range(near_ref.shape[0]):
-        near_ref[copy, 0:rows, :] = weight_ref[...]
+    near_ref[0:rows, :] = weight_ref[...]
     line = lax.broadcasted_iota(jnp.int32, (META, S), 0)
     lane = lax.broadcasted_iota(jnp.int32, (META, S), 1)
     words = jnp.zeros((META, S), jnp.int32)
@@ -128,18 +127,16 @@
         for n in range(2):
             for at, number in enumerate(places(dest_ref, off_ref, block, n)):
                 words = jnp.where((line == n) & (lane == 8 * block + at), number, words)
-    words = words.astype(jnp.float32).astype(jnp.bfloat16)
-    for copy in range(near_ref.shape[0]):
-        near_ref[copy, rows : rows + META, :] = words
-
-
-def with_lines(weight, destinations, offsets, copies):
+    near_ref[rows : rows + META, :] = words.astype(jnp.float32).astype(jnp.bfloat16)
+
+
+def with_lines(weight, destinations, offsets):
     smem = pl.BlockSpec(memory_space=pltpu.SMEM)
     vmem = pl.BlockSpec(memory_space=pltpu.VMEM)
     rows = weight.shape[0] * S
     return pl.pallas_call(
         lines_kernel,
-        out_shape=jax.ShapeDtypeStruct((copies, rows + META, S), jnp.bfloat16),
+        out_shape=jax.ShapeDtypeStruct((rows + META, S), jnp.bfloat16),
         in_specs=[smem, smem, vmem],
         out_specs=vmem,
         compiler_params=pltpu.CompilerParams(vmem_limit_bytes=8 * 2**20),
@@ -148,23 +145,83 @@
     )(destinations.T, jnp.transpose(offsets, (1, 2, 0)), weight.reshape(rows, S))
 
 
-def together_kernel(large_ref, small_ref, large_out, small_out):
-    small_out[...] = small_ref[...]
-
-
-def together(large, small):
+def held_kernel(large_ref, *refs):
+    pass
+
+
+def held_until(large, *others):
     hbm = pl.BlockSpec(memory_space=pltpu.HBM)
+    return pl.pallas_call(
+        held_kernel,
+        out_shape=jax.ShapeDtypeStruct(large.shape, large.dtype),
+        in_specs=[hbm] + [pl.BlockSpec(memory_space=pl.ANY)] * len(others),
+        out_specs=hbm,
+        input_output_aliases={0: 0},
+        name="held_until",
+    )(large, *others)
+
+
+def turn_kernel(where_ref, den_ref, *out_refs):
+    for lag, out_ref in enumerate(out_refs):
+        out_ref[...] = den_ref[lax.rem(where_ref[2] + lag, len(out_refs))]
+
+
+def turned(where, den):
     vmem = pl.BlockSpec(memory_space=pltpu.VMEM)
     return pl.pallas_call(
-        together_kernel,
-        out_shape=[jax.ShapeDtypeStruct(array.shape, array.dtype) for array in (large, small)],
-        in_specs=[hbm, vmem],
-        out_specs=[hbm, vmem],
-        input_output_aliases={0: 0},
-        compiler_params=pltpu.CompilerParams(vmem_limit_bytes=12 * 2**20),
-        cost_estimate=pl.CostEstimate(flops=2**16, bytes_accessed=2**22, transcendentals=0),
-        name="together",
-    )(large, small)
+        turn_kernel,
+        out_shape=[jax.ShapeDtypeStruct(den.shape[1:], den.dtype)] * den.shape[0],
+        in_specs=[pl.BlockSpec(memory_space=pltpu.SMEM), vmem],
+        out_specs=[vmem] * den.shape[0],
+        cost_estimate=pl.CostEstimate(flops=2**16, bytes_accessed=2**21, transcendentals=0),
+        name="turned",
+    )(where, den)
+
+
+def sum_kernel(where_ref, *refs):
+    blocks, (keep_ref, give_ref) = refs[:-2], refs[-2:]
+    total = blocks[0][...].astype(jnp.float32)
+    for block in blocks[1:]:
+        total += block[...].astype(jnp.float32)
+    even = where_ref[1] == 0
+    keep_ref[...] = jnp.where(even, total[0:BAND], total[BAND : 2 * BAND])
+    give_ref[...] = jnp.where(even, total[BAND : 2 * BAND], total[0:BAND])
+
+
+def summed(where, blocks):
+    vmem = pl.BlockSpec(memory_space=pltpu.VMEM)
+    return pl.pallas_call(
+        sum_kernel,
+        out_shape=[jax.ShapeDtypeStruct((BAND, blocks[0].shape[1]), jnp.float32)] * 2,
+        in_specs=[pl.BlockSpec(memory_space=pltpu.SMEM)] + [vmem] * len(blocks),
+        out_specs=[vmem, vmem],
+        cost_estimate=pl.CostEstimate(flops=2**18, bytes_accessed=2**21, transcendentals=0),
+        name="summed",
+    )(where, *blocks)
+
+
+def divide_kernel(where_ref, num_ref, kept_ref, given_ref, out_ref):
+    num = num_ref[0].astype(jnp.float32)
+    for visit in range(1, num_ref.shape[0]):
+        num += num_ref[visit].astype(jnp.float32)
+    even = where_ref[1] == 0
+    width = kept_ref.shape[1]
+    left = jnp.where(even, kept_ref[...], given_ref[...])
+    right = jnp.where(even, given_ref[...], kept_ref[...])
+    out_ref[0, :, 0:width] = num[:, 0:width] / jnp.maximum(left, 1.0)
+    out_ref[0, :, width : 2 * width] = num[:, width : 2 * width] / jnp.maximum(right, 1.0)
+
+
+def divided(where, num, kept, given):
+    vmem = pl.BlockSpec(memory_space=pltpu.VMEM)
+    return pl.pallas_call(
+        divide_kernel,
+        out_shape=jax.ShapeDtypeStruct((1, BAND, P_SIZE), jnp.float32),
+        in_specs=[pl.BlockSpec(memory_space=pltpu.SMEM), vmem, vmem, vmem],
+        out_specs=vmem,
+        cost_estimate=pl.CostEstimate(flops=2**18, bytes_accessed=2**20, transcendentals=0),
+        name="divided",
+    )(where, num, kept, given)
 
 
 def listed(codes, total, queue, idle):
@@ -238,19 +295,16 @@
             pltpu.SMEM((2 * sources + 2,), jnp.int32),
             pltpu.SemaphoreType.DMA,
         ],
-        compiler_params=pltpu.CompilerParams(vmem_limit_bytes=24 * 2**20),
+        compiler_params=pltpu.CompilerParams(vmem_limit_bytes=8 * 2**20),
         cost_estimate=pl.CostEstimate(flops=2**23, bytes_accessed=16 * 2**20, transcendentals=0),
         name="place_whole",
     )(slots)
 
 
 def halves_kernel(where_ref, *refs):
-    parts, (out_ref, held, canvas, told, codes, queue, sems) = refs[:2], refs[2:]
-    sources, count = held.shape[0], held.shape[1] // S
-    copies = [
-        pltpu.make_async_copy(part, held.at[pl.ds(i * sources // 2, sources // 2)], sems.at[i])
-        for i, part in enumerate(parts)
-    ]
+    parts, (out_ref, held, canvas, told, codes, queue, sems) = refs[:8], refs[8:]
+    count, sources = held.shape[1] // S, len(parts)
+    copies = [pltpu.make_async_copy(part, held.at[i], sems.at[i]) for i, part in enumerate(parts)]
     for copy in copies:
         copy.start()
     mine, core = where_ref[0], where_ref[1]
@@ -272,7 +326,7 @@
     for i in range(sources):
         words += pltpu.roll(jnp.where(first, code[8 * i : 8 * i + 8, :], 0), i, 1)
     told[...] = words
-    tell = pltpu.make_async_copy(told, codes, sems.at[len(parts)])
+    tell = pltpu.make_async_copy(told, codes, sems.at[sources])
     tell.start()
     tell.wait()
 
@@ -291,21 +345,22 @@
 
 
 def place_halves(where, parts):
-    sources, rows = 2 * parts[0].shape[0], parts[0].shape[1]
+    sources = len(parts)
+    pieces = 2 * sources * (parts[0].shape[0] // S)
     return pl.pallas_call(
         halves_kernel,
         out_shape=jax.ShapeDtypeStruct((P_SIZE // (2 * BAND), 8, 2 * BAND, 2 * LANES), jnp.bfloat16),
-        in_specs=[pl.BlockSpec(memory_space=pltpu.SMEM)] + [pl.BlockSpec(memory_space=pl.ANY)] * len(parts),
+        in_specs=[pl.BlockSpec(memory_space=pltpu.SMEM)] + [pl.BlockSpec(memory_space=pl.ANY)] * sources,
         out_specs=pl.BlockSpec(memory_space=pltpu.VMEM),
         scratch_shapes=[
-            pltpu.VMEM((sources, rows, S), jnp.bfloat16),
+            pltpu.VMEM((sources,) + parts[0].shape, jnp.bfloat16),
             pltpu.VMEM((5, 8 * P_SIZE, LANES), jnp.float32),
             pltpu.VMEM((8, S), jnp.int32),
             pltpu.SMEM((8, S), jnp.int32),
-            pltpu.SMEM((2 * sources * (rows // S) + 2,), jnp.int32),
-            pltpu.SemaphoreType.DMA((len(parts) + 1,)),
+            pltpu.SMEM((pieces + 2,), jnp.int32),
+            pltpu.SemaphoreType.DMA((sources + 1,)),
         ],
-        compiler_params=pltpu.CompilerParams(vmem_limit_bytes=40 * 2**20),
+        compiler_params=pltpu.CompilerParams(vmem_limit_bytes=22 * 2**20),
         cost_estimate=pl.CostEstimate(flops=2**24, bytes_accessed=24 * 2**20, transcendentals=0),
         name="place_halves",
     )(where, *parts)
@@ -313,26 +368,28 @@
 
 def body(blocks, inv_variance, destinations, offsets, coefficients, basis_rows, basis_cols):
     owners = lax.axis_size("x") * lax.axis_size("z")
-    where = jnp.stack([lax.axis_index("x"), lax.axis_index("core")]).astype(jnp.int32)
+    where = jnp.stack([lax.axis_index("x"), lax.axis_index("core"), lax.axis_index("z")]).astype(jnp.int32)
     weight = inv_variance[0]
-    near = with_lines(weight, destinations[0], offsets[0], lax.axis_size("x"))
-    near = lax.all_to_all(near, "x", 0, 0, tiled=True)
+    swap = [(0, 1), (1, 0)]
+
+    near = with_lines(weight, destinations[0], offsets[0])
+    along = [lax.ppermute(near, "x", [(i, (i + lag) % 4) for i in range(4)]) for lag in (2, 1, 3)]
+    parts = [near] + along
+    parts = parts + [lax.ppermute(part, "core", swap) for part in parts]
+    den = place_halves(where, parts)
+    den = lax.psum_scatter(den, "y", scatter_dimension=0, tiled=True)[0]
+
     slots = match(blocks[0], weight, destinations[0], offsets[0], coefficients[0], basis_rows, basis_cols, owners)
-    slots, near = together(slots, near)
-
-    parts = [near, lax.ppermute(near, "core", [(0, 1), (1, 0)])]
-    den = place_halves(where, parts)
-    den = lax.psum_scatter(den, "y", scatter_dimension=0, tiled=True)
-    den = lax.all_to_all(den.reshape(16, BAND, 2 * LANES), ("z", "core"), 0, 0, tiled=True)
-
-    slots = lax.all_to_all(slots, ("x", "z"), 0, 0, tiled=True)
+    slots = lax.all_to_all(held_until(slots, *along, parts[4]), ("x", "z"), 0, 0, tiled=True)
     num = place_whole(slots).reshape(16, BAND, P_SIZE)
     num = lax.all_to_all(num, ("y", "core"), 0, 0, tiled=True)
 
-    num = jnp.sum(num.astype(jnp.float32), axis=0)
-    den = jnp.sum(den.reshape(8, 2, BAND, 2 * LANES).astype(jnp.float32), axis=0)
-    den = jnp.concatenate([den[0], den[1]], axis=-1)
-    return (num / jnp.maximum(den, 1.0))[None]
+    steps = list(turned(where, den))
+    steps = steps[:1] + [
+        lax.ppermute(step, "z", [(i, (i + lag) % 8) for i in range(8)]) for lag, step in enumerate(steps) if lag
+    ]
+    kept, given = summed(where, steps)
+    return divided(where, num, kept, lax.ppermute(given, "core", swap))
 
 
 def solution(mesh):

time: 167 us -> 183 us (1.096)
  starting transfers between devices: 30.4 us -> 81.8 us
  blocking collectives: 25.5 us -> 0 us
  waiting for transfers between devices: 70.1 us -> 46 us
  local copies, waits for them, and re-layouts: 5.09 us -> 16.8 us
  Pallas kernels: 20.6 us -> 22.9 us
    ppermute x1 -> x15, starting transfers between devices: 9.35 us -> 64.9 us  [the longest x7 26.1 us: body(): lax.ppermute(step, 'z', [(i, (i + lag) % 8) for i in range(8)])]
    all_to_all x3 -> x2, waiting for transfers between devices: 70.1 us -> 29.3 us  [the longest x1 29.3 us: body(): lax.all_to_all(held_until(slots, *along, parts[4]), ('x', 'z'), 0, 0, til...]
    all_to_all x1 -> x0, blocking collectives: 25.5 us -> none  [body(): num = lax.all_to_all(num, ('y', 'core'), 0, 0, tiled=True)]
    ppermute x1 -> x15, waiting for transfers between devices: 0.01 us -> 16.7 us  [the longest x3 12 us: body(): lax.ppermute(near, 'x', [(i, (i + lag) % 4) for i in range(4)])]
    unnamed x25 -> x63, local copies, waits for them, and re-layouts: 5.09 us -> 16.8 us
    all_to_all x3 -> x2, starting transfers between devices: 21 us -> 16.8 us  [the longest x1 9.52 us: body(): num = lax.all_to_all(num, ('y', 'core'), 0, 0, tiled=True)]
    pallas_call x1, Pallas kernels: 2.65 us -> 5.24 us  [place_whole(): pl.pallas_call(whole_kernel, out_shape=jax.ShapeDtypeStruct((P_SIZE, P_SI...]
    pallas_call x2 -> x5, Pallas kernels: 5.52 us -> 5.9 us  [the longest x1 1.78 us: divided(): pl.pallas_call(divide_kernel, out_shape=jax.ShapeDtypeStruct((1, BAND, P_...]
  transfers between devices with their start and end apart: 5 -> 18, of which waited for: 3 -> 5; matrix products, arithmetic and copies ran while one was open for 0% -> 0% of each run, Pallas kernels for 9% -> 11%
where the time goes in v7:
time: 183 us; the launch traced here: 181 us
  starting transfers between devices  81.8 us (45%)
  waiting for transfers between devices  46 us (25%)
  Pallas kernels  22.9 us (13%)
  local copies, waits for them, and re-layouts  16.8 us (9%)
  between operations  13.8 us (8%)
    all_to_all x1, waiting for transfers between devices, body(): lax.all_to_all(held_until(slots, *along, parts[4]), ('x', 'z'), 0, 0, til...  29.3 us
    ppermute x7, starting transfers between devices, body(): lax.ppermute(step, 'z', [(i, (i + lag) % 8) for i in range(8)])  26.1 us
    unnamed x63, local copies, waits for them, and re-layouts  16.8 us
    ppermute x4, starting transfers between devices, body(): parts = parts + [lax.ppermute(part, 'core', swap) for part in parts]  16.4 us
    ppermute x1, starting transfers between devices, body(): return divided(where, num, kept, lax.ppermute(given, 'core', swap))  15.3 us
    ppermute x3, waiting for transfers between devices, body(): lax.ppermute(near, 'x', [(i, (i + lag) % 4) for i in range(4)])  12 us
    all_to_all x1, starting transfers between devices, body(): num = lax.all_to_all(num, ('y', 'core'), 0, 0, tiled=True)  9.52 us
    pallas_call x1, Pallas kernels, place_halves(): pl.pallas_call(halves_kernel, out_shape=jax.ShapeDtypeStruct((P_SIZE // (...  7.86 us
  transfers between devices with their start and end apart: 18, of which 5 were waited for; matrix products, arithmetic and copies ran while one was open for 0% of the time, Pallas kernels for 11%

profile of v7, /device:TPU:1, one launch (start us, length us, event | category | flops | bytes accessed | tf_op | source)
XLA Modules:
  0.0 181.3 jit_solution(10934647136927267090)
XLA Ops:
  9.8 8.8 %collective-permute-start.3 = (bf16[2064,128]{1,0:T(8,128)(2,1)S(1)}, bf16[2064,128]{1,0:T(8,128)(2,1)S(1)}, u32[]{:S(2)}, u32[]{:S(2)}) collective-permute-start(bf16[2064,128]{1,0:T(8,128)(2,1)S(1)} %lines.1.refs_0_), channel_id=1, source_target_pairs={{0,32},{32,0},{1,33},{33,1},{2,34},{34,2},{3,35},{35,3},{4,36},{36... | collective-permute-start | bytes 1585160 | tf_op jit(solution)/shard_map/ppermute | solution.py:378
  18.6 1.9 %collective-permute-start.2 = (bf16[2064,128]{1,0:T(8,128)(2,1)S(1)}, bf16[2064,128]{1,0:T(8,128)(2,1)S(1)}, u32[]{:S(2)}, u32[]{:S(2)}) collective-permute-start(bf16[2064,128]{1,0:T(8,128)(2,1)S(1)} %lines.1.refs_0_), channel_id=1, source_target_pairs={{0,24},{8,0},{16,8},{24,16},{1,25},{9,1},{17,9},{25,17},{2,26},{10... | collective-permute-start | bytes 1585160 | tf_op jit(solution)/shard_map/ppermute | solution.py:376
  20.6 3.4 %collective-permute-start.1 = (bf16[2064,128]{1,0:T(8,128)(2,1)S(1)}, bf16[2064,128]{1,0:T(8,128)(2,1)S(1)}, u32[]{:S(2)}, u32[]{:S(2)}) collective-permute-start(bf16[2064,128]{1,0:T(8,128)(2,1)S(1)} %lines.1.refs_0_), channel_id=1, source_target_pairs={{0,8},{8,16},{16,24},{24,0},{1,9},{9,17},{17,25},{25,1},{2,10},{10... | collective-permute-start | bytes 1585160 | tf_op jit(solution)/shard_map/ppermute | solution.py:376
  23.9 1.9 %collective-permute-start = (bf16[2064,128]{1,0:T(8,128)(2,1)S(1)}, bf16[2064,128]{1,0:T(8,128)(2,1)S(1)}, u32[]{:S(2)}, u32[]{:S(2)}) collective-permute-start(bf16[2064,128]{1,0:T(8,128)(2,1)S(1)} %lines.1.refs_0_), channel_id=1, source_target_pairs={{0,16},{8,24},{16,0},{24,8},{1,17},{9,25},{17,1},{25,9},{2,18},{10... | collective-permute-start | bytes 1585160 | tf_op jit(solution)/shard_map/ppermute | solution.py:376
  31.4 3.9 %match.1.large_ref = bf16[32,272,128]{2,1,0:T(8,128)(2,1)S(1)} custom-call(f32[15,16]{1,0:T(8,128)S(1)} %bitcast.21, s32[2,16]{1,0:T(2,128)S(1)} %bitcast.25, s32[2,2,16]{2,1,0:T(2,128)S(1)} %bitcast.23, bf16[5,41]{1,0:T(8,128)(2,1)S(1)} %copy-done.20, bf16[5,41]{1,0:T(8,128)(2,1)S(1)} %copy-done.21, bf16[16,128,128]{2,1,0:T(8,128)(2,1)S(1)} %bitcast.26, ...), custom_call_target="tpu_custom_call" | custom-call | flops 1073741824 | bytes 16777216 | tf_op jit(solution)/shard_map/match/pallas_call | solution.py:94
  36.7 12.0 %collective-permute-done.1.refs_1_.refs_2_ = bf16[2064,128]{1,0:T(8,128)(2,1)S(1)} collective-permute-done((bf16[2064,128]{1,0:T(8,128)(2,1)S(1)}, bf16[2064,128]{1,0:T(8,128)(2,1)S(1)}, u32[]{:S(2)}, u32[]{:S(2)}) %collective-permute-start.1) | collective-permute-done | bytes 528416 | tf_op jit(solution)/shard_map/ppermute | solution.py:376
  50.3 7.3 %all-to-all-start = ((bf16[32,272,128]{2,1,0:T(8,128)(2,1)}), bf16[32,272,128]{2,1,0:T(8,128)(2,1)S(1)}, u32[]{:S(2)}, u32[]{:S(2)}) async-start(bf16[32,272,128]{2,1,0:T(8,128)(2,1)} %held_until.1), calls=%async_computation | async-start | bytes 4456448 | tf_op jit(solution)/shard_map/all_to_all | solution.py:383
  57.7 3.3 %collective-permute-start.6 = (bf16[2064,128]{1,0:T(8,128)(2,1)S(1)}, bf16[2064,128]{1,0:T(8,128)(2,1)}, u32[]{:S(2)}, u32[]{:S(2)}) collective-permute-start(bf16[2064,128]{1,0:T(8,128)(2,1)S(1)} %copy-done.5), channel_id=1, source_target_pairs={{0,32},{32,0},{1,33},{33,1},{2,34},{34,2},{3,35},{35,3},{4,36},{36... | collective-permute-start | bytes 1585160 | tf_op jit(solution)/shard_map/ppermute | solution.py:378
  61.0 1.9 %collective-permute-start.5 = (bf16[2064,128]{1,0:T(8,128)(2,1)}, bf16[2064,128]{1,0:T(8,128)(2,1)}, u32[]{:S(2)}, u32[]{:S(2)}) collective-permute-start(bf16[2064,128]{1,0:T(8,128)(2,1)} %copy-done.6), channel_id=1, source_target_pairs={{0,32},{32,0},{1,33},{33,1},{2,34},{34,2},{3,35},{35,3},{4,36},{36... | collective-permute-start | bytes 1585160 | tf_op jit(solution)/shard_map/ppermute | solution.py:378
  62.9 2.4 %collective-permute-start.4 = (bf16[2064,128]{1,0:T(8,128)(2,1)}, bf16[2064,128]{1,0:T(8,128)(2,1)}, u32[]{:S(2)}, u32[]{:S(2)}) collective-permute-start(bf16[2064,128]{1,0:T(8,128)(2,1)} %copy-done.8), channel_id=1, source_target_pairs={{0,32},{32,0},{1,33},{33,1},{2,34},{34,2},{3,35},{35,3},{4,36},{36... | collective-permute-start | bytes 1585160 | tf_op jit(solution)/shard_map/ppermute | solution.py:378
  70.3 7.9 %place_halves.1 = bf16[8,8,64,256]{3,2,1,0:T(8,128)(2,1)S(1)} custom-call(s32[3]{0:T(128)S(1)} %pad_add_fusion.where_ref, bf16[2064,128]{1,0:T(8,128)(2,1)S(1)} %copy-done.11, bf16[2064,128]{1,0:T(8,128)(2,1)S(1)} %copy-done.9, bf16[2064,128]{1,0:T(8,128)(2,1)S(1)} %copy-done.7, bf16[2064,128]{1,0:T(8,128)(2,1)S(1)} %copy-done.5, ...), custom_call_target="tpu_custom_call" | custom-call | flops 16777216 | bytes 25165824 | tf_op jit(solution)/shard_map/place_halves/pallas_call | solution.py:350
  79.6 29.3 %all-to-all-done.slots_ref = bf16[32,272,128]{2,1,0:T(8,128)(2,1)S(1)} async-done(((bf16[32,272,128]{2,1,0:T(8,128)(2,1)}), bf16[32,272,128]{2,1,0:T(8,128)(2,1)S(1)}, u32[]{:S(2)}, u32[]{:S(2)}) %all-to-all-start) | async-done | bytes 2228256 | tf_op jit(solution)/shard_map/all_to_all | solution.py:383
  108.9 5.2 %place_whole.1 = bf16[512,512]{1,0:T(8,128)(2,1)} custom-call(bf16[32,272,128]{2,1,0:T(8,128)(2,1)S(1)} %all-to-all-done.slots_ref), custom_call_target="tpu_custom_call" | custom-call | flops 8388608 | bytes 16777216 | tf_op jit(solution)/shard_map/place_whole/pallas_call | solution.py:286
  114.1 9.5 %all-to-all-start.1 = ((bf16[16,32,512]{2,1,0:T(8,128)(2,1)}), bf16[16,32,512]{2,1,0:T(8,128)(2,1)S(1)}, u32[]{:S(2)}, u32[]{:S(2)}) async-start(bf16[16,32,512]{2,1,0:T(8,128)(2,1)} %bitcast.13), calls=%async_computation.1 | async-start | bytes 1048576 | tf_op jit(solution)/shard_map/all_to_all | solution.py:385
  125.3 1.9 %collective-permute-start.7 = (bf16[64,256]{1,0:T(8,128)(2,1)}, bf16[64,256]{1,0:T(8,128)(2,1)S(1)}, u32[]{:S(2)}, u32[]{:S(2)}) collective-permute-start(bf16[64,256]{1,0:T(8,128)(2,1)} %get-tuple-element.16), channel_id=1, source_target_pairs={{0,1},{1,2},{2,3},{3,4},{4,5},{5,6},{6,7},{7,0},{8,9},{9,10},{10,1... | collective-permute-start | bytes 98312 | tf_op jit(solution)/shard_map/ppermute | solution.py:389
  127.3 5.1 %collective-permute-start.8 = (bf16[64,256]{1,0:T(8,128)(2,1)}, bf16[64,256]{1,0:T(8,128)(2,1)S(1)}, u32[]{:S(2)}, u32[]{:S(2)}) collective-permute-start(bf16[64,256]{1,0:T(8,128)(2,1)} %get-tuple-element.17), channel_id=1, source_target_pairs={{0,2},{1,3},{2,4},{3,5},{4,6},{5,7},{6,0},{7,1},{8,10},{9,11},{10,... | collective-permute-start | bytes 98312 | tf_op jit(solution)/shard_map/ppermute | solution.py:389
  132.3 2.8 %collective-permute-start.9 = (bf16[64,256]{1,0:T(8,128)(2,1)}, bf16[64,256]{1,0:T(8,128)(2,1)S(1)}, u32[]{:S(2)}, u32[]{:S(2)}) collective-permute-start(bf16[64,256]{1,0:T(8,128)(2,1)} %get-tuple-element.18), channel_id=1, source_target_pairs={{0,3},{1,4},{2,5},{3,6},{4,7},{5,0},{6,1},{7,2},{8,11},{9,12},{10,... | collective-permute-start | bytes 98312 | tf_op jit(solution)/shard_map/ppermute | solution.py:389
  135.1 4.2 %collective-permute-start.10 = (bf16[64,256]{1,0:T(8,128)(2,1)}, bf16[64,256]{1,0:T(8,128)(2,1)S(1)}, u32[]{:S(2)}, u32[]{:S(2)}) collective-permute-start(bf16[64,256]{1,0:T(8,128)(2,1)} %get-tuple-element.19), channel_id=1, source_target_pairs={{0,4},{1,5},{2,6},{3,7},{4,0},{5,1},{6,2},{7,3},{8,12},{9,13},{10,... | collective-permute-start | bytes 98312 | tf_op jit(solution)/shard_map/ppermute | solution.py:389
  139.4 4.3 %collective-permute-start.11 = (bf16[64,256]{1,0:T(8,128)(2,1)}, bf16[64,256]{1,0:T(8,128)(2,1)S(1)}, u32[]{:S(2)}, u32[]{:S(2)}) collective-permute-start(bf16[64,256]{1,0:T(8,128)(2,1)} %get-tuple-element.20), channel_id=1, source_target_pairs={{0,5},{1,6},{2,7},{3,0},{4,1},{5,2},{6,3},{7,4},{8,13},{9,14},{10,... | collective-permute-start | bytes 98312 | tf_op jit(solution)/shard_map/ppermute | solution.py:389
  143.7 4.8 %collective-permute-start.12 = (bf16[64,256]{1,0:T(8,128)(2,1)}, bf16[64,256]{1,0:T(8,128)(2,1)S(1)}, u32[]{:S(2)}, u32[]{:S(2)}) collective-permute-start(bf16[64,256]{1,0:T(8,128)(2,1)} %get-tuple-element.21), channel_id=1, source_target_pairs={{0,6},{1,7},{2,0},{3,1},{4,2},{5,3},{6,4},{7,5},{8,14},{9,15},{10,... | collective-permute-start | bytes 98312 | tf_op jit(solution)/shard_map/ppermute | solution.py:389
  148.6 2.9 %collective-permute-start.13 = (bf16[64,256]{1,0:T(8,128)(2,1)}, bf16[64,256]{1,0:T(8,128)(2,1)S(1)}, u32[]{:S(2)}, u32[]{:S(2)}) collective-permute-start(bf16[64,256]{1,0:T(8,128)(2,1)} %get-tuple-element.22), channel_id=1, source_target_pairs={{0,7},{1,0},{2,1},{3,2},{4,3},{5,4},{6,5},{7,6},{8,15},{9,8},{10,9... | collective-permute-start | bytes 98312 | tf_op jit(solution)/shard_map/ppermute | solution.py:389
  151.6 1.9 %collective-permute-done.13.refs_7_ = bf16[64,256]{1,0:T(8,128)(2,1)S(1)} collective-permute-done((bf16[64,256]{1,0:T(8,128)(2,1)}, bf16[64,256]{1,0:T(8,128)(2,1)S(1)}, u32[]{:S(2)}, u32[]{:S(2)}) %collective-permute-start.13) | collective-permute-done | bytes 32800 | tf_op jit(solution)/shard_map/ppermute | solution.py:389
  155.6 15.3 %collective-permute-start.14 = (f32[32,256]{1,0:T(8,128)}, f32[32,256]{1,0:T(8,128)S(1)}, u32[]{:S(2)}, u32[]{:S(2)}) collective-permute-start(f32[32,256]{1,0:T(8,128)} %get-tuple-element.24), channel_id=1, source_target_pairs={{0,32},{32,0},{1,33},{33,1},{2,34},{34,2},{3,35},{35,3},{4,36},{36... | collective-permute-start | bytes 98312 | tf_op jit(solution)/shard_map/ppermute | solution.py:392
  172.7 1.8 divided.1
  (85 shorter events, 23.9 us)
Async XLA Ops:
  9.8 38.8 %copy-start.10 = (bf16[2064,128]{1,0:T(8,128)(2,1)}, bf16[2064,128]{1,0:T(8,128)(2,1)S(1)}, u32[]{:S(2)}) copy-start(bf16[2064,128]{1,0:T(8,128)(2,1)S(1)} %lines.1.refs_0_) | copy-start | bytes 1585156
  9.8 26.8 %collective-permute-start.3 = (bf16[2064,128]{1,0:T(8,128)(2,1)S(1)}, bf16[2064,128]{1,0:T(8,128)(2,1)S(1)}, u32[]{:S(2)}, u32[]{:S(2)}) collective-permute-start(bf16[2064,128]{1,0:T(8,128)(2,1)S(1)} %lines.1.refs_0_), channel_id=1, source_target_pairs={{0,32},{32,0},{1,33},{33,1},{2,34},{34,2},{3,35},{35,3},{4,36},{36... | collective-permute-start | bytes 1585160 | tf_op jit(solution)/shard_map/ppermute | solution.py:378
  18.6 18.0 %collective-permute-start.2 = (bf16[2064,128]{1,0:T(8,128)(2,1)S(1)}, bf16[2064,128]{1,0:T(8,128)(2,1)S(1)}, u32[]{:S(2)}, u32[]{:S(2)}) collective-permute-start(bf16[2064,128]{1,0:T(8,128)(2,1)S(1)} %lines.1.refs_0_), channel_id=1, source_target_pairs={{0,24},{8,0},{16,8},{24,16},{1,25},{9,1},{17,9},{25,17},{2,26},{10... | collective-permute-start | bytes 1585160 | tf_op jit(solution)/shard_map/ppermute | solution.py:376
  20.6 28.1 %collective-permute-start.1 = (bf16[2064,128]{1,0:T(8,128)(2,1)S(1)}, bf16[2064,128]{1,0:T(8,128)(2,1)S(1)}, u32[]{:S(2)}, u32[]{:S(2)}) collective-permute-start(bf16[2064,128]{1,0:T(8,128)(2,1)S(1)} %lines.1.refs_0_), channel_id=1, source_target_pairs={{0,8},{8,16},{16,24},{24,0},{1,9},{9,17},{17,25},{25,1},{2,10},{10... | collective-permute-start | bytes 1585160 | tf_op jit(solution)/shard_map/ppermute | solution.py:376
  23.9 24.7 %collective-permute-start = (bf16[2064,128]{1,0:T(8,128)(2,1)S(1)}, bf16[2064,128]{1,0:T(8,128)(2,1)S(1)}, u32[]{:S(2)}, u32[]{:S(2)}) collective-permute-start(bf16[2064,128]{1,0:T(8,128)(2,1)S(1)} %lines.1.refs_0_), channel_id=1, source_target_pairs={{0,16},{8,24},{16,0},{24,8},{1,17},{9,25},{17,1},{25,9},{2,18},{10... | collective-permute-start | bytes 1585160 | tf_op jit(solution)/shard_map/ppermute | solution.py:376
  36.7 12.0 %copy-start.2 = (bf16[2064,128]{1,0:T(8,128)(2,1)}, bf16[2064,128]{1,0:T(8,128)(2,1)S(1)}, u32[]{:S(2)}) copy-start(bf16[2064,128]{1,0:T(8,128)(2,1)S(1)} %collective-permute-done.3.refs_3_.refs_4_) | copy-start | bytes 1585156
  36.7 12.0 %copy-start.4 = (bf16[2064,128]{1,0:T(8,128)(2,1)}, bf16[2064,128]{1,0:T(8,128)(2,1)S(1)}, u32[]{:S(2)}) copy-start(bf16[2064,128]{1,0:T(8,128)(2,1)S(1)} %collective-permute-done.2.refs_2_.refs_3_) | copy-start | bytes 1585156
  50.3 16.9 %copy-start.3 = (bf16[2064,128]{1,0:T(8,128)(2,1)S(1)}, bf16[2064,128]{1,0:T(8,128)(2,1)}, u32[]{:S(2)}) copy-start(bf16[2064,128]{1,0:T(8,128)(2,1)} %copy-done.2) | copy-start | bytes 1585156
  50.3 58.6 %all-to-all-start = ((bf16[32,272,128]{2,1,0:T(8,128)(2,1)}), bf16[32,272,128]{2,1,0:T(8,128)(2,1)S(1)}, u32[]{:S(2)}, u32[]{:S(2)}) async-start(bf16[32,272,128]{2,1,0:T(8,128)(2,1)} %held_until.1), calls=%async_computation | async-start | bytes 4456448 | tf_op jit(solution)/shard_map/all_to_all | solution.py:383
  57.6 66.1 %reduce-scatter.2.cloned.1.call-start = ((), (), s32[]{:S(2)}) async-start(), calls=%async_computation.3 | async-start | bytes 2359296 | tf_op jit(solution)/shard_map/reduce_scatter | solution.py:380
  57.7 7.7 %collective-permute-start.6 = (bf16[2064,128]{1,0:T(8,128)(2,1)S(1)}, bf16[2064,128]{1,0:T(8,128)(2,1)}, u32[]{:S(2)}, u32[]{:S(2)}) collective-permute-start(bf16[2064,128]{1,0:T(8,128)(2,1)S(1)} %copy-done.5), channel_id=1, source_target_pairs={{0,32},{32,0},{1,33},{33,1},{2,34},{34,2},{3,35},{35,3},{4,36},{36... | collective-permute-start | bytes 1585160 | tf_op jit(solution)/shard_map/ppermute | solution.py:378
  61.0 4.4 %collective-permute-start.5 = (bf16[2064,128]{1,0:T(8,128)(2,1)}, bf16[2064,128]{1,0:T(8,128)(2,1)}, u32[]{:S(2)}, u32[]{:S(2)}) collective-permute-start(bf16[2064,128]{1,0:T(8,128)(2,1)} %copy-done.6), channel_id=1, source_target_pairs={{0,32},{32,0},{1,33},{33,1},{2,34},{34,2},{3,35},{35,3},{4,36},{36... | collective-permute-start | bytes 1585160 | tf_op jit(solution)/shard_map/ppermute | solution.py:378
  62.9 4.3 %collective-permute-start.4 = (bf16[2064,128]{1,0:T(8,128)(2,1)}, bf16[2064,128]{1,0:T(8,128)(2,1)}, u32[]{:S(2)}, u32[]{:S(2)}) collective-permute-start(bf16[2064,128]{1,0:T(8,128)(2,1)} %copy-done.8), channel_id=1, source_target_pairs={{0,32},{32,0},{1,33},{33,1},{2,34},{34,2},{3,35},{35,3},{4,36},{36... | collective-permute-start | bytes 1585160 | tf_op jit(solution)/shard_map/ppermute | solution.py:378
  65.4 12.8 %copy-start.14 = (s32[3]{0:T(128)}, s32[3]{0:T(128)S(1)}, u32[]{:S(2)}) copy-start(s32[3]{0:T(128)S(1)} %pad_add_fusion.where_ref) | copy-start | bytes 40
  114.1 57.8 %all-to-all-start.1 = ((bf16[16,32,512]{2,1,0:T(8,128)(2,1)}), bf16[16,32,512]{2,1,0:T(8,128)(2,1)S(1)}, u32[]{:S(2)}, u32[]{:S(2)}) async-start(bf16[16,32,512]{2,1,0:T(8,128)(2,1)} %bitcast.13), calls=%async_computation.1 | async-start | bytes 1048576 | tf_op jit(solution)/shard_map/all_to_all | solution.py:385
  125.3 18.3 %collective-permute-start.7 = (bf16[64,256]{1,0:T(8,128)(2,1)}, bf16[64,256]{1,0:T(8,128)(2,1)S(1)}, u32[]{:S(2)}, u32[]{:S(2)}) collective-permute-start(bf16[64,256]{1,0:T(8,128)(2,1)} %get-tuple-element.16), channel_id=1, source_target_pairs={{0,1},{1,2},{2,3},{3,4},{4,5},{5,6},{6,7},{7,0},{8,9},{9,10},{10,1... | collective-permute-start | bytes 98312 | tf_op jit(solution)/shard_map/ppermute | solution.py:389
  127.3 21.3 %collective-permute-start.8 = (bf16[64,256]{1,0:T(8,128)(2,1)}, bf16[64,256]{1,0:T(8,128)(2,1)S(1)}, u32[]{:S(2)}, u32[]{:S(2)}) collective-permute-start(bf16[64,256]{1,0:T(8,128)(2,1)} %get-tuple-element.17), channel_id=1, source_target_pairs={{0,2},{1,3},{2,4},{3,5},{4,6},{5,7},{6,0},{7,1},{8,10},{9,11},{10,... | collective-permute-start | bytes 98312 | tf_op jit(solution)/shard_map/ppermute | solution.py:389
  132.3 19.2 %collective-permute-start.9 = (bf16[64,256]{1,0:T(8,128)(2,1)}, bf16[64,256]{1,0:T(8,128)(2,1)S(1)}, u32[]{:S(2)}, u32[]{:S(2)}) collective-permute-start(bf16[64,256]{1,0:T(8,128)(2,1)} %get-tuple-element.18), channel_id=1, source_target_pairs={{0,3},{1,4},{2,5},{3,6},{4,7},{5,0},{6,1},{7,2},{8,11},{9,12},{10,... | collective-permute-start | bytes 98312 | tf_op jit(solution)/shard_map/ppermute | solution.py:389
  135.1 16.4 %collective-permute-start.10 = (bf16[64,256]{1,0:T(8,128)(2,1)}, bf16[64,256]{1,0:T(8,128)(2,1)S(1)}, u32[]{:S(2)}, u32[]{:S(2)}) collective-permute-start(bf16[64,256]{1,0:T(8,128)(2,1)} %get-tuple-element.19), channel_id=1, source_target_pairs={{0,4},{1,5},{2,6},{3,7},{4,0},{5,1},{6,2},{7,3},{8,12},{9,13},{10,... | collective-permute-start | bytes 98312 | tf_op jit(solution)/shard_map/ppermute | solution.py:389
  139.4 12.1 %collective-permute-start.11 = (bf16[64,256]{1,0:T(8,128)(2,1)}, bf16[64,256]{1,0:T(8,128)(2,1)S(1)}, u32[]{:S(2)}, u32[]{:S(2)}) collective-permute-start(bf16[64,256]{1,0:T(8,128)(2,1)} %get-tuple-element.20), channel_id=1, source_target_pairs={{0,5},{1,6},{2,7},{3,0},{4,1},{5,2},{6,3},{7,4},{8,13},{9,14},{10,... | collective-permute-start | bytes 98312 | tf_op jit(solution)/shard_map/ppermute | solution.py:389
  143.7 9.7 %copy-start.24 = (bf16[64,256]{1,0:T(8,128)(2,1)}, bf16[64,256]{1,0:T(8,128)(2,1)S(1)}, u32[]{:S(2)}) copy-start(bf16[64,256]{1,0:T(8,128)(2,1)S(1)} %collective-permute-done.7.refs_1_) | copy-start | bytes 98308
  143.7 7.9 %collective-permute-start.12 = (bf16[64,256]{1,0:T(8,128)(2,1)}, bf16[64,256]{1,0:T(8,128)(2,1)S(1)}, u32[]{:S(2)}, u32[]{:S(2)}) collective-permute-start(bf16[64,256]{1,0:T(8,128)(2,1)} %get-tuple-element.21), channel_id=1, source_target_pairs={{0,6},{1,7},{2,0},{3,1},{4,2},{5,3},{6,4},{7,5},{8,14},{9,15},{10,... | collective-permute-start | bytes 98312 | tf_op jit(solution)/shard_map/ppermute | solution.py:389
  148.6 4.9 %collective-permute-start.13 = (bf16[64,256]{1,0:T(8,128)(2,1)}, bf16[64,256]{1,0:T(8,128)(2,1)S(1)}, u32[]{:S(2)}, u32[]{:S(2)}) collective-permute-start(bf16[64,256]{1,0:T(8,128)(2,1)} %get-tuple-element.22), channel_id=1, source_target_pairs={{0,7},{1,0},{2,1},{3,2},{4,3},{5,4},{6,5},{7,6},{8,15},{9,8},{10,9... | collective-permute-start | bytes 98312 | tf_op jit(solution)/shard_map/ppermute | solution.py:389
  155.6 16.3 %collective-permute-start.14 = (f32[32,256]{1,0:T(8,128)}, f32[32,256]{1,0:T(8,128)S(1)}, u32[]{:S(2)}, u32[]{:S(2)}) collective-permute-start(f32[32,256]{1,0:T(8,128)} %get-tuple-element.24), channel_id=1, source_target_pairs={{0,32},{32,0},{1,33},{33,1},{2,34},{34,2},{3,35},{35,3},{4,36},{36... | collective-permute-start | bytes 98312 | tf_op jit(solution)/shard_map/ppermute | solution.py:392
  (25 other events, 36.7 us)
Sparse Core Ops, SparseCore 0:
  79.7 41.2 reduce-scatter.1

commit v8 on v6

--- a/solution.py
+++ b/solution.py
@@ -103,7 +103,7 @@
             pltpu.VMEM((GROUP, BASIS * S, 2 * S), jnp.bfloat16),
             pltpu.SMEM((owners,), jnp.int32),
         ],
-        compiler_params=pltpu.CompilerParams(vmem_limit_bytes=32 * 2**20),
+        compiler_params=pltpu.CompilerParams(vmem_limit_bytes=60 * 2**20),
         cost_estimate=pl.CostEstimate(flops=2**30, bytes_accessed=16 * 2**20, transcendentals=0),
         name="match",
     )(
@@ -119,8 +119,7 @@
 
 def lines_kernel(dest_ref, off_ref, weight_ref, near_ref):
     rows = weight_ref.shape[0]
-    for copy in range(near_ref.shape[0]):
-        near_ref[copy, 0:rows, :] = weight_ref[...]
+    near_ref[0:rows, :] = weight_ref[...]
     line = lax.broadcasted_iota(jnp.int32, (META, S), 0)
     lane = lax.broadcasted_iota(jnp.int32, (META, S), 1)
     words = jnp.zeros((META, S), jnp.int32)
@@ -128,43 +127,22 @@
         for n in range(2):
             for at, number in enumerate(places(dest_ref, off_ref, block, n)):
                 words = jnp.where((line == n) & (lane == 8 * block + at), number, words)
-    words = words.astype(jnp.float32).astype(jnp.bfloat16)
-    for copy in range(near_ref.shape[0]):
-        near_ref[copy, rows : rows + META, :] = words
-
-
-def with_lines(weight, destinations, offsets, copies):
+    near_ref[rows : rows + META, :] = words.astype(jnp.float32).astype(jnp.bfloat16)
+
+
+def with_lines(weight, destinations, offsets):
     smem = pl.BlockSpec(memory_space=pltpu.SMEM)
     vmem = pl.BlockSpec(memory_space=pltpu.VMEM)
     rows = weight.shape[0] * S
     return pl.pallas_call(
         lines_kernel,
-        out_shape=jax.ShapeDtypeStruct((copies, rows + META, S), jnp.bfloat16),
+        out_shape=jax.ShapeDtypeStruct((rows + META, S), jnp.bfloat16),
         in_specs=[smem, smem, vmem],
         out_specs=vmem,
-        compiler_params=pltpu.CompilerParams(vmem_limit_bytes=8 * 2**20),
+        compiler_params=pltpu.CompilerParams(vmem_limit_bytes=60 * 2**20),
         cost_estimate=pl.CostEstimate(flops=2**16, bytes_accessed=2**22, transcendentals=0),
         name="lines",
     )(destinations.T, jnp.transpose(offsets, (1, 2, 0)), weight.reshape(rows, S))
-
-
-def together_kernel(large_ref, small_ref, large_out, small_out):
-    small_out[...] = small_ref[...]
-
-
-def together(large, small):
-    hbm = pl.BlockSpec(memory_space=pltpu.HBM)
-    vmem = pl.BlockSpec(memory_space=pltpu.VMEM)
-    return pl.pallas_call(
-        together_kernel,
-        out_shape=[jax.ShapeDtypeStruct(array.shape, array.dtype) for array in (large, small)],
-        in_specs=[hbm, vmem],
-        out_specs=[hbm, vmem],
-        input_output_aliases={0: 0},
-        compiler_params=pltpu.CompilerParams(vmem_limit_bytes=12 * 2**20),
-        cost_estimate=pl.CostEstimate(flops=2**16, bytes_accessed=2**22, transcendentals=0),
-        name="together",
-    )(large, small)
 
 
 def listed(codes, total, queue, idle):
@@ -238,26 +216,21 @@
             pltpu.SMEM((2 * sources + 2,), jnp.int32),
             pltpu.SemaphoreType.DMA,
         ],
-        compiler_params=pltpu.CompilerParams(vmem_limit_bytes=24 * 2**20),
+        compiler_params=pltpu.CompilerParams(vmem_limit_bytes=8 * 2**20),
         cost_estimate=pl.CostEstimate(flops=2**23, bytes_accessed=16 * 2**20, transcendentals=0),
         name="place_whole",
     )(slots)
 
 
-def halves_kernel(where_ref, *refs):
-    parts, (out_ref, held, canvas, told, codes, queue, sems) = refs[:2], refs[2:]
+def halves_kernel(where_ref, parts_ref, out_ref, held, canvas, packed, told, codes, queue, sems):
     sources, count = held.shape[0], held.shape[1] // S
-    copies = [
-        pltpu.make_async_copy(part, held.at[pl.ds(i * sources // 2, sources // 2)], sems.at[i])
-        for i, part in enumerate(parts)
-    ]
-    for copy in copies:
-        copy.start()
+    patches = out_ref.shape[0]
+    fetch = pltpu.make_async_copy(parts_ref, held, sems.at[patches])
+    fetch.start()
     mine, core = where_ref[0], where_ref[1]
     for tile in (1, 2):
-        canvas[tile] = jnp.zeros((8 * P_SIZE, LANES), jnp.float32)
-    for copy in copies:
-        copy.wait()
+        canvas[tile] = jnp.zeros((patches * P_SIZE, LANES), jnp.float32)
+    fetch.wait()
     notes = held[:, count * S : count * S + META, :].astype(jnp.float32).astype(jnp.int32)[:, 0:8, :]
     notes = notes.reshape(sources * 8, S)
     at = [notes] + [pltpu.roll(notes, S - i, 1) for i in range(1, 5)]
@@ -272,59 +245,59 @@
     for i in range(sources):
         words += pltpu.roll(jnp.where(first, code[8 * i : 8 * i + 8, :], 0), i, 1)
     told[...] = words
-    tell = pltpu.make_async_copy(told, codes, sems.at[len(parts)])
+    tell = pltpu.make_async_copy(told, codes, sems.at[patches + 1])
     tell.start()
     tell.wait()
-
     found = listed(lambda i: codes[i // S, lax.rem(i, S)], 2 * sources * count, queue, 3 << 14)
 
     def block(i):
         return held[lax.div(i, count), pl.ds(pl.multiple_of(lax.rem(i, count) * S, S), S), :]
 
     add_pieces(queue, found, block, canvas)
-    for band in range(out_ref.shape[0]):
-        for patch in range(8):
-            start = patch * P_SIZE + band * 2 * BAND
-            for half in range(2):
-                rows = canvas[half + 1, start : start + 2 * BAND, :]
-                out_ref[band, patch, :, half * LANES : (half + 1) * LANES] = rows.astype(jnp.bfloat16)
+    copies = []
+    for patch in range(patches):
+        for half in range(2):
+            rows = canvas[half + 1, patch * P_SIZE : (patch + 1) * P_SIZE, :]
+            packed[patch, :, half * LANES : (half + 1) * LANES] = rows.astype(jnp.bfloat16)
+        copies.append(pltpu.make_async_copy(packed.at[patch], out_ref.at[patch], sems.at[patch]))
+        copies[-1].start()
+    for copy in copies:
+        copy.wait()
 
 
 def place_halves(where, parts):
-    sources, rows = 2 * parts[0].shape[0], parts[0].shape[1]
+    sources, rows, patches = parts.shape[0], parts.shape[1], 8
+    hbm = pl.BlockSpec(memory_space=pltpu.HBM)
     return pl.pallas_call(
         halves_kernel,
-        out_shape=jax.ShapeDtypeStruct((P_SIZE // (2 * BAND), 8, 2 * BAND, 2 * LANES), jnp.bfloat16),
-        in_specs=[pl.BlockSpec(memory_space=pltpu.SMEM)] + [pl.BlockSpec(memory_space=pl.ANY)] * len(parts),
-        out_specs=pl.BlockSpec(memory_space=pltpu.VMEM),
+        out_shape=jax.ShapeDtypeStruct((patches, P_SIZE, 2 * LANES), jnp.bfloat16),
+        in_specs=[pl.BlockSpec(memory_space=pltpu.SMEM), hbm],
+        out_specs=hbm,
         scratch_shapes=[
             pltpu.VMEM((sources, rows, S), jnp.bfloat16),
-            pltpu.VMEM((5, 8 * P_SIZE, LANES), jnp.float32),
+            pltpu.VMEM((5, patches * P_SIZE, LANES), jnp.float32),
+            pltpu.VMEM((patches, P_SIZE, 2 * LANES), jnp.bfloat16),
             pltpu.VMEM((8, S), jnp.int32),
             pltpu.SMEM((8, S), jnp.int32),
             pltpu.SMEM((2 * sources * (rows // S) + 2,), jnp.int32),
-            pltpu.SemaphoreType.DMA((len(parts) + 1,)),
+            pltpu.SemaphoreType.DMA((patches + 2,)),
         ],
-        compiler_params=pltpu.CompilerParams(vmem_limit_bytes=40 * 2**20),
+        compiler_params=pltpu.CompilerParams(vmem_limit_bytes=60 * 2**20),
         cost_estimate=pl.CostEstimate(flops=2**24, bytes_accessed=24 * 2**20, transcendentals=0),
         name="place_halves",
-    )(where, *parts)
+    )(where, parts)
 
 
 def body(blocks, inv_variance, destinations, offsets, coefficients, basis_rows, basis_cols):
     owners = lax.axis_size("x") * lax.axis_size("z")
     where = jnp.stack([lax.axis_index("x"), lax.axis_index("core")]).astype(jnp.int32)
     weight = inv_variance[0]
-    near = with_lines(weight, destinations[0], offsets[0], lax.axis_size("x"))
-    near = lax.all_to_all(near, "x", 0, 0, tiled=True)
+
+    near = lax.all_gather(with_lines(weight, destinations[0], offsets[0]), ("core", "x"))
+    den = lax.psum_scatter(place_halves(where, near), "z", scatter_dimension=0, tiled=True)
+    den = lax.all_to_all(den.reshape(16, BAND, 2 * LANES), ("y", "core"), 0, 0, tiled=True)
+
     slots = match(blocks[0], weight, destinations[0], offsets[0], coefficients[0], basis_rows, basis_cols, owners)
-    slots, near = together(slots, near)
-
-    parts = [near, lax.ppermute(near, "core", [(0, 1), (1, 0)])]
-    den = place_halves(where, parts)
-    den = lax.psum_scatter(den, "y", scatter_dimension=0, tiled=True)
-    den = lax.all_to_all(den.reshape(16, BAND, 2 * LANES), ("z", "core"), 0, 0, tiled=True)
-
     slots = lax.all_to_all(slots, ("x", "z"), 0, 0, tiled=True)
     num = place_whole(slots).reshape(16, BAND, P_SIZE)
     num = lax.all_to_all(num, ("y", "core"), 0, 0, tiled=True)

time: 167 us -> 154 us (0.922)
  waiting for transfers between devices: 70.1 us -> 64.5 us
  starting transfers between devices: 30.4 us -> 25.8 us
  local copies, waits for them, and re-layouts: 5.09 us -> 1.3 us
    all_to_all x1, waiting for transfers between devices: 42.1 us -> 1.4 us  [body(): slots = lax.all_to_all(slots, ('x', 'z'), 0, 0, tiled=True)]
    all_gather x0 -> x1, waiting for transfers between devices: none -> 39.8 us  [body(): lax.all_gather(with_lines(weight, destinations[0], offsets[0]), ('core',...]
    all_to_all x2 -> x1, waiting for transfers between devices: 28 us -> 11.6 us  [body(): lax.all_to_all(den.reshape(16, BAND, 2 * LANES), ('y', 'core'), 0, 0, til...]
    reduce_scatter x1, waiting for transfers between devices: 0.01 us -> 11.7 us  [body(): lax.psum_scatter(place_halves(where, near), 'z', scatter_dimension=0, til...]
    ppermute x1 -> x0, starting transfers between devices: 9.35 us -> none  [body(): parts = [near, lax.ppermute(near, 'core', [(0, 1), (1, 0)])]]
    unnamed x25 -> x1, local copies, waits for them, and re-layouts: 5.09 us -> 1.3 us
    all_to_all x1, starting transfers between devices: 11.2 us -> 13.7 us  [body(): slots = lax.all_to_all(slots, ('x', 'z'), 0, 0, tiled=True)]
    pallas_call x3 -> x2, Pallas kernels: 14.1 us -> 11.7 us  [the longest x1 9.52 us: place_halves(): pl.pallas_call(halves_kernel, out_shape=jax.ShapeDtypeStruct((patches, P_...]
  transfers between devices with their start and end apart: 5 -> 4, of which waited for: 3 -> 4; matrix products, arithmetic and copies ran while one was open for 0% -> 1% of each run, Pallas kernels for 9% -> 12%
where the time goes in v8:
time: 154 us; the launch traced here: 153 us
  waiting for transfers between devices  64.5 us (42%)
  blocking collectives  26.5 us (17%)
  starting transfers between devices  25.8 us (17%)
  Pallas kernels  20.1 us (13%)
  between operations  13.4 us (9%)
    all_gather x1, waiting for transfers between devices, body(): lax.all_gather(with_lines(weight, destinations[0], offsets[0]), ('core',...  39.8 us
    all_to_all x1, blocking collectives, body(): num = lax.all_to_all(num, ('y', 'core'), 0, 0, tiled=True)  26.5 us
    all_to_all x1, starting transfers between devices, body(): slots = lax.all_to_all(slots, ('x', 'z'), 0, 0, tiled=True)  13.7 us
    all_to_all x1, starting transfers between devices, body(): lax.all_to_all(den.reshape(16, BAND, 2 * LANES), ('y', 'core'), 0, 0, til...  12 us
    reduce_scatter x1, waiting for transfers between devices, body(): lax.psum_scatter(place_halves(where, near), 'z', scatter_dimension=0, til...  11.7 us
    all_to_all x1, waiting for transfers between devices, body(): lax.all_to_all(den.reshape(16, BAND, 2 * LANES), ('y', 'core'), 0, 0, til...  11.6 us
    pallas_call x1, Pallas kernels, place_halves(): pl.pallas_call(halves_kernel, out_shape=jax.ShapeDtypeStruct((patches, P_...  9.52 us
    pallas_call x1, Pallas kernels, match(): pl.pallas_call(match_kernel, out_shape=jax.ShapeDtypeStruct((owners, 2 *...  5.77 us
  transfers between devices with their start and end apart: 4, of which 4 were waited for; matrix products, arithmetic and copies ran while one was open for 1% of the time, Pallas kernels for 12%

profile of v8, /device:TPU:1, one launch (start us, length us, event | category | flops | bytes accessed | tf_op | source)
XLA Modules:
  0.0 153.1 jit_solution(10015181034909260336)
XLA Ops:
  6.5 0.0 all-gather.3.cloned.1.call-start
  6.5 2.2 %lines.1 = bf16[2064,128]{1,0:T(8,128)(2,1)} custom-call(s32[2,16]{1,0:T(2,128)} %bitcast.32, s32[2,2,16]{2,1,0:T(2,128)} %bitcast.30, bf16[2048,128]{1,0:T(8,128)(2,1)} %bitcast.26), custom_call_target="tpu_custom_call" | custom-call | flops 65536 | bytes 4194304 | tf_op jit(solution)/shard_map/lines/pallas_call | solution.py:137
  8.7 0.0 all-gather.3.cloned.1.call-update
  8.7 1.3 copy.10
  10.0 5.8 %match.1 = bf16[32,272,128]{2,1,0:T(8,128)(2,1)} custom-call(f32[15,16]{1,0:T(8,128)} %bitcast.29, s32[2,16]{1,0:T(2,128)} %bitcast.33, s32[2,2,16]{2,1,0:T(2,128)} %bitcast.31, bf16[5,41]{1,0:T(8,128)(2,1)} %rows_ref.1, bf16[5,41]{1,0:T(8,128)(2,1)} %cols_ref.1, bf16[16,128,128]{2,1,0:T(8,128)(2,1)} %bitcast.34, bf16[16,128,128]{2,1,0:T(8,128)(2,1)} %bitcast.27), custom_call_target="tpu_custom_call" | custom-call | flops 1073741824 | bytes 16777216 | tf_op jit(solution)/shard_map/match/pallas_call | solution.py:94
  15.8 13.7 %all-to-all-start = ((bf16[32,272,128]{2,1,0:T(8,128)(2,1)}), bf16[32,272,128]{2,1,0:T(8,128)(2,1)S(1)}, u32[]{:S(2)}, u32[]{:S(2)}) async-start(bf16[32,272,128]{2,1,0:T(8,128)(2,1)} %match.1), calls=%async_computation | async-start | bytes 4456448 | tf_op jit(solution)/shard_map/all_to_all | solution.py:301
  29.5 0.0 reduce-scatter.2.cloned.1.call-start
  29.6 0.7 pad_add_fusion.where_ref
  30.2 39.8 %all-gather.3.cloned.1.call-done = bf16[16512,128]{1,0:T(8,128)(2,1)} async-done(((bf16[2064,128]{1,0:T(8,128)(2,1)}), bf16[16512,128]{1,0:T(8,128)(2,1)}) %all-gather.3.cloned.1.call-update) | async-done | bytes 4227088 | tf_op jit(solution)/shard_map/all_gather | solution.py:296
  70.0 9.5 %place_halves.1 = bf16[8,512,256]{2,1,0:T(8,128)(2,1)} custom-call(s32[2]{0:T(128)} %pad_add_fusion.where_ref, bf16[8,2064,128]{2,1,0:T(8,128)(2,1)} %bitcast.24), custom_call_target="tpu_custom_call" | custom-call | flops 16777216 | bytes 25165824 | tf_op jit(solution)/shard_map/place_halves/pallas_call | solution.py:271
  79.5 0.0 reduce-scatter.2.cloned.1.call-update
  79.6 1.4 all-to-all-done.slots_ref
  81.0 2.7 %place_whole.1 = bf16[512,512]{1,0:T(8,128)(2,1)S(1)} custom-call(bf16[32,272,128]{2,1,0:T(8,128)(2,1)S(1)} %all-to-all-done.slots_ref), custom_call_target="tpu_custom_call" | custom-call | flops 8388608 | bytes 16777216 | tf_op jit(solution)/shard_map/place_whole/pallas_call | solution.py:207
  83.6 26.5 %all_to_all.15 = bf16[16,32,512]{2,1,0:T(8,128)(2,1)S(1)} all-to-all(bf16[16,32,512]{2,1,0:T(8,128)(2,1)S(1)} %bitcast.23), channel_id=1, replica_groups=mesh['y'=8,'core'=2,'x'=4,'z'=8] {'y','core'}, dimensions={0} | all-to-all | bytes 1048576 | tf_op jit(solution)/shard_map/all_to_all | solution.py:303
  110.1 11.7 %reduce-scatter.2.cloned.1.call-done = bf16[1,512,256]{2,1,0:T(8,128)(2,1)} async-done(((bf16[8,512,256]{2,1,0:T(8,128)(2,1)}), bf16[1,512,256]{2,1,0:T(8,128)(2,1)}) %reduce-scatter.2.cloned.1.call-update) | async-done | bytes 262160 | tf_op jit(solution)/shard_map/reduce_scatter | solution.py:297
  121.8 12.0 %all-to-all-start.2 = ((bf16[16,32,256]{2,1,0:T(8,128)(2,1)}), bf16[16,32,256]{2,1,0:T(8,128)(2,1)S(1)}, u32[]{:S(2)}, u32[]{:S(2)}) async-start(bf16[16,32,256]{2,1,0:T(8,128)(2,1)} %bitcast.28), calls=%async_computation.3 | async-start | bytes 524288 | tf_op jit(solution)/shard_map/all_to_all | solution.py:298
  133.8 0.1 convert_reduce_fusion
  133.9 11.6 %all-to-all-done.2 = bf16[16,32,256]{2,1,0:T(8,128)(2,1)S(1)} async-done(((bf16[16,32,256]{2,1,0:T(8,128)(2,1)}), bf16[16,32,256]{2,1,0:T(8,128)(2,1)S(1)}, u32[]{:S(2)}, u32[]{:S(2)}) %all-to-all-start.2) | async-done | bytes 262176 | tf_op jit(solution)/shard_map/all_to_all | solution.py:298
  145.6 0.6 fusion
  (2 shorter events, 0.0 us)
Async XLA Ops:
  6.5 63.5 %all-gather.3.cloned.1.call-start = ((), (), s32[]{:S(2)}) async-start(), calls=%async_computation.5 | async-start | bytes 4755456 | tf_op jit(solution)/shard_map/all_gather | solution.py:296
  15.8 65.2 %all-to-all-start = ((bf16[32,272,128]{2,1,0:T(8,128)(2,1)}), bf16[32,272,128]{2,1,0:T(8,128)(2,1)S(1)}, u32[]{:S(2)}, u32[]{:S(2)}) async-start(bf16[32,272,128]{2,1,0:T(8,128)(2,1)} %match.1), calls=%async_computation | async-start | bytes 4456448 | tf_op jit(solution)/shard_map/all_to_all | solution.py:301
  29.5 92.3 %reduce-scatter.2.cloned.1.call-start = ((), (), s32[]{:S(2)}) async-start(), calls=%async_computation.4 | async-start | bytes 2359296 | tf_op jit(solution)/shard_map/reduce_scatter | solution.py:297
  121.8 23.7 %all-to-all-start.2 = ((bf16[16,32,256]{2,1,0:T(8,128)(2,1)}), bf16[16,32,256]{2,1,0:T(8,128)(2,1)S(1)}, u32[]{:S(2)}, u32[]{:S(2)}) async-start(bf16[16,32,256]{2,1,0:T(8,128)(2,1)} %bitcast.28), calls=%async_computation.3 | async-start | bytes 524288 | tf_op jit(solution)/shard_map/all_to_all | solution.py:298
Sparse Core Ops, SparseCore 0:
  9.5 60.4 all-gather.2
  79.7 42.0 reduce-scatter.1

commit v9 on v8

--- a/solution.py
+++ b/solution.py
@@ -67,11 +67,15 @@
             for k in range(BASIS):
                 image = across[:, k * S : (k + 1) * S]
                 plain = coef_ref[3 * k, i] + coef_ref[3 * k + 2, i] * x
-                stack[part, k * S : (k + 1) * S, 0:S] = (image * plain).astype(jnp.bfloat16)
-                stack[part, k * S : (k + 1) * S, S : 2 * S] = (image * coef_ref[3 * k + 1, i]).astype(jnp.bfloat16)
+                for at, value in ((0, image * plain), (S, image * coef_ref[3 * k + 1, i])):
+                    upper = value.astype(jnp.bfloat16)
+                    lower = (value - upper.astype(jnp.float32)).astype(jnp.bfloat16)
+                    stack[part, k * S : (k + 1) * S, at : at + S] = upper
+                    stack[part, k * S : (k + 1) * S, 2 * S + at : 3 * S + at] = lower
         for part in range(GROUP):
             i = step * GROUP + part
             sums = jnp.dot(cols_tab[...], stack[part], preferred_element_type=jnp.float32)
+            sums = sums[:, 0 : 2 * S] + sums[:, 2 * S : 4 * S]
             weight = weight_ref[i].astype(jnp.float32)
             term = ((sums[:, 0:S] + y * sums[:, S : 2 * S]) * weight).astype(jnp.bfloat16)
             for n in range(2):
@@ -100,7 +104,7 @@
             pltpu.VMEM((16, S), jnp.float32),
             pltpu.VMEM((BASIS * S, S), jnp.bfloat16),
             pltpu.VMEM((S, BASIS * S), jnp.bfloat16),
-            pltpu.VMEM((GROUP, BASIS * S, 2 * S), jnp.bfloat16),
+            pltpu.VMEM((GROUP, BASIS * S, 4 * S), jnp.bfloat16),
             pltpu.SMEM((owners,), jnp.int32),
         ],
         compiler_params=pltpu.CompilerParams(vmem_limit_bytes=60 * 2**20),
@@ -117,32 +121,47 @@
     )
 
 
-def lines_kernel(dest_ref, off_ref, weight_ref, near_ref):
-    rows = weight_ref.shape[0]
-    near_ref[0:rows, :] = weight_ref[...]
+def lines_kernel(dest_ref, off_ref, out_ref):
     line = lax.broadcasted_iota(jnp.int32, (META, S), 0)
     lane = lax.broadcasted_iota(jnp.int32, (META, S), 1)
     words = jnp.zeros((META, S), jnp.int32)
-    for block in range(rows // S):
+    for block in range(dest_ref.shape[1]):
         for n in range(2):
             for at, number in enumerate(places(dest_ref, off_ref, block, n)):
                 words = jnp.where((line == n) & (lane == 8 * block + at), number, words)
-    near_ref[rows : rows + META, :] = words.astype(jnp.float32).astype(jnp.bfloat16)
-
-
-def with_lines(weight, destinations, offsets):
+    words = words.astype(jnp.float32).astype(jnp.bfloat16)
+    for taker in range(out_ref.shape[0]):
+        out_ref[taker] = words
+
+
+def lines_of(destinations, offsets, takers):
     smem = pl.BlockSpec(memory_space=pltpu.SMEM)
-    vmem = pl.BlockSpec(memory_space=pltpu.VMEM)
-    rows = weight.shape[0] * S
     return pl.pallas_call(
         lines_kernel,
-        out_shape=jax.ShapeDtypeStruct((rows + META, S), jnp.bfloat16),
-        in_specs=[smem, smem, vmem],
-        out_specs=vmem,
+        out_shape=jax.ShapeDtypeStruct((takers, META, S), jnp.bfloat16),
+        in_specs=[smem, smem],
+        out_specs=pl.BlockSpec(memory_space=pltpu.VMEM),
         compiler_params=pltpu.CompilerParams(vmem_limit_bytes=60 * 2**20),
         cost_estimate=pl.CostEstimate(flops=2**16, bytes_accessed=2**22, transcendentals=0),
         name="lines",
-    )(destinations.T, jnp.transpose(offsets, (1, 2, 0)), weight.reshape(rows, S))
+    )(destinations.T, jnp.transpose(offsets, (1, 2, 0)))
+
+
+def held_kernel(large_ref, small_ref, out_ref):
+    pass
+
+
+def held_until(large, small):
+    hbm = pl.BlockSpec(memory_space=pltpu.HBM)
+    return pl.pallas_call(
+        held_kernel,
+        out_shape=jax.ShapeDtypeStruct(large.shape, large.dtype),
+        in_specs=[hbm, hbm],
+        out_specs=hbm,
+        input_output_aliases={0: 0},
+        compiler_params=pltpu.CompilerParams(vmem_limit_bytes=60 * 2**20),
+        name="held_until",
+    )(large, small)
 
 
 def listed(codes, total, queue, idle):
@@ -152,18 +171,18 @@
         return found + jnp.where(code >= 0, 1, 0)
 
     found = lax.fori_loop(0, total, one, jnp.int32(0), unroll=8)
-    queue[found] = idle
-    queue[found + 1] = idle
+    for after in range(4):
+        queue[found + after] = idle
     return found
 
 
 def add_pieces(queue, found, blocks, canvas):
     lane = lax.broadcasted_iota(jnp.int32, (S, LANES), 1)
 
-    def pair(step, carry):
+    def some(step, carry):
         values = []
-        for part in range(2):
-            code = queue[2 * step + part]
+        for part in range(4):
+            code = queue[4 * step + part]
             shift = code & 127
             value = pltpu.roll(blocks((code >> 7) & 127).astype(jnp.float32), shift, 1)
             values.append((code >> 17, (code >> 14) & 7, value, lane >= shift))
@@ -172,7 +191,7 @@
             canvas[tile + 1, pl.ds(row, S), :] += jnp.where(here, 0.0, value)
         return carry
 
-    lax.fori_loop(0, (found + 1) // 2, pair, 0)
+    lax.fori_loop(0, (found + 3) // 4, some, 0)
 
 
 def whole_kernel(slots_ref, out_ref, canvas, told, codes, queue, sem):
@@ -213,7 +232,7 @@
             pltpu.VMEM((P_SIZE // LANES + 2, P_SIZE, LANES), jnp.float32),
             pltpu.VMEM((8, S), jnp.int32),
             pltpu.SMEM((8, S), jnp.int32),
-            pltpu.SMEM((2 * sources + 2,), jnp.int32),
+            pltpu.SMEM((2 * sources + 4,), jnp.int32),
             pltpu.SemaphoreType.DMA,
         ],
         compiler_params=pltpu.CompilerParams(vmem_limit_bytes=8 * 2**20),
@@ -222,7 +241,7 @@
     )(slots)
 
 
-def halves_kernel(where_ref, parts_ref, out_ref, held, canvas, packed, told, codes, queue, sems):
+def halves_kernel(where_ref, parts_ref, lines_ref, out_ref, held, canvas, packed, told, codes, queue, sems):
     sources, count = held.shape[0], held.shape[1] // S
     patches = out_ref.shape[0]
     fetch = pltpu.make_async_copy(parts_ref, held, sems.at[patches])
@@ -230,8 +249,7 @@
     mine, core = where_ref[0], where_ref[1]
     for tile in (1, 2):
         canvas[tile] = jnp.zeros((patches * P_SIZE, LANES), jnp.float32)
-    fetch.wait()
-    notes = held[:, count * S : count * S + META, :].astype(jnp.float32).astype(jnp.int32)[:, 0:8, :]
+    notes = lines_ref[...].astype(jnp.float32).astype(jnp.int32)[:, 0:8, :]
     notes = notes.reshape(sources * 8, S)
     at = [notes] + [pltpu.roll(notes, S - i, 1) for i in range(1, 5)]
     place = lax.broadcasted_iota(jnp.int32, notes.shape, 0) >> 3
@@ -249,6 +267,7 @@
     tell.start()
     tell.wait()
     found = listed(lambda i: codes[i // S, lax.rem(i, S)], 2 * sources * count, queue, 3 << 14)
+    fetch.wait()
 
     def block(i):
         return held[lax.div(i, count), pl.ds(pl.multiple_of(lax.rem(i, count) * S, S), S), :]
@@ -265,13 +284,13 @@
         copy.wait()
 
 
-def place_halves(where, parts):
+def place_halves(where, parts, lines):
     sources, rows, patches = parts.shape[0], parts.shape[1], 8
     hbm = pl.BlockSpec(memory_space=pltpu.HBM)
     return pl.pallas_call(
         halves_kernel,
         out_shape=jax.ShapeDtypeStruct((patches, P_SIZE, 2 * LANES), jnp.bfloat16),
-        in_specs=[pl.BlockSpec(memory_space=pltpu.SMEM), hbm],
+        in_specs=[pl.BlockSpec(memory_space=pltpu.SMEM), hbm, pl.BlockSpec(memory_space=pltpu.VMEM)],
         out_specs=hbm,
         scratch_shapes=[
             pltpu.VMEM((sources, rows, S), jnp.bfloat16),
@@ -279,13 +298,13 @@
             pltpu.VMEM((patches, P_SIZE, 2 * LANES), jnp.bfloat16),
             pltpu.VMEM((8, S), jnp.int32),
             pltpu.SMEM((8, S), jnp.int32),
-            pltpu.SMEM((2 * sources * (rows // S) + 2,), jnp.int32),
+            pltpu.SMEM((2 * sources * (rows // S) + 4,), jnp.int32),
             pltpu.SemaphoreType.DMA((patches + 2,)),
         ],
         compiler_params=pltpu.CompilerParams(vmem_limit_bytes=60 * 2**20),
         cost_estimate=pl.CostEstimate(flops=2**24, bytes_accessed=24 * 2**20, transcendentals=0),
         name="place_halves",
-    )(where, parts)
+    )(where, parts, lines)
 
 
 def body(blocks, inv_variance, destinations, offsets, coefficients, basis_rows, basis_cols):
@@ -293,12 +312,14 @@
     where = jnp.stack([lax.axis_index("x"), lax.axis_index("core")]).astype(jnp.int32)
     weight = inv_variance[0]
 
-    near = lax.all_gather(with_lines(weight, destinations[0], offsets[0]), ("core", "x"))
-    den = lax.psum_scatter(place_halves(where, near), "z", scatter_dimension=0, tiled=True)
+    near = lax.all_gather(weight.reshape(-1, S), ("core", "x"))
+    lines = lines_of(destinations[0], offsets[0], near.shape[0])
+    lines = lax.all_to_all(lines, ("core", "x"), 0, 0, tiled=True)
+    den = lax.psum_scatter(place_halves(where, near, lines), "z", scatter_dimension=0, tiled=True)
     den = lax.all_to_all(den.reshape(16, BAND, 2 * LANES), ("y", "core"), 0, 0, tiled=True)
 
     slots = match(blocks[0], weight, destinations[0], offsets[0], coefficients[0], basis_rows, basis_cols, owners)
-    slots = lax.all_to_all(slots, ("x", "z"), 0, 0, tiled=True)
+    slots = lax.all_to_all(held_until(slots, lines), ("x", "z"), 0, 0, tiled=True)
     num = place_whole(slots).reshape(16, BAND, P_SIZE)
     num = lax.all_to_all(num, ("y", "core"), 0, 0, tiled=True)
 

time: 154 us -> 149 us (0.968)
  waiting for transfers between devices: 64.5 us -> 56.4 us
  blocking collectives: 26.5 us -> 28.8 us
  starting transfers between devices: 25.8 us -> 28.1 us
  Pallas kernels: 20.1 us -> 18 us
    all_to_all x1 -> x2, waiting for transfers between devices: 1.4 us -> 18.6 us  [the longest x1 18.6 us: body(): lax.all_to_all(held_until(slots, lines), ('x', 'z'), 0, 0, tiled=True)]
    all_gather x1, waiting for transfers between devices: 39.8 us -> 25.4 us  [body(): near = lax.all_gather(weight.reshape(-1, S), ('core', 'x'))]
    reduce_scatter x1, waiting for transfers between devices: 11.7 us -> 0.01 us  [body(): lax.psum_scatter(place_halves(where, near, lines), 'z', scatter_dimension...]
    all_to_all x1 -> x2, starting transfers between devices: 13.7 us -> 18.8 us  [the longest x1 10.1 us: body(): lines = lax.all_to_all(lines, ('core', 'x'), 0, 0, tiled=True)]
    pallas_call x1, Pallas kernels: 9.52 us -> 6.45 us  [place_halves(): pl.pallas_call(halves_kernel, out_shape=jax.ShapeDtypeStruct((patches, P_...]
    all_to_all x1, starting transfers between devices: 12 us -> 9.18 us  [body(): lax.all_to_all(den.reshape(16, BAND, 2 * LANES), ('y', 'core'), 0, 0, til...]
    all_to_all x1, blocking collectives: 26.5 us -> 28.8 us  [body(): num = lax.all_to_all(num, ('y', 'core'), 0, 0, tiled=True)]
    pallas_call x1, Pallas kernels: 5.77 us -> 7.62 us  [match(): pl.pallas_call(match_kernel, out_shape=jax.ShapeDtypeStruct((owners, 2 *...]
  transfers between devices with their start and end apart: 4 -> 5, of which waited for: 4 -> 3; matrix products, arithmetic and copies ran while one was open for 1% -> 1% of each run, Pallas kernels for 12% -> 12%
where the time goes in v9:
time: 149 us; the launch traced here: 148 us
  waiting for transfers between devices  56.4 us (38%)
  blocking collectives  28.8 us (19%)
  starting transfers between devices  28.1 us (19%)
  Pallas kernels  18 us (12%)
  between operations  13.4 us (9%)
  local copies, waits for them, and re-layouts  1.91 us (1%)
    all_to_all x1, blocking collectives, body(): num = lax.all_to_all(num, ('y', 'core'), 0, 0, tiled=True)  28.8 us
    all_gather x1, waiting for transfers between devices, body(): near = lax.all_gather(weight.reshape(-1, S), ('core', 'x'))  25.4 us
    all_to_all x1, waiting for transfers between devices, body(): lax.all_to_all(held_until(slots, lines), ('x', 'z'), 0, 0, tiled=True)  18.6 us
    all_to_all x1, waiting for transfers between devices, body(): lax.all_to_all(den.reshape(16, BAND, 2 * LANES), ('y', 'core'), 0, 0, til...  11.6 us
    all_to_all x1, starting transfers between devices, body(): lines = lax.all_to_all(lines, ('core', 'x'), 0, 0, tiled=True)  10.1 us
    all_to_all x1, starting transfers between devices, body(): lax.all_to_all(den.reshape(16, BAND, 2 * LANES), ('y', 'core'), 0, 0, til...  9.18 us
    all_to_all x1, starting transfers between devices, body(): lax.all_to_all(held_until(slots, lines), ('x', 'z'), 0, 0, tiled=True)  8.69 us
    pallas_call x1, Pallas kernels, match(): pl.pallas_call(match_kernel, out_shape=jax.ShapeDtypeStruct((owners, 2 *...  7.62 us
  transfers between devices with their start and end apart: 5, of which 3 were waited for; matrix products, arithmetic and copies ran while one was open for 1% of the time, Pallas kernels for 12%

profile of v9, /device:TPU:1, one launch (start us, length us, event | category | flops | bytes accessed | tf_op | source)
XLA Modules:
  0.0 148.0 jit_solution(9801303479235589026)
XLA Ops:
  6.5 0.0 all-gather.2.cloned.1.call-start
  6.5 0.7 all-gather.2.cloned.1.call-update
  7.3 1.6 %lines.1 = bf16[8,16,128]{2,1,0:T(8,128)(2,1)} custom-call(s32[2,16]{1,0:T(2,128)} %bitcast.30, s32[2,2,16]{2,1,0:T(2,128)} %bitcast.28), custom_call_target="tpu_custom_call" | custom-call | flops 65536 | bytes 4194304 | tf_op jit(solution)/shard_map/lines/pallas_call | solution.py:139
  8.9 10.1 %all-to-all-start = ((bf16[8,16,128]{2,1,0:T(8,128)(2,1)}), bf16[8,16,128]{2,1,0:T(8,128)(2,1)S(1)}, u32[]{:S(2)}, u32[]{:S(2)}) async-start(bf16[8,16,128]{2,1,0:T(8,128)(2,1)} %lines.1), calls=%async_computation | async-start | bytes 65536 | tf_op jit(solution)/shard_map/all_to_all | solution.py:317
  19.0 1.3 copy.11
  20.3 7.6 %match.1.large_ref = bf16[32,272,128]{2,1,0:T(8,128)(2,1)} custom-call(f32[15,16]{1,0:T(8,128)} %bitcast.27, s32[2,16]{1,0:T(2,128)} %bitcast.31, s32[2,2,16]{2,1,0:T(2,128)} %bitcast.29, bf16[5,41]{1,0:T(8,128)(2,1)} %rows_ref.1, bf16[5,41]{1,0:T(8,128)(2,1)} %cols_ref.1, bf16[16,128,128]{2,1,0:T(8,128)(2,1)} %bitcast.32, bf16[16,128,128]{2,1,0:T(8,128)(2,1)} %bitcast.25), custom_call_target="tpu_custom_call" | custom-call | flops 1073741824 | bytes 16777216 | tf_op jit(solution)/shard_map/match/pallas_call | solution.py:98
  27.9 0.0 all-to-all-done.small_ref.lines_ref
  27.9 0.0 copy-start
  27.9 0.6 copy-done
  28.6 8.7 %all-to-all-start.1 = ((bf16[32,272,128]{2,1,0:T(8,128)(2,1)}), bf16[32,272,128]{2,1,0:T(8,128)(2,1)S(1)}, u32[]{:S(2)}, u32[]{:S(2)}) async-start(bf16[32,272,128]{2,1,0:T(8,128)(2,1)} %held_until.1), calls=%async_computation.1 | async-start | bytes 4456448 | tf_op jit(solution)/shard_map/all_to_all | solution.py:322
  37.3 0.0 reduce-scatter.2.cloned.1.call-start
  37.3 0.6 pad_add_fusion.where_ref
  38.0 25.4 %all-gather.2.cloned.1.call-done.parts_ref = bf16[8,2048,128]{2,1,0:T(8,128)(2,1)} async-done(((bf16[1,2048,128]{2,1,0:T(8,128)(2,1)}), bf16[8,2048,128]{2,1,0:T(8,128)(2,1)}) %all-gather.2.cloned.1.call-update) | async-done | bytes 4194320 | tf_op jit(solution)/shard_map/all_gather | solution.py:315
  63.4 6.5 %place_halves.1 = bf16[8,512,256]{2,1,0:T(8,128)(2,1)} custom-call(s32[2]{0:T(128)} %pad_add_fusion.where_ref, bf16[8,2048,128]{2,1,0:T(8,128)(2,1)} %all-gather.2.cloned.1.call-done.parts_ref, bf16[8,16,128]{2,1,0:T(8,128)(2,1)} %copy-done), custom_call_target="tpu_custom_call" | custom-call | flops 16777216 | bytes 25165824 | tf_op jit(solution)/shard_map/place_halves/pallas_call | solution.py:290
  69.8 0.0 reduce-scatter.2.cloned.1.call-update
  69.9 18.6 %all-to-all-done.1.slots_ref = bf16[32,272,128]{2,1,0:T(8,128)(2,1)S(1)} async-done(((bf16[32,272,128]{2,1,0:T(8,128)(2,1)}), bf16[32,272,128]{2,1,0:T(8,128)(2,1)S(1)}, u32[]{:S(2)}, u32[]{:S(2)}) %all-to-all-start.1) | async-done | bytes 2228256 | tf_op jit(solution)/shard_map/all_to_all | solution.py:322
  88.5 2.3 %place_whole.1 = bf16[512,512]{1,0:T(8,128)(2,1)S(1)} custom-call(bf16[32,272,128]{2,1,0:T(8,128)(2,1)S(1)} %all-to-all-done.1.slots_ref), custom_call_target="tpu_custom_call" | custom-call | flops 8388608 | bytes 16777216 | tf_op jit(solution)/shard_map/place_whole/pallas_call | solution.py:226
  90.8 28.8 %all_to_all.20 = bf16[16,32,512]{2,1,0:T(8,128)(2,1)S(1)} all-to-all(bf16[16,32,512]{2,1,0:T(8,128)(2,1)S(1)} %bitcast.22), channel_id=1, replica_groups=mesh['y'=8,'core'=2,'x'=4,'z'=8] {'y','core'}, dimensions={0} | all-to-all | bytes 1048576 | tf_op jit(solution)/shard_map/all_to_all | solution.py:324
  119.6 0.0 reduce-scatter.2.cloned.1.call-done
  119.6 9.2 %all-to-all-start.3 = ((bf16[16,32,256]{2,1,0:T(8,128)(2,1)}), bf16[16,32,256]{2,1,0:T(8,128)(2,1)S(1)}, u32[]{:S(2)}, u32[]{:S(2)}) async-start(bf16[16,32,256]{2,1,0:T(8,128)(2,1)} %bitcast.26), calls=%async_computation.4 | async-start | bytes 524288 | tf_op jit(solution)/shard_map/all_to_all | solution.py:319
  128.8 0.1 convert_reduce_fusion
  128.8 11.6 %all-to-all-done.3 = bf16[16,32,256]{2,1,0:T(8,128)(2,1)S(1)} async-done(((bf16[16,32,256]{2,1,0:T(8,128)(2,1)}), bf16[16,32,256]{2,1,0:T(8,128)(2,1)S(1)}, u32[]{:S(2)}, u32[]{:S(2)}) %all-to-all-start.3) | async-done | bytes 262176 | tf_op jit(solution)/shard_map/all_to_all | solution.py:319
  140.5 0.6 fusion
  (3 shorter events, 0.0 us)
Async XLA Ops:
  6.5 56.8 %all-gather.2.cloned.1.call-start = ((), (), s32[]{:S(2)}) async-start(), calls=%async_computation.5 | async-start | bytes 4718592 | tf_op jit(solution)/shard_map/all_gather | solution.py:315
  8.9 19.1 %all-to-all-start = ((bf16[8,16,128]{2,1,0:T(8,128)(2,1)}), bf16[8,16,128]{2,1,0:T(8,128)(2,1)S(1)}, u32[]{:S(2)}, u32[]{:S(2)}) async-start(bf16[8,16,128]{2,1,0:T(8,128)(2,1)} %lines.1), calls=%async_computation | async-start | bytes 65536 | tf_op jit(solution)/shard_map/all_to_all | solution.py:317
  27.9 0.6 copy-start
  28.6 59.9 %all-to-all-start.1 = ((bf16[32,272,128]{2,1,0:T(8,128)(2,1)}), bf16[32,272,128]{2,1,0:T(8,128)(2,1)S(1)}, u32[]{:S(2)}, u32[]{:S(2)}) async-start(bf16[32,272,128]{2,1,0:T(8,128)(2,1)} %held_until.1), calls=%async_computation.1 | async-start | bytes 4456448 | tf_op jit(solution)/shard_map/all_to_all | solution.py:322
  37.3 82.3 %reduce-scatter.2.cloned.1.call-start = ((), (), s32[]{:S(2)}) async-start(), calls=%async_computation.6 | async-start | bytes 2359296 | tf_op jit(solution)/shard_map/reduce_scatter | solution.py:318
  119.6 20.9 %all-to-all-start.3 = ((bf16[16,32,256]{2,1,0:T(8,128)(2,1)}), bf16[16,32,256]{2,1,0:T(8,128)(2,1)S(1)}, u32[]{:S(2)}, u32[]{:S(2)}) async-start(bf16[16,32,256]{2,1,0:T(8,128)(2,1)} %bitcast.26), calls=%async_computation.4 | async-start | bytes 524288 | tf_op jit(solution)/shard_map/all_to_all | solution.py:319
Sparse Core Ops, SparseCore 0:
  9.5 53.8 all-gather.1
  70.0 47.2 reduce-scatter.1

commit v10 on v9

--- a/solution.py
+++ b/solution.py
@@ -18,6 +18,8 @@
 META = 16
 LEAD = 4
 GROUP = 4
+MARGIN = 48
+WINDOW = 48
 
 
 def places(dest_ref, off_ref, block, n):
@@ -167,28 +169,31 @@
 def listed(codes, total, queue, idle):
     def one(i, found):
         code = codes(i)
-        queue[found] = code
+        queue[0, found] = code
+        queue[1, found] = i
         return found + jnp.where(code >= 0, 1, 0)
 
     found = lax.fori_loop(0, total, one, jnp.int32(0), unroll=8)
     for after in range(4):
-        queue[found + after] = idle
+        queue[0, found + after] = idle
+        queue[1, found + after] = 0
     return found
 
 
-def add_pieces(queue, found, blocks, canvas):
-    lane = lax.broadcasted_iota(jnp.int32, (S, LANES), 1)
+def add_pieces(queue, found, rows, piece, canvas):
+    lane = lax.broadcasted_iota(jnp.int32, (rows, LANES), 1)
 
     def some(step, carry):
         values = []
         for part in range(4):
-            code = queue[4 * step + part]
+            code = queue[0, 4 * step + part]
             shift = code & 127
-            value = pltpu.roll(blocks((code >> 7) & 127).astype(jnp.float32), shift, 1)
-            values.append((code >> 17, (code >> 14) & 7, value, lane >= shift))
+            value = piece(queue[1, 4 * step + part], ((code >> 7) & 7) * 16)
+            value = pltpu.roll(value.astype(jnp.float32), shift, 1)
+            values.append((code >> 13, (code >> 10) & 7, value, lane >= shift))
         for row, tile, value, here in values:
-            canvas[tile, pl.ds(row, S), :] += jnp.where(here, value, 0.0)
-            canvas[tile + 1, pl.ds(row, S), :] += jnp.where(here, 0.0, value)
+            canvas[tile, pl.ds(row, rows), :] += jnp.where(here, value, 0.0)
+            canvas[tile + 1, pl.ds(row, rows), :] += jnp.where(here, 0.0, value)
         return carry
 
     lax.fori_loop(0, (found + 3) // 4, some, 0)
@@ -199,9 +204,7 @@
     notes = slots_ref[:, 2 * S : 2 * S + META, :].astype(jnp.float32).astype(jnp.int32)[:, 0:8, :]
     notes = notes.reshape(sources * 8, S)
     at = [notes] + [pltpu.roll(notes, S - i, 1) for i in range(1, 5)]
-    place = lax.broadcasted_iota(jnp.int32, notes.shape, 0)
-    place = (place >> 3) * 2 + (place & 7)
-    code = ((at[1] * LANES + at[2]) << 17) + (at[3] << 14) + (place << 7) + at[4]
+    code = ((at[1] * LANES + at[2]) << 13) + (at[3] << 10) + at[4]
     code = jnp.where(at[0] > 0, code, -1)[:, 0:1].reshape(sources, 8, 1)
     lane = lax.broadcasted_iota(jnp.int32, (sources, 8, S), 2)
     source = lax.broadcasted_iota(jnp.int32, (sources, 8, S), 0)
@@ -211,12 +214,12 @@
     for tile in range(P_SIZE // LANES):
         canvas[tile] = jnp.zeros((P_SIZE, LANES), jnp.float32)
     tell.wait()
-    found = listed(lambda i: codes[i & 1, i >> 1], 2 * sources, queue, (P_SIZE // LANES) << 14)
-
-    def block(i):
+    found = listed(lambda i: codes[i & 1, i >> 1], 2 * sources, queue, (P_SIZE // LANES) << 10)
+
+    def piece(i, start):
         return slots_ref[i >> 1, pl.ds(pl.multiple_of((i & 1) * S, S), S), :]
 
-    add_pieces(queue, found, block, canvas)
+    add_pieces(queue, found, S, piece, canvas)
     for tile in range(P_SIZE // LANES):
         out_ref[:, tile * LANES : (tile + 1) * LANES] = canvas[tile].astype(jnp.bfloat16)
 
@@ -232,7 +235,7 @@
             pltpu.VMEM((P_SIZE // LANES + 2, P_SIZE, LANES), jnp.float32),
             pltpu.VMEM((8, S), jnp.int32),
             pltpu.SMEM((8, S), jnp.int32),
-            pltpu.SMEM((2 * sources + 4,), jnp.int32),
+            pltpu.SMEM((2, 2 * sources + 4), jnp.int32),
             pltpu.SemaphoreType.DMA,
         ],
         compiler_params=pltpu.CompilerParams(vmem_limit_bytes=8 * 2**20),
@@ -241,82 +244,82 @@
     )(slots)
 
 
-def halves_kernel(where_ref, parts_ref, lines_ref, out_ref, held, canvas, packed, told, codes, queue, sems):
+def band_kernel(where_ref, parts_ref, lines_ref, out_ref, held, canvas, told, codes, queue, sems):
     sources, count = held.shape[0], held.shape[1] // S
     patches = out_ref.shape[0]
-    fetch = pltpu.make_async_copy(parts_ref, held, sems.at[patches])
+    fetch = pltpu.make_async_copy(parts_ref, held, sems.at[0])
     fetch.start()
-    mine, core = where_ref[0], where_ref[1]
-    for tile in (1, 2):
-        canvas[tile] = jnp.zeros((patches * P_SIZE, LANES), jnp.float32)
+    band = where_ref[0] * BAND
+    for patch in range(patches):
+        for tile in range(P_SIZE // LANES):
+            canvas[tile, patch * S + MARGIN : patch * S + MARGIN + BAND, :] = jnp.zeros((BAND, LANES), jnp.float32)
     notes = lines_ref[...].astype(jnp.float32).astype(jnp.int32)[:, 0:8, :]
     notes = notes.reshape(sources * 8, S)
     at = [notes] + [pltpu.roll(notes, S - i, 1) for i in range(1, 5)]
-    place = lax.broadcasted_iota(jnp.int32, notes.shape, 0) >> 3
-    place = place * count + (lax.broadcasted_iota(jnp.int32, notes.shape, 1) >> 3)
-    tile = at[3] - 2 * core + 1
-    row = (at[0] & 7) * P_SIZE + at[1] * LANES + at[2]
-    code = (row << 17) + (tile << 14) + (place << 7) + at[4]
-    code = jnp.where(((at[0] >> 3) == mine) & (tile >= 0) & (tile <= 2), code, -1)
+    ahead = band - (at[1] * LANES + at[2])
+    start = jnp.clip((ahead >> 4) << 4, 0, S - WINDOW)
+    row = at[0] * S + MARGIN + start - ahead
+    code = (row << 13) + (at[3] << 10) + ((start >> 4) << 7) + at[4]
+    code = jnp.where((ahead > -BAND) & (ahead < S), code, -1)
     first = (lax.broadcasted_iota(jnp.int32, (8, S), 1) & 7) == 0
-    words = jnp.zeros((8, S), jnp.int32)
-    for i in range(sources):
-        words += pltpu.roll(jnp.where(first, code[8 * i : 8 * i + 8, :], 0), i, 1)
-    told[...] = words
-    tell = pltpu.make_async_copy(told, codes, sems.at[patches + 1])
+    for group in range(sources // 8):
+        words = jnp.zeros((8, S), jnp.int32)
+        for i in range(8):
+            source = 8 * group + i
+            words += pltpu.roll(jnp.where(first, code[8 * source : 8 * source + 8, :], 0), i, 1)
+        told[group] = words
+    tell = pltpu.make_async_copy(told, codes, sems.at[1])
     tell.start()
     tell.wait()
-    found = listed(lambda i: codes[i // S, lax.rem(i, S)], 2 * sources * count, queue, 3 << 14)
+    idle = ((patches - 1) * S + MARGIN + BAND) << 13
+    found = listed(lambda i: codes[i >> 8, (i >> 7) & 1, i & 127], 2 * sources * count, queue, idle)
     fetch.wait()
 
-    def block(i):
-        return held[lax.div(i, count), pl.ds(pl.multiple_of(lax.rem(i, count) * S, S), S), :]
-
-    add_pieces(queue, found, block, canvas)
-    copies = []
+    def piece(i, start):
+        begin = ((i & 127) >> 3) * S + start
+        return held[(i >> 8) * 8 + (i & 7), pl.ds(pl.multiple_of(begin, 16), WINDOW), :]
+
+    add_pieces(queue, found, WINDOW, piece, canvas)
     for patch in range(patches):
-        for half in range(2):
-            rows = canvas[half + 1, patch * P_SIZE : (patch + 1) * P_SIZE, :]
-            packed[patch, :, half * LANES : (half + 1) * LANES] = rows.astype(jnp.bfloat16)
-        copies.append(pltpu.make_async_copy(packed.at[patch], out_ref.at[patch], sems.at[patch]))
-        copies[-1].start()
-    for copy in copies:
-        copy.wait()
-
-
-def place_halves(where, parts, lines):
-    sources, rows, patches = parts.shape[0], parts.shape[1], 8
-    hbm = pl.BlockSpec(memory_space=pltpu.HBM)
-    return pl.pallas_call(
-        halves_kernel,
-        out_shape=jax.ShapeDtypeStruct((patches, P_SIZE, 2 * LANES), jnp.bfloat16),
-        in_specs=[pl.BlockSpec(memory_space=pltpu.SMEM), hbm, pl.BlockSpec(memory_space=pltpu.VMEM)],
-        out_specs=hbm,
+        for tile in range(P_SIZE // LANES):
+            rows = canvas[tile, patch * S + MARGIN : patch * S + MARGIN + BAND, :]
+            out_ref[patch, :, tile * LANES : (tile + 1) * LANES] = rows.astype(jnp.bfloat16)
+
+
+def place_band(where, parts, lines, patches):
+    sources, rows = parts.shape[0], parts.shape[1]
+    vmem = pl.BlockSpec(memory_space=pltpu.VMEM)
+    return pl.pallas_call(
+        band_kernel,
+        out_shape=jax.ShapeDtypeStruct((patches, BAND, P_SIZE), jnp.bfloat16),
+        in_specs=[pl.BlockSpec(memory_space=pltpu.SMEM), pl.BlockSpec(memory_space=pltpu.HBM), vmem],
+        out_specs=vmem,
         scratch_shapes=[
             pltpu.VMEM((sources, rows, S), jnp.bfloat16),
-            pltpu.VMEM((5, patches * P_SIZE, LANES), jnp.float32),
-            pltpu.VMEM((patches, P_SIZE, 2 * LANES), jnp.bfloat16),
-            pltpu.VMEM((8, S), jnp.int32),
-            pltpu.SMEM((8, S), jnp.int32),
-            pltpu.SMEM((2 * sources * (rows // S) + 4,), jnp.int32),
-            pltpu.SemaphoreType.DMA((patches + 2,)),
+            pltpu.VMEM((P_SIZE // LANES + 1, patches * S, LANES), jnp.float32),
+            pltpu.VMEM((sources // 8, 8, S), jnp.int32),
+            pltpu.SMEM((sources // 8, 8, S), jnp.int32),
+            pltpu.SMEM((2, 2 * sources * (rows // S) + 4), jnp.int32),
+            pltpu.SemaphoreType.DMA((2,)),
         ],
         compiler_params=pltpu.CompilerParams(vmem_limit_bytes=60 * 2**20),
         cost_estimate=pl.CostEstimate(flops=2**24, bytes_accessed=24 * 2**20, transcendentals=0),
-        name="place_halves",
+        name="place_band",
     )(where, parts, lines)
 
 
 def body(blocks, inv_variance, destinations, offsets, coefficients, basis_rows, basis_cols):
-    owners = lax.axis_size("x") * lax.axis_size("z")
-    where = jnp.stack([lax.axis_index("x"), lax.axis_index("core")]).astype(jnp.int32)
+    along = lax.axis_size("x")
+    owners = along * lax.axis_size("z")
+    where = lax.axis_index(("y", "core")).astype(jnp.int32).reshape(1)
     weight = inv_variance[0]
 
-    near = lax.all_gather(weight.reshape(-1, S), ("core", "x"))
+    near = lax.all_gather(weight.reshape(-1, S), ("y", "core"))
     lines = lines_of(destinations[0], offsets[0], near.shape[0])
-    lines = lax.all_to_all(lines, ("core", "x"), 0, 0, tiled=True)
-    den = lax.psum_scatter(place_halves(where, near, lines), "z", scatter_dimension=0, tiled=True)
-    den = lax.all_to_all(den.reshape(16, BAND, 2 * LANES), ("y", "core"), 0, 0, tiled=True)
+    lines = lax.all_to_all(lines, ("y", "core"), 0, 0, tiled=True)
+    den = place_band(where, near, lines, owners).reshape(along, owners // along, BAND, P_SIZE)
+    den = lax.psum_scatter(den, "x", scatter_dimension=0, tiled=True)[0]
+    den = lax.all_to_all(den, "z", 0, 0, tiled=True)
 
     slots = match(blocks[0], weight, destinations[0], offsets[0], coefficients[0], basis_rows, basis_cols, owners)
     slots = lax.all_to_all(held_until(slots, lines), ("x", "z"), 0, 0, tiled=True)
@@ -324,8 +327,7 @@
     num = lax.all_to_all(num, ("y", "core"), 0, 0, tiled=True)
 
     num = jnp.sum(num.astype(jnp.float32), axis=0)
-    den = jnp.sum(den.reshape(8, 2, BAND, 2 * LANES).astype(jnp.float32), axis=0)
-    den = jnp.concatenate([den[0], den[1]], axis=-1)
+    den = jnp.sum(den.astype(jnp.float32), axis=0)
     return (num / jnp.maximum(den, 1.0))[None]
 
 

time: 149 us -> 145 us (0.973)
  starting transfers between devices: 28.1 us -> 25 us
  Pallas kernels: 18 us -> 20.1 us
    all_to_all x1, waiting for transfers between devices: 18.6 us -> 9.75 us  [body(): lax.all_to_all(held_until(slots, lines), ('x', 'z'), 0, 0, tiled=True)]
    all_gather x1, waiting for transfers between devices: 25.4 us -> 33.6 us  [body(): near = lax.all_gather(weight.reshape(-1, S), ('y', 'core'))]
    all_to_all x2, starting transfers between devices: 19.3 us -> 13.6 us  [the longest x1 10.2 us: body(): lines = lax.all_to_all(lines, ('y', 'core'), 0, 0, tiled=True)]
    all_to_all x1, starting transfers between devices: 8.69 us -> 11.4 us  [body(): lax.all_to_all(held_until(slots, lines), ('x', 'z'), 0, 0, tiled=True)]
    pallas_call x1, Pallas kernels: 6.45 us -> 8.38 us  [place_band(): pl.pallas_call(band_kernel, out_shape=jax.ShapeDtypeStruct((patches, BAND...]
  transfers between devices with their start and end apart: 5 -> 5, of which waited for: 3 -> 3; matrix products, arithmetic and copies ran while one was open for 1% -> 1% of each run, Pallas kernels for 12% -> 14%
where the time goes in v10:
time: 145 us; the launch traced here: 144 us
  waiting for transfers between devices  55.3 us (38%)
  blocking collectives  28 us (19%)
  starting transfers between devices  25 us (17%)
  Pallas kernels  20.1 us (14%)
  between operations  13.5 us (9%)
  local copies, waits for them, and re-layouts  1.92 us (1%)
    all_gather x1, waiting for transfers between devices, body(): near = lax.all_gather(weight.reshape(-1, S), ('y', 'core'))  33.6 us
    all_to_all x1, blocking collectives, body(): num = lax.all_to_all(num, ('y', 'core'), 0, 0, tiled=True)  28 us
    all_to_all x1, starting transfers between devices, body(): lax.all_to_all(held_until(slots, lines), ('x', 'z'), 0, 0, tiled=True)  11.4 us
    all_to_all x1, waiting for transfers between devices, body(): den = lax.all_to_all(den, 'z', 0, 0, tiled=True)  11.2 us
    all_to_all x1, starting transfers between devices, body(): lines = lax.all_to_all(lines, ('y', 'core'), 0, 0, tiled=True)  10.2 us
    all_to_all x1, waiting for transfers between devices, body(): lax.all_to_all(held_until(slots, lines), ('x', 'z'), 0, 0, tiled=True)  9.75 us
    pallas_call x1, Pallas kernels, place_band(): pl.pallas_call(band_kernel, out_shape=jax.ShapeDtypeStruct((patches, BAND...  8.38 us
    pallas_call x1, Pallas kernels, match(): pl.pallas_call(match_kernel, out_shape=jax.ShapeDtypeStruct((owners, 2 *...  7.66 us
  transfers between devices with their start and end apart: 5, of which 3 were waited for; matrix products, arithmetic and copies ran while one was open for 1% of the time, Pallas kernels for 14%

profile of v10, /device:TPU:1, one launch (start us, length us, event | category | flops | bytes accessed | tf_op | source)
XLA Modules:
  0.0 144.4 jit_solution(17565471060432182890)
XLA Ops:
  6.5 0.0 all-gather.2.cloned.1.call-start
  6.5 0.7 all-gather.2.cloned.1.call-update
  7.3 1.6 %lines.1 = bf16[16,16,128]{2,1,0:T(8,128)(2,1)} custom-call(s32[2,16]{1,0:T(2,128)} %bitcast.28, s32[2,2,16]{2,1,0:T(2,128)} %bitcast.26), custom_call_target="tpu_custom_call" | custom-call | flops 65536 | bytes 4194304 | tf_op jit(solution)/shard_map/lines/pallas_call | solution.py:141
  8.9 10.2 %all-to-all-start = ((bf16[16,16,128]{2,1,0:T(8,128)(2,1)}), bf16[16,16,128]{2,1,0:T(8,128)(2,1)S(1)}, u32[]{:S(2)}, u32[]{:S(2)}) async-start(bf16[16,16,128]{2,1,0:T(8,128)(2,1)} %lines.1), calls=%async_computation | async-start | bytes 131072 | tf_op jit(solution)/shard_map/all_to_all | solution.py:319
  19.1 1.3 copy.11
  20.4 7.7 %match.1.large_ref = bf16[32,272,128]{2,1,0:T(8,128)(2,1)} custom-call(f32[15,16]{1,0:T(8,128)} %bitcast.25, s32[2,16]{1,0:T(2,128)} %bitcast.29, s32[2,2,16]{2,1,0:T(2,128)} %bitcast.27, bf16[5,41]{1,0:T(8,128)(2,1)} %rows_ref.1, bf16[5,41]{1,0:T(8,128)(2,1)} %cols_ref.1, bf16[16,128,128]{2,1,0:T(8,128)(2,1)} %bitcast.30, bf16[16,128,128]{2,1,0:T(8,128)(2,1)} %bitcast.23), custom_call_target="tpu_custom_call" | custom-call | flops 1073741824 | bytes 16777216 | tf_op jit(solution)/shard_map/match/pallas_call | solution.py:100
  28.0 0.0 all-to-all-done.small_ref.lines_ref
  28.0 0.0 copy-start
  28.0 0.6 copy-done
  28.7 11.4 %all-to-all-start.1 = ((bf16[32,272,128]{2,1,0:T(8,128)(2,1)}), bf16[32,272,128]{2,1,0:T(8,128)(2,1)S(1)}, u32[]{:S(2)}, u32[]{:S(2)}) async-start(bf16[32,272,128]{2,1,0:T(8,128)(2,1)} %held_until.1), calls=%async_computation.1 | async-start | bytes 4456448 | tf_op jit(solution)/shard_map/all_to_all | solution.py:325
  40.0 0.0 reduce-scatter.2.cloned.1.call-start
  40.1 33.6 %all-gather.2.cloned.1.call-done.parts_ref = bf16[16,2048,128]{2,1,0:T(8,128)(2,1)} async-done(((bf16[1,2048,128]{2,1,0:T(8,128)(2,1)}), bf16[16,2048,128]{2,1,0:T(8,128)(2,1)}) %all-gather.2.cloned.1.call-update) | async-done | bytes 8388624 | tf_op jit(solution)/shard_map/all_gather | solution.py:317
  73.6 8.4 %place_band.1 = bf16[32,32,512]{2,1,0:T(8,128)(2,1)} custom-call(s32[1]{0:T(128)} %bitcast.10.where_ref, bf16[16,2048,128]{2,1,0:T(8,128)(2,1)} %all-gather.2.cloned.1.call-done.parts_ref, bf16[16,16,128]{2,1,0:T(8,128)(2,1)} %copy-done), custom_call_target="tpu_custom_call" | custom-call | flops 16777216 | bytes 25165824 | tf_op jit(solution)/shard_map/place_band/pallas_call | solution.py:292
  82.0 0.0 reduce-scatter.2.cloned.1.call-update
  82.0 9.7 %all-to-all-done.1.slots_ref = bf16[32,272,128]{2,1,0:T(8,128)(2,1)S(1)} async-done(((bf16[32,272,128]{2,1,0:T(8,128)(2,1)}), bf16[32,272,128]{2,1,0:T(8,128)(2,1)S(1)}, u32[]{:S(2)}, u32[]{:S(2)}) %all-to-all-start.1) | async-done | bytes 2228256 | tf_op jit(solution)/shard_map/all_to_all | solution.py:325
  91.8 2.4 %place_whole.1 = bf16[512,512]{1,0:T(8,128)(2,1)S(1)} custom-call(bf16[32,272,128]{2,1,0:T(8,128)(2,1)S(1)} %all-to-all-done.1.slots_ref), custom_call_target="tpu_custom_call" | custom-call | flops 8388608 | bytes 16777216 | tf_op jit(solution)/shard_map/place_whole/pallas_call | solution.py:229
  94.2 28.0 %all_to_all.20 = bf16[16,32,512]{2,1,0:T(8,128)(2,1)S(1)} all-to-all(bf16[16,32,512]{2,1,0:T(8,128)(2,1)S(1)} %bitcast.20), channel_id=1, replica_groups=mesh['y'=8,'core'=2,'x'=4,'z'=8] {'y','core'}, dimensions={0} | all-to-all | bytes 1048576 | tf_op jit(solution)/shard_map/all_to_all | solution.py:327
  122.2 0.0 reduce-scatter.2.cloned.1.call-done
  122.2 3.4 %all-to-all-start.3 = ((bf16[8,32,512]{2,1,0:T(8,128)(2,1)}), bf16[8,32,512]{2,1,0:T(8,128)(2,1)S(1)}, u32[]{:S(2)}, u32[]{:S(2)}) async-start(bf16[8,32,512]{2,1,0:T(8,128)(2,1)} %bitcast.24), calls=%async_computation.4 | async-start | bytes 524288 | tf_op jit(solution)/shard_map/all_to_all | solution.py:322
  125.6 0.1 convert_reduce_fusion
  125.7 11.2 %all-to-all-done.3 = bf16[8,32,512]{2,1,0:T(8,128)(2,1)S(1)} async-done(((bf16[8,32,512]{2,1,0:T(8,128)(2,1)}), bf16[8,32,512]{2,1,0:T(8,128)(2,1)S(1)}, u32[]{:S(2)}, u32[]{:S(2)}) %all-to-all-start.3) | async-done | bytes 262176 | tf_op jit(solution)/shard_map/all_to_all | solution.py:322
  136.9 0.6 divide_bitcast_fusion
  (2 shorter events, 0.0 us)
Async XLA Ops:
  6.5 67.1 %all-gather.2.cloned.1.call-start = ((), (), s32[]{:S(2)}) async-start(), calls=%async_computation.5 | async-start | bytes 8912896 | tf_op jit(solution)/shard_map/all_gather | solution.py:317
  8.9 19.1 %all-to-all-start = ((bf16[16,16,128]{2,1,0:T(8,128)(2,1)}), bf16[16,16,128]{2,1,0:T(8,128)(2,1)S(1)}, u32[]{:S(2)}, u32[]{:S(2)}) async-start(bf16[16,16,128]{2,1,0:T(8,128)(2,1)} %lines.1), calls=%async_computation | async-start | bytes 131072 | tf_op jit(solution)/shard_map/all_to_all | solution.py:319
  28.0 0.6 copy-start
  28.7 63.1 %all-to-all-start.1 = ((bf16[32,272,128]{2,1,0:T(8,128)(2,1)}), bf16[32,272,128]{2,1,0:T(8,128)(2,1)S(1)}, u32[]{:S(2)}, u32[]{:S(2)}) async-start(bf16[32,272,128]{2,1,0:T(8,128)(2,1)} %held_until.1), calls=%async_computation.1 | async-start | bytes 4456448 | tf_op jit(solution)/shard_map/all_to_all | solution.py:325
  40.0 82.1 %reduce-scatter.2.cloned.1.call-start = ((), (), s32[]{:S(2)}) async-start(), calls=%async_computation.6 | async-start | bytes 1310720 | tf_op jit(solution)/shard_map/reduce_scatter | solution.py:321
  122.2 14.7 %all-to-all-start.3 = ((bf16[8,32,512]{2,1,0:T(8,128)(2,1)}), bf16[8,32,512]{2,1,0:T(8,128)(2,1)S(1)}, u32[]{:S(2)}, u32[]{:S(2)}) async-start(bf16[8,32,512]{2,1,0:T(8,128)(2,1)} %bitcast.24), calls=%async_computation.4 | async-start | bytes 524288 | tf_op jit(solution)/shard_map/all_to_all | solution.py:322
Sparse Core Ops, SparseCore 0:
  9.5 64.1 all-gather.1
  82.2 29.4 reduce-scatter.1

commit v11 on v10

--- a/solution.py
+++ b/solution.py
@@ -68,16 +68,12 @@
             )
             for k in range(BASIS):
                 image = across[:, k * S : (k + 1) * S]
-                plain = coef_ref[3 * k, i] + coef_ref[3 * k + 2, i] * x
-                for at, value in ((0, image * plain), (S, image * coef_ref[3 * k + 1, i])):
-                    upper = value.astype(jnp.bfloat16)
-                    lower = (value - upper.astype(jnp.float32)).astype(jnp.bfloat16)
-                    stack[part, k * S : (k + 1) * S, at : at + S] = upper
-                    stack[part, k * S : (k + 1) * S, 2 * S + at : 3 * S + at] = lower
+                plain = coef_ref[3 * k, 0, i] + coef_ref[3 * k + 2, 0, i] * x
+                stack[part, k * S : (k + 1) * S, 0:S] = (image * plain).astype(jnp.bfloat16)
+                stack[part, k * S : (k + 1) * S, S : 2 * S] = (image * coef_ref[3 * k + 1, 0, i]).astype(jnp.bfloat16)
         for part in range(GROUP):
             i = step * GROUP + part
             sums = jnp.dot(cols_tab[...], stack[part], preferred_element_type=jnp.float32)
-            sums = sums[:, 0 : 2 * S] + sums[:, 2 * S : 4 * S]
             weight = weight_ref[i].astype(jnp.float32)
             term = ((sums[:, 0:S] + y * sums[:, S : 2 * S]) * weight).astype(jnp.bfloat16)
             for n in range(2):
@@ -106,14 +102,14 @@
             pltpu.VMEM((16, S), jnp.float32),
             pltpu.VMEM((BASIS * S, S), jnp.bfloat16),
             pltpu.VMEM((S, BASIS * S), jnp.bfloat16),
-            pltpu.VMEM((GROUP, BASIS * S, 4 * S), jnp.bfloat16),
+            pltpu.VMEM((GROUP, BASIS * S, 2 * S), jnp.bfloat16),
             pltpu.SMEM((owners,), jnp.int32),
         ],
         compiler_params=pltpu.CompilerParams(vmem_limit_bytes=60 * 2**20),
         cost_estimate=pl.CostEstimate(flops=2**30, bytes_accessed=16 * 2**20, transcendentals=0),
         name="match",
     )(
-        coefficients.T,
+        jnp.transpose(coefficients, (2, 0, 1)),
         destinations.T,
         jnp.transpose(offsets, (1, 2, 0)),
         basis_rows,
@@ -123,47 +119,38 @@
     )
 
 
-def lines_kernel(dest_ref, off_ref, out_ref):
+def lines_kernel(dest_ref, off_ref, weight_ref, near_ref, told, sems):
+    rows = weight_ref.shape[0]
+    main = pltpu.make_async_copy(weight_ref, near_ref.at[pl.ds(0, rows)], sems.at[0])
+    main.start()
     line = lax.broadcasted_iota(jnp.int32, (META, S), 0)
     lane = lax.broadcasted_iota(jnp.int32, (META, S), 1)
     words = jnp.zeros((META, S), jnp.int32)
-    for block in range(dest_ref.shape[1]):
+    for block in range(rows // S):
         for n in range(2):
             for at, number in enumerate(places(dest_ref, off_ref, block, n)):
                 words = jnp.where((line == n) & (lane == 8 * block + at), number, words)
-    words = words.astype(jnp.float32).astype(jnp.bfloat16)
-    for taker in range(out_ref.shape[0]):
-        out_ref[taker] = words
-
-
-def lines_of(destinations, offsets, takers):
+    told[...] = words.astype(jnp.float32).astype(jnp.bfloat16)
+    tail = pltpu.make_async_copy(told, near_ref.at[pl.ds(rows, META)], sems.at[1])
+    tail.start()
+    main.wait()
+    tail.wait()
+
+
+def with_lines(weight, destinations, offsets):
     smem = pl.BlockSpec(memory_space=pltpu.SMEM)
+    hbm = pl.BlockSpec(memory_space=pltpu.HBM)
+    rows = weight.shape[0] * S
     return pl.pallas_call(
         lines_kernel,
-        out_shape=jax.ShapeDtypeStruct((takers, META, S), jnp.bfloat16),
-        in_specs=[smem, smem],
-        out_specs=pl.BlockSpec(memory_space=pltpu.VMEM),
+        out_shape=jax.ShapeDtypeStruct((rows + META, S), jnp.bfloat16),
+        in_specs=[smem, smem, hbm],
+        out_specs=hbm,
+        scratch_shapes=[pltpu.VMEM((META, S), jnp.bfloat16), pltpu.SemaphoreType.DMA((2,))],
         compiler_params=pltpu.CompilerParams(vmem_limit_bytes=60 * 2**20),
         cost_estimate=pl.CostEstimate(flops=2**16, bytes_accessed=2**22, transcendentals=0),
         name="lines",
-    )(destinations.T, jnp.transpose(offsets, (1, 2, 0)))
-
-
-def held_kernel(large_ref, small_ref, out_ref):
-    pass
-
-
-def held_until(large, small):
-    hbm = pl.BlockSpec(memory_space=pltpu.HBM)
-    return pl.pallas_call(
-        held_kernel,
-        out_shape=jax.ShapeDtypeStruct(large.shape, large.dtype),
-        in_specs=[hbm, hbm],
-        out_specs=hbm,
-        input_output_aliases={0: 0},
-        compiler_params=pltpu.CompilerParams(vmem_limit_bytes=60 * 2**20),
-        name="held_until",
-    )(large, small)
+    )(destinations.T, jnp.transpose(offsets, (1, 2, 0)), weight.reshape(rows, S))
 
 
 def listed(codes, total, queue, idle):
@@ -244,16 +231,19 @@
     )(slots)
 
 
-def band_kernel(where_ref, parts_ref, lines_ref, out_ref, held, canvas, told, codes, queue, sems):
-    sources, count = held.shape[0], held.shape[1] // S
-    patches = out_ref.shape[0]
-    fetch = pltpu.make_async_copy(parts_ref, held, sems.at[0])
+def band_kernel(where_ref, parts_ref, out_ref, held, lines, canvas, told, codes, queue, sems):
+    sources, rows = held.shape[0], held.shape[1]
+    count, patches = rows // S, out_ref.shape[0]
+    ask = pltpu.make_async_copy(parts_ref.at[:, pl.ds(rows, META)], lines, sems.at[2])
+    ask.start()
+    fetch = pltpu.make_async_copy(parts_ref.at[:, pl.ds(0, rows)], held, sems.at[0])
     fetch.start()
     band = where_ref[0] * BAND
     for patch in range(patches):
         for tile in range(P_SIZE // LANES):
             canvas[tile, patch * S + MARGIN : patch * S + MARGIN + BAND, :] = jnp.zeros((BAND, LANES), jnp.float32)
-    notes = lines_ref[...].astype(jnp.float32).astype(jnp.int32)[:, 0:8, :]
+    ask.wait()
+    notes = lines[...].astype(jnp.float32).astype(jnp.int32)[:, 0:8, :]
     notes = notes.reshape(sources * 8, S)
     at = [notes] + [pltpu.roll(notes, S - i, 1) for i in range(1, 5)]
     ahead = band - (at[1] * LANES + at[2])
@@ -286,26 +276,26 @@
             out_ref[patch, :, tile * LANES : (tile + 1) * LANES] = rows.astype(jnp.bfloat16)
 
 
-def place_band(where, parts, lines, patches):
-    sources, rows = parts.shape[0], parts.shape[1]
-    vmem = pl.BlockSpec(memory_space=pltpu.VMEM)
+def place_band(where, parts, patches):
+    sources, rows = parts.shape[0], parts.shape[1] - META
     return pl.pallas_call(
         band_kernel,
         out_shape=jax.ShapeDtypeStruct((patches, BAND, P_SIZE), jnp.bfloat16),
-        in_specs=[pl.BlockSpec(memory_space=pltpu.SMEM), pl.BlockSpec(memory_space=pltpu.HBM), vmem],
-        out_specs=vmem,
+        in_specs=[pl.BlockSpec(memory_space=pltpu.SMEM), pl.BlockSpec(memory_space=pltpu.HBM)],
+        out_specs=pl.BlockSpec(memory_space=pltpu.VMEM),
         scratch_shapes=[
             pltpu.VMEM((sources, rows, S), jnp.bfloat16),
+            pltpu.VMEM((sources, META, S), jnp.bfloat16),
             pltpu.VMEM((P_SIZE // LANES + 1, patches * S, LANES), jnp.float32),
             pltpu.VMEM((sources // 8, 8, S), jnp.int32),
             pltpu.SMEM((sources // 8, 8, S), jnp.int32),
             pltpu.SMEM((2, 2 * sources * (rows // S) + 4), jnp.int32),
-            pltpu.SemaphoreType.DMA((2,)),
+            pltpu.SemaphoreType.DMA((3,)),
         ],
         compiler_params=pltpu.CompilerParams(vmem_limit_bytes=60 * 2**20),
         cost_estimate=pl.CostEstimate(flops=2**24, bytes_accessed=24 * 2**20, transcendentals=0),
         name="place_band",
-    )(where, parts, lines)
+    )(where, parts)
 
 
 def body(blocks, inv_variance, destinations, offsets, coefficients, basis_rows, basis_cols):
@@ -314,15 +304,13 @@
     where = lax.axis_index(("y", "core")).astype(jnp.int32).reshape(1)
     weight = inv_variance[0]
 
-    near = lax.all_gather(weight.reshape(-1, S), ("y", "core"))
-    lines = lines_of(destinations[0], offsets[0], near.shape[0])
-    lines = lax.all_to_all(lines, ("y", "core"), 0, 0, tiled=True)
-    den = place_band(where, near, lines, owners).reshape(along, owners // along, BAND, P_SIZE)
+    near = lax.all_gather(with_lines(weight, destinations[0], offsets[0]), ("y", "core"))
+    den = place_band(where, near, owners).reshape(along, owners // along, BAND, P_SIZE)
     den = lax.psum_scatter(den, "x", scatter_dimension=0, tiled=True)[0]
     den = lax.all_to_all(den, "z", 0, 0, tiled=True)
 
-    slots = match(blocks[0], weight, destinations[0], offsets[0], coefficients[0], basis_rows, basis_cols, owners)
-    slots = lax.all_to_all(held_until(slots, lines), ("x", "z"), 0, 0, tiled=True)
+    slots = match(blocks[0], weight, destinations[0], offsets[0], coefficients, basis_rows, basis_cols, owners)
+    slots = lax.all_to_all(slots, ("x", "z"), 0, 0, tiled=True)
     num = place_whole(slots).reshape(16, BAND, P_SIZE)
     num = lax.all_to_all(num, ("y", "core"), 0, 0, tiled=True)
 

time: 145 us -> 154 us (1.062); the launches traced: 144 us -> 152 us
  Pallas kernels: 20.1 us -> 34.2 us
  starting transfers between devices: 25 us -> 20.8 us
  local copies, waits for them, and re-layouts: 1.92 us -> 0 us
  blocking collectives: 28 us -> 26.1 us
    pallas_call x2 -> x1, Pallas kernels: 1.65 us -> 17.7 us  [with_lines(): pl.pallas_call(lines_kernel, out_shape=jax.ShapeDtypeStruct((rows + META,...]
    all_gather x1, waiting for transfers between devices: 33.6 us -> 45 us  [body(): lax.all_gather(with_lines(weight, destinations[0], offsets[0]), ('y', 'co...]
    all_to_all x2 -> x1, waiting for transfers between devices: 9.75 us -> 0.01 us  [body(): slots = lax.all_to_all(slots, ('x', 'z'), 0, 0, tiled=True)]
    all_to_all x2 -> x1, starting transfers between devices: 21.5 us -> 13.7 us  [body(): slots = lax.all_to_all(slots, ('x', 'z'), 0, 0, tiled=True)]
    all_to_all x1, starting transfers between devices: 3.41 us -> 7.08 us  [body(): den = lax.all_to_all(den, 'z', 0, 0, tiled=True)]
    unnamed x3 -> x0, local copies, waits for them, and re-layouts: 1.92 us -> none
    all_to_all x1, waiting for transfers between devices: 11.2 us -> 9.39 us  [body(): den = lax.all_to_all(den, 'z', 0, 0, tiled=True)]
    pallas_call x1, Pallas kernels: 7.66 us -> 5.82 us  [match(): pl.pallas_call(match_kernel, out_shape=jax.ShapeDtypeStruct((owners, 2 *...]
  transfers between devices with their start and end apart: 5 -> 4, of which waited for: 3 -> 3; matrix products, arithmetic and copies ran while one was open for 1% -> 0% of each run, Pallas kernels for 14% -> 11%
where the time goes in v11:
time: 154 us; the launch traced here: 152 us
  waiting for transfers between devices  56.2 us (36%)
  Pallas kernels  34.2 us (22%)
  blocking collectives  26.1 us (17%)
  starting transfers between devices  20.8 us (14%)
  between operations  13.4 us (9%)
    all_gather x1, waiting for transfers between devices, body(): lax.all_gather(with_lines(weight, destinations[0], offsets[0]), ('y', 'co...  45 us
    all_to_all x1, blocking collectives, body(): num = lax.all_to_all(num, ('y', 'core'), 0, 0, tiled=True)  26.1 us
    pallas_call x1, Pallas kernels, with_lines(): pl.pallas_call(lines_kernel, out_shape=jax.ShapeDtypeStruct((rows + META,...  17.7 us
    all_to_all x1, starting transfers between devices, body(): slots = lax.all_to_all(slots, ('x', 'z'), 0, 0, tiled=True)  13.7 us
    all_to_all x1, waiting for transfers between devices, body(): den = lax.all_to_all(den, 'z', 0, 0, tiled=True)  9.39 us
    pallas_call x1, Pallas kernels, place_band(): pl.pallas_call(band_kernel, out_shape=jax.ShapeDtypeStruct((patches, BAND...  8.53 us
    all_to_all x1, starting transfers between devices, body(): den = lax.all_to_all(den, 'z', 0, 0, tiled=True)  7.08 us
    pallas_call x1, Pallas kernels, match(): pl.pallas_call(match_kernel, out_shape=jax.ShapeDtypeStruct((owners, 2 *...  5.82 us
  transfers between devices with their start and end apart: 4, of which 3 were waited for; matrix products, arithmetic and copies ran while one was open for 0% of the time, Pallas kernels for 11%

profile of v11, /device:TPU:1, one launch (start us, length us, event | category | flops | bytes accessed | tf_op | source)
XLA Modules:
  0.0 151.6 jit_solution(10257580543897183694)
XLA Ops:
  6.5 0.0 all-gather.3.cloned.1.call-start
  6.5 17.7 %lines.1 = bf16[2064,128]{1,0:T(8,128)(2,1)} custom-call(s32[2,16]{1,0:T(2,128)} %bitcast.25, s32[2,2,16]{2,1,0:T(2,128)} %bitcast.23, bf16[2048,128]{1,0:T(8,128)(2,1)} %bitcast.20), custom_call_target="tpu_custom_call" | custom-call | flops 65536 | bytes 4194304 | tf_op jit(solution)/shard_map/lines/pallas_call | solution.py:144
  24.3 0.0 all-gather.3.cloned.1.call-update
  24.3 5.8 %match.1 = bf16[32,272,128]{2,1,0:T(8,128)(2,1)} custom-call(f32[15,1,16]{2,1,0:T(1,128)} %bitcast.28, s32[2,16]{1,0:T(2,128)} %bitcast.26, s32[2,2,16]{2,1,0:T(2,128)} %bitcast.24, bf16[5,41]{1,0:T(8,128)(2,1)} %rows_ref.1, bf16[5,41]{1,0:T(8,128)(2,1)} %cols_ref.1, bf16[16,128,128]{2,1,0:T(8,128)(2,1)} %bitcast.27, bf16[16,128,128]{2,1,0:T(8,128)(2,1)} %bitcast.21), custom_call_target="tpu_custom_call" | custom-call | flops 1073741824 | bytes 16777216 | tf_op jit(solution)/shard_map/match/pallas_call | solution.py:96
  30.1 13.7 %all-to-all-start = ((bf16[32,272,128]{2,1,0:T(8,128)(2,1)}), bf16[32,272,128]{2,1,0:T(8,128)(2,1)S(1)}, u32[]{:S(2)}, u32[]{:S(2)}) async-start(bf16[32,272,128]{2,1,0:T(8,128)(2,1)} %match.1), calls=%async_computation | async-start | bytes 4456448 | tf_op jit(solution)/shard_map/all_to_all | solution.py:313
  43.8 0.0 reduce-scatter.2.cloned.1.call-start
  43.9 45.0 %all-gather.3.cloned.1.call-done = bf16[33024,128]{1,0:T(8,128)(2,1)} async-done(((bf16[2064,128]{1,0:T(8,128)(2,1)}), bf16[33024,128]{1,0:T(8,128)(2,1)}) %all-gather.3.cloned.1.call-update) | async-done | bytes 8454160 | tf_op jit(solution)/shard_map/all_gather | solution.py:307
  88.9 8.5 %place_band.1 = bf16[32,32,512]{2,1,0:T(8,128)(2,1)} custom-call(s32[1]{0:T(128)} %bitcast.8.where_ref, bf16[16,2064,128]{2,1,0:T(8,128)(2,1)} %bitcast.18), custom_call_target="tpu_custom_call" | custom-call | flops 16777216 | bytes 25165824 | tf_op jit(solution)/shard_map/place_band/pallas_call | solution.py:281
  97.4 0.0 reduce-scatter.2.cloned.1.call-update
  97.4 0.0 all-to-all-done.slots_ref
  97.4 2.1 %place_whole.1 = bf16[512,512]{1,0:T(8,128)(2,1)S(1)} custom-call(bf16[32,272,128]{2,1,0:T(8,128)(2,1)S(1)} %all-to-all-done.slots_ref), custom_call_target="tpu_custom_call" | custom-call | flops 8388608 | bytes 16777216 | tf_op jit(solution)/shard_map/place_whole/pallas_call | solution.py:216
  99.6 26.1 %all_to_all.15 = bf16[16,32,512]{2,1,0:T(8,128)(2,1)S(1)} all-to-all(bf16[16,32,512]{2,1,0:T(8,128)(2,1)S(1)} %bitcast.17), channel_id=1, replica_groups=mesh['y'=8,'core'=2,'x'=4,'z'=8] {'y','core'}, dimensions={0} | all-to-all | bytes 1048576 | tf_op jit(solution)/shard_map/all_to_all | solution.py:315
  125.7 1.8 %reduce-scatter.2.cloned.1.call-done = bf16[1,8,32,512]{3,2,1,0:T(8,128)(2,1)} async-done(((bf16[4,8,32,512]{3,2,1,0:T(8,128)(2,1)}), bf16[1,8,32,512]{3,2,1,0:T(8,128)(2,1)}) %reduce-scatter.2.cloned.1.call-update) | async-done | bytes 262160 | tf_op jit(solution)/shard_map/reduce_scatter | solution.py:309
  127.5 7.1 %all-to-all-start.2 = ((bf16[8,32,512]{2,1,0:T(8,128)(2,1)}), bf16[8,32,512]{2,1,0:T(8,128)(2,1)S(1)}, u32[]{:S(2)}, u32[]{:S(2)}) async-start(bf16[8,32,512]{2,1,0:T(8,128)(2,1)} %bitcast.22), calls=%async_computation.3 | async-start | bytes 524288 | tf_op jit(solution)/shard_map/all_to_all | solution.py:310
  134.6 0.1 convert_reduce_fusion
  134.7 9.4 %all-to-all-done.2 = bf16[8,32,512]{2,1,0:T(8,128)(2,1)S(1)} async-done(((bf16[8,32,512]{2,1,0:T(8,128)(2,1)}), bf16[8,32,512]{2,1,0:T(8,128)(2,1)S(1)}, u32[]{:S(2)}, u32[]{:S(2)}) %all-to-all-start.2) | async-done | bytes 262176 | tf_op jit(solution)/shard_map/all_to_all | solution.py:310
  144.1 0.6 divide_bitcast_fusion
  (1 shorter events, 0.0 us)
Async XLA Ops:
  6.5 82.3 %all-gather.3.cloned.1.call-start = ((), (), s32[]{:S(2)}) async-start(), calls=%async_computation.5 | async-start | bytes 8982528 | tf_op jit(solution)/shard_map/all_gather | solution.py:307
  30.1 67.3 %all-to-all-start = ((bf16[32,272,128]{2,1,0:T(8,128)(2,1)}), bf16[32,272,128]{2,1,0:T(8,128)(2,1)S(1)}, u32[]{:S(2)}, u32[]{:S(2)}) async-start(bf16[32,272,128]{2,1,0:T(8,128)(2,1)} %match.1), calls=%async_computation | async-start | bytes 4456448 | tf_op jit(solution)/shard_map/all_to_all | solution.py:313
  43.8 83.7 %reduce-scatter.2.cloned.1.call-start = ((), (), s32[]{:S(2)}) async-start(), calls=%async_computation.4 | async-start | bytes 1310720 | tf_op jit(solution)/shard_map/reduce_scatter | solution.py:309
  127.5 16.6 %all-to-all-start.2 = ((bf16[8,32,512]{2,1,0:T(8,128)(2,1)}), bf16[8,32,512]{2,1,0:T(8,128)(2,1)S(1)}, u32[]{:S(2)}, u32[]{:S(2)}) async-start(bf16[8,32,512]{2,1,0:T(8,128)(2,1)} %bitcast.22), calls=%async_computation.3 | async-start | bytes 524288 | tf_op jit(solution)/shard_map/all_to_all | solution.py:310
Sparse Core Ops, SparseCore 0:
  24.4 64.4 all-gather.2
  97.6 29.9 reduce-scatter.1

commit v12 on v11

--- a/solution.py
+++ b/solution.py
@@ -119,10 +119,10 @@
     )
 
 
-def lines_kernel(dest_ref, off_ref, weight_ref, near_ref, told, sems):
+def lines_kernel(dest_ref, off_ref, weight_ref, near_ref, held, sems):
     rows = weight_ref.shape[0]
-    main = pltpu.make_async_copy(weight_ref, near_ref.at[pl.ds(0, rows)], sems.at[0])
-    main.start()
+    fetch = pltpu.make_async_copy(weight_ref, held.at[pl.ds(0, rows)], sems.at[0])
+    fetch.start()
     line = lax.broadcasted_iota(jnp.int32, (META, S), 0)
     lane = lax.broadcasted_iota(jnp.int32, (META, S), 1)
     words = jnp.zeros((META, S), jnp.int32)
@@ -130,11 +130,11 @@
         for n in range(2):
             for at, number in enumerate(places(dest_ref, off_ref, block, n)):
                 words = jnp.where((line == n) & (lane == 8 * block + at), number, words)
-    told[...] = words.astype(jnp.float32).astype(jnp.bfloat16)
-    tail = pltpu.make_async_copy(told, near_ref.at[pl.ds(rows, META)], sems.at[1])
-    tail.start()
-    main.wait()
-    tail.wait()
+    held[rows : rows + META, :] = words.astype(jnp.float32).astype(jnp.bfloat16)
+    fetch.wait()
+    put = pltpu.make_async_copy(held, near_ref, sems.at[1])
+    put.start()
+    put.wait()
 
 
 def with_lines(weight, destinations, offsets):
@@ -146,7 +146,7 @@
         out_shape=jax.ShapeDtypeStruct((rows + META, S), jnp.bfloat16),
         in_specs=[smem, smem, hbm],
         out_specs=hbm,
-        scratch_shapes=[pltpu.VMEM((META, S), jnp.bfloat16), pltpu.SemaphoreType.DMA((2,))],
+        scratch_shapes=[pltpu.VMEM((rows + META, S), jnp.bfloat16), pltpu.SemaphoreType.DMA((2,))],
         compiler_params=pltpu.CompilerParams(vmem_limit_bytes=60 * 2**20),
         cost_estimate=pl.CostEstimate(flops=2**16, bytes_accessed=2**22, transcendentals=0),
         name="lines",
@@ -161,21 +161,21 @@
         return found + jnp.where(code >= 0, 1, 0)
 
     found = lax.fori_loop(0, total, one, jnp.int32(0), unroll=8)
-    for after in range(4):
+    for after in range(8):
         queue[0, found + after] = idle
         queue[1, found + after] = 0
     return found
 
 
-def add_pieces(queue, found, rows, piece, canvas):
+def add_pieces(queue, found, many, rows, piece, canvas):
     lane = lax.broadcasted_iota(jnp.int32, (rows, LANES), 1)
 
     def some(step, carry):
         values = []
-        for part in range(4):
-            code = queue[0, 4 * step + part]
+        for part in range(many):
+            code = queue[0, many * step + part]
             shift = code & 127
-            value = piece(queue[1, 4 * step + part], ((code >> 7) & 7) * 16)
+            value = piece(queue[1, many * step + part], ((code >> 7) & 7) * 16)
             value = pltpu.roll(value.astype(jnp.float32), shift, 1)
             values.append((code >> 13, (code >> 10) & 7, value, lane >= shift))
         for row, tile, value, here in values:
@@ -183,7 +183,7 @@
             canvas[tile + 1, pl.ds(row, rows), :] += jnp.where(here, 0.0, value)
         return carry
 
-    lax.fori_loop(0, (found + 3) // 4, some, 0)
+    lax.fori_loop(0, (found + many - 1) // many, some, 0)
 
 
 def whole_kernel(slots_ref, out_ref, canvas, told, codes, queue, sem):
@@ -206,7 +206,7 @@
     def piece(i, start):
         return slots_ref[i >> 1, pl.ds(pl.multiple_of((i & 1) * S, S), S), :]
 
-    add_pieces(queue, found, S, piece, canvas)
+    add_pieces(queue, found, 4, S, piece, canvas)
     for tile in range(P_SIZE // LANES):
         out_ref[:, tile * LANES : (tile + 1) * LANES] = canvas[tile].astype(jnp.bfloat16)
 
@@ -222,7 +222,7 @@
             pltpu.VMEM((P_SIZE // LANES + 2, P_SIZE, LANES), jnp.float32),
             pltpu.VMEM((8, S), jnp.int32),
             pltpu.SMEM((8, S), jnp.int32),
-            pltpu.SMEM((2, 2 * sources + 4), jnp.int32),
+            pltpu.SMEM((2, 2 * sources + 8), jnp.int32),
             pltpu.SemaphoreType.DMA,
         ],
         compiler_params=pltpu.CompilerParams(vmem_limit_bytes=8 * 2**20),
@@ -269,7 +269,7 @@
         begin = ((i & 127) >> 3) * S + start
         return held[(i >> 8) * 8 + (i & 7), pl.ds(pl.multiple_of(begin, 16), WINDOW), :]
 
-    add_pieces(queue, found, WINDOW, piece, canvas)
+    add_pieces(queue, found, 8, WINDOW, piece, canvas)
     for patch in range(patches):
         for tile in range(P_SIZE // LANES):
             rows = canvas[tile, patch * S + MARGIN : patch * S + MARGIN + BAND, :]
@@ -289,7 +289,7 @@
             pltpu.VMEM((P_SIZE // LANES + 1, patches * S, LANES), jnp.float32),
             pltpu.VMEM((sources // 8, 8, S), jnp.int32),
             pltpu.SMEM((sources // 8, 8, S), jnp.int32),
-            pltpu.SMEM((2, 2 * sources * (rows // S) + 4), jnp.int32),
+            pltpu.SMEM((2, 2 * sources * (rows // S) + 8), jnp.int32),
             pltpu.SemaphoreType.DMA((3,)),
         ],
         compiler_params=pltpu.CompilerParams(vmem_limit_bytes=60 * 2**20),

time: 154 us -> 137 us (0.89)
  Pallas kernels: 34.2 us -> 18.7 us
    pallas_call x1, Pallas kernels: 17.7 us -> 2.57 us  [with_lines(): pl.pallas_call(lines_kernel, out_shape=jax.ShapeDtypeStruct((rows + META,...]
    all_to_all x1, blocking collectives: 26.1 us -> 24.6 us  [body(): num = lax.all_to_all(num, ('y', 'core'), 0, 0, tiled=True)]
  transfers between devices with their start and end apart: 4 -> 4, of which waited for: 3 -> 3; matrix products, arithmetic and copies ran while one was open for 0% -> 0% of each run, Pallas kernels for 11% -> 12%
where the time goes in v12:
time: 137 us; the launch traced here: 135 us
  waiting for transfers between devices  56.3 us (41%)
  blocking collectives  24.6 us (18%)
  starting transfers between devices  20.9 us (15%)
  Pallas kernels  18.7 us (14%)
  between operations  13.4 us (10%)
    all_gather x1, waiting for transfers between devices, body(): lax.all_gather(with_lines(weight, destinations[0], offsets[0]), ('y', 'co...  45.2 us
    all_to_all x1, blocking collectives, body(): num = lax.all_to_all(num, ('y', 'core'), 0, 0, tiled=True)  24.6 us
    all_to_all x1, starting transfers between devices, body(): slots = lax.all_to_all(slots, ('x', 'z'), 0, 0, tiled=True)  13.7 us
    all_to_all x1, waiting for transfers between devices, body(): den = lax.all_to_all(den, 'z', 0, 0, tiled=True)  9.4 us
    pallas_call x1, Pallas kernels, place_band(): pl.pallas_call(band_kernel, out_shape=jax.ShapeDtypeStruct((patches, BAND...  8.05 us
    all_to_all x1, starting transfers between devices, body(): den = lax.all_to_all(den, 'z', 0, 0, tiled=True)  7.1 us
    pallas_call x1, Pallas kernels, match(): pl.pallas_call(match_kernel, out_shape=jax.ShapeDtypeStruct((owners, 2 *...  5.82 us
  transfers between devices with their start and end apart: 4, of which 3 were waited for; matrix products, arithmetic and copies ran while one was open for 0% of the time, Pallas kernels for 12%

profile of v12, /device:TPU:1, one launch (start us, length us, event | category | flops | bytes accessed | tf_op | source)
XLA Modules:
  0.0 134.6 jit_solution(13169493772226002410)
XLA Ops:
  6.5 0.0 all-gather.3.cloned.1.call-start
  6.5 2.6 %lines.1 = bf16[2064,128]{1,0:T(8,128)(2,1)} custom-call(s32[2,16]{1,0:T(2,128)} %bitcast.25, s32[2,2,16]{2,1,0:T(2,128)} %bitcast.23, bf16[2048,128]{1,0:T(8,128)(2,1)} %bitcast.20), custom_call_target="tpu_custom_call" | custom-call | flops 65536 | bytes 4194304 | tf_op jit(solution)/shard_map/lines/pallas_call | solution.py:144
  9.1 0.0 all-gather.3.cloned.1.call-update
  9.1 5.8 %match.1 = bf16[32,272,128]{2,1,0:T(8,128)(2,1)} custom-call(f32[15,1,16]{2,1,0:T(1,128)} %bitcast.28, s32[2,16]{1,0:T(2,128)} %bitcast.26, s32[2,2,16]{2,1,0:T(2,128)} %bitcast.24, bf16[5,41]{1,0:T(8,128)(2,1)} %rows_ref.1, bf16[5,41]{1,0:T(8,128)(2,1)} %cols_ref.1, bf16[16,128,128]{2,1,0:T(8,128)(2,1)} %bitcast.27, bf16[16,128,128]{2,1,0:T(8,128)(2,1)} %bitcast.21), custom_call_target="tpu_custom_call" | custom-call | flops 1073741824 | bytes 16777216 | tf_op jit(solution)/shard_map/match/pallas_call | solution.py:96
  15.0 13.7 %all-to-all-start = ((bf16[32,272,128]{2,1,0:T(8,128)(2,1)}), bf16[32,272,128]{2,1,0:T(8,128)(2,1)S(1)}, u32[]{:S(2)}, u32[]{:S(2)}) async-start(bf16[32,272,128]{2,1,0:T(8,128)(2,1)} %match.1), calls=%async_computation | async-start | bytes 4456448 | tf_op jit(solution)/shard_map/all_to_all | solution.py:313
  28.7 0.0 reduce-scatter.2.cloned.1.call-start
  28.7 45.2 %all-gather.3.cloned.1.call-done = bf16[33024,128]{1,0:T(8,128)(2,1)} async-done(((bf16[2064,128]{1,0:T(8,128)(2,1)}), bf16[33024,128]{1,0:T(8,128)(2,1)}) %all-gather.3.cloned.1.call-update) | async-done | bytes 8454160 | tf_op jit(solution)/shard_map/all_gather | solution.py:307
  74.0 8.1 %place_band.1 = bf16[32,32,512]{2,1,0:T(8,128)(2,1)} custom-call(s32[1]{0:T(128)} %bitcast.8.where_ref, bf16[16,2064,128]{2,1,0:T(8,128)(2,1)} %bitcast.18), custom_call_target="tpu_custom_call" | custom-call | flops 16777216 | bytes 25165824 | tf_op jit(solution)/shard_map/place_band/pallas_call | solution.py:281
  82.0 0.0 reduce-scatter.2.cloned.1.call-update
  82.0 0.0 all-to-all-done.slots_ref
  82.0 2.3 %place_whole.1 = bf16[512,512]{1,0:T(8,128)(2,1)S(1)} custom-call(bf16[32,272,128]{2,1,0:T(8,128)(2,1)S(1)} %all-to-all-done.slots_ref), custom_call_target="tpu_custom_call" | custom-call | flops 8388608 | bytes 16777216 | tf_op jit(solution)/shard_map/place_whole/pallas_call | solution.py:216
  84.3 24.6 %all_to_all.15 = bf16[16,32,512]{2,1,0:T(8,128)(2,1)S(1)} all-to-all(bf16[16,32,512]{2,1,0:T(8,128)(2,1)S(1)} %bitcast.17), channel_id=1, replica_groups=mesh['y'=8,'core'=2,'x'=4,'z'=8] {'y','core'}, dimensions={0} | all-to-all | bytes 1048576 | tf_op jit(solution)/shard_map/all_to_all | solution.py:315
  108.9 1.6 %reduce-scatter.2.cloned.1.call-done = bf16[1,8,32,512]{3,2,1,0:T(8,128)(2,1)} async-done(((bf16[4,8,32,512]{3,2,1,0:T(8,128)(2,1)}), bf16[1,8,32,512]{3,2,1,0:T(8,128)(2,1)}) %reduce-scatter.2.cloned.1.call-update) | async-done | bytes 262160 | tf_op jit(solution)/shard_map/reduce_scatter | solution.py:309
  110.5 7.1 %all-to-all-start.2 = ((bf16[8,32,512]{2,1,0:T(8,128)(2,1)}), bf16[8,32,512]{2,1,0:T(8,128)(2,1)S(1)}, u32[]{:S(2)}, u32[]{:S(2)}) async-start(bf16[8,32,512]{2,1,0:T(8,128)(2,1)} %bitcast.22), calls=%async_computation.3 | async-start | bytes 524288 | tf_op jit(solution)/shard_map/all_to_all | solution.py:310
  117.6 0.1 convert_reduce_fusion
  117.7 9.4 %all-to-all-done.2 = bf16[8,32,512]{2,1,0:T(8,128)(2,1)S(1)} async-done(((bf16[8,32,512]{2,1,0:T(8,128)(2,1)}), bf16[8,32,512]{2,1,0:T(8,128)(2,1)S(1)}, u32[]{:S(2)}, u32[]{:S(2)}) %all-to-all-start.2) | async-done | bytes 262176 | tf_op jit(solution)/shard_map/all_to_all | solution.py:310
  127.2 0.6 divide_bitcast_fusion
  (1 shorter events, 0.0 us)
Async XLA Ops:
  6.5 67.4 %all-gather.3.cloned.1.call-start = ((), (), s32[]{:S(2)}) async-start(), calls=%async_computation.5 | async-start | bytes 8982528 | tf_op jit(solution)/shard_map/all_gather | solution.py:307
  15.0 67.1 %all-to-all-start = ((bf16[32,272,128]{2,1,0:T(8,128)(2,1)}), bf16[32,272,128]{2,1,0:T(8,128)(2,1)S(1)}, u32[]{:S(2)}, u32[]{:S(2)}) async-start(bf16[32,272,128]{2,1,0:T(8,128)(2,1)} %match.1), calls=%async_computation | async-start | bytes 4456448 | tf_op jit(solution)/shard_map/all_to_all | solution.py:313
  28.7 81.9 %reduce-scatter.2.cloned.1.call-start = ((), (), s32[]{:S(2)}) async-start(), calls=%async_computation.4 | async-start | bytes 1310720 | tf_op jit(solution)/shard_map/reduce_scatter | solution.py:309
  110.5 16.6 %all-to-all-start.2 = ((bf16[8,32,512]{2,1,0:T(8,128)(2,1)}), bf16[8,32,512]{2,1,0:T(8,128)(2,1)S(1)}, u32[]{:S(2)}, u32[]{:S(2)}) async-start(bf16[8,32,512]{2,1,0:T(8,128)(2,1)} %bitcast.22), calls=%async_computation.3 | async-start | bytes 524288 | tf_op jit(solution)/shard_map/all_to_all | solution.py:310
Sparse Core Ops, SparseCore 0:
  9.5 64.4 all-gather.2
  82.2 28.3 reduce-scatter.1

commit v13 on v12

--- a/solution.py
+++ b/solution.py
@@ -153,29 +153,27 @@
     )(destinations.T, jnp.transpose(offsets, (1, 2, 0)), weight.reshape(rows, S))
 
 
-def listed(codes, total, queue, idle):
+def listed(code_of, first, total, queue, idle):
     def one(i, found):
-        code = codes(i)
-        queue[0, found] = code
-        queue[1, found] = i
-        return found + jnp.where(code >= 0, 1, 0)
-
-    found = lax.fori_loop(0, total, one, jnp.int32(0), unroll=8)
+        queue[found] = i
+        return found + jnp.where(code_of(i) >= 0, 1, 0)
+
+    found = lax.fori_loop(first, first + total, one, jnp.int32(0), unroll=16)
     for after in range(8):
-        queue[0, found + after] = idle
-        queue[1, found + after] = 0
+        queue[found + after] = idle
     return found
 
 
-def add_pieces(queue, found, many, rows, piece, canvas):
+def add_pieces(queue, found, code_of, many, rows, piece, canvas):
     lane = lax.broadcasted_iota(jnp.int32, (rows, LANES), 1)
 
     def some(step, carry):
         values = []
         for part in range(many):
-            code = queue[0, many * step + part]
+            number = queue[many * step + part]
+            code = code_of(number)
             shift = code & 127
-            value = piece(queue[1, many * step + part], ((code >> 7) & 7) * 16)
+            value = piece(number, ((code >> 7) & 7) * 16)
             value = pltpu.roll(value.astype(jnp.float32), shift, 1)
             values.append((code >> 13, (code >> 10) & 7, value, lane >= shift))
         for row, tile, value, here in values:
@@ -201,12 +199,18 @@
     for tile in range(P_SIZE // LANES):
         canvas[tile] = jnp.zeros((P_SIZE, LANES), jnp.float32)
     tell.wait()
-    found = listed(lambda i: codes[i & 1, i >> 1], 2 * sources, queue, (P_SIZE // LANES) << 10)
+    codes[0, sources] = (P_SIZE // LANES) << 10
+
+    def code_of(i):
+        return codes[i & 1, i >> 1]
+
+    found = listed(code_of, 0, 2 * sources, queue, 2 * sources)
 
     def piece(i, start):
-        return slots_ref[i >> 1, pl.ds(pl.multiple_of((i & 1) * S, S), S), :]
-
-    add_pieces(queue, found, 4, S, piece, canvas)
+        source = lax.rem(i >> 1, sources)
+        return slots_ref[source, pl.ds(pl.multiple_of((i & 1) * S, S), S), :]
+
+    add_pieces(queue, found, code_of, 4, S, piece, canvas)
     for tile in range(P_SIZE // LANES):
         out_ref[:, tile * LANES : (tile + 1) * LANES] = canvas[tile].astype(jnp.bfloat16)
 
@@ -222,7 +226,7 @@
             pltpu.VMEM((P_SIZE // LANES + 2, P_SIZE, LANES), jnp.float32),
             pltpu.VMEM((8, S), jnp.int32),
             pltpu.SMEM((8, S), jnp.int32),
-            pltpu.SMEM((2, 2 * sources + 8), jnp.int32),
+            pltpu.SMEM((2 * sources + 8,), jnp.int32),
             pltpu.SemaphoreType.DMA,
         ],
         compiler_params=pltpu.CompilerParams(vmem_limit_bytes=8 * 2**20),
@@ -236,12 +240,13 @@
     count, patches = rows // S, out_ref.shape[0]
     ask = pltpu.make_async_copy(parts_ref.at[:, pl.ds(rows, META)], lines, sems.at[2])
     ask.start()
-    fetch = pltpu.make_async_copy(parts_ref.at[:, pl.ds(0, rows)], held, sems.at[0])
-    fetch.start()
+    half = sources // 2
+    fetches = []
+    for part in range(2):
+        taken = pl.ds(part * half, half)
+        fetches.append(pltpu.make_async_copy(parts_ref.at[taken, pl.ds(0, rows)], held.at[taken], sems.at[part]))
+        fetches[-1].start()
     band = where_ref[0] * BAND
-    for patch in range(patches):
-        for tile in range(P_SIZE // LANES):
-            canvas[tile, patch * S + MARGIN : patch * S + MARGIN + BAND, :] = jnp.zeros((BAND, LANES), jnp.float32)
     ask.wait()
     notes = lines[...].astype(jnp.float32).astype(jnp.int32)[:, 0:8, :]
     notes = notes.reshape(sources * 8, S)
@@ -258,18 +263,27 @@
             source = 8 * group + i
             words += pltpu.roll(jnp.where(first, code[8 * source : 8 * source + 8, :], 0), i, 1)
         told[group] = words
-    tell = pltpu.make_async_copy(told, codes, sems.at[1])
+    tell = pltpu.make_async_copy(told, codes.at[pl.ds(0, sources // 8)], sems.at[3])
     tell.start()
+    for patch in range(patches):
+        for tile in range(P_SIZE // LANES):
+            canvas[tile, patch * S + MARGIN : patch * S + MARGIN + BAND, :] = jnp.zeros((BAND, LANES), jnp.float32)
     tell.wait()
-    idle = ((patches - 1) * S + MARGIN + BAND) << 13
-    found = listed(lambda i: codes[i >> 8, (i >> 7) & 1, i & 127], 2 * sources * count, queue, idle)
-    fetch.wait()
+    codes[sources // 8, 0, 0] = ((patches - 1) * S + MARGIN + BAND) << 13
+
+    def code_of(i):
+        return codes[i >> 8, (i >> 7) & 1, i & 127]
 
     def piece(i, start):
         begin = ((i & 127) >> 3) * S + start
-        return held[(i >> 8) * 8 + (i & 7), pl.ds(pl.multiple_of(begin, 16), WINDOW), :]
-
-    add_pieces(queue, found, 8, WINDOW, piece, canvas)
+        return held[lax.rem(i >> 8, sources // 8) * 8 + (i & 7), pl.ds(pl.multiple_of(begin, 16), WINDOW), :]
+
+    for part in range(2):
+        number = half * count * 2
+        first = part * number
+        found = listed(code_of, first, number, queue, 2 * number)
+        fetches[part].wait()
+        add_pieces(queue, found, code_of, 8, WINDOW, piece, canvas)
     for patch in range(patches):
         for tile in range(P_SIZE // LANES):
             rows = canvas[tile, patch * S + MARGIN : patch * S + MARGIN + BAND, :]
@@ -288,9 +302,9 @@
             pltpu.VMEM((sources, META, S), jnp.bfloat16),
             pltpu.VMEM((P_SIZE // LANES + 1, patches * S, LANES), jnp.float32),
             pltpu.VMEM((sources // 8, 8, S), jnp.int32),
-            pltpu.SMEM((sources // 8, 8, S), jnp.int32),
-            pltpu.SMEM((2, 2 * sources * (rows // S) + 8), jnp.int32),
-            pltpu.SemaphoreType.DMA((3,)),
+            pltpu.SMEM((sources // 8 + 1, 8, S), jnp.int32),
+            pltpu.SMEM((2 * sources * (rows // S) + 8,), jnp.int32),
+            pltpu.SemaphoreType.DMA((4,)),
         ],
         compiler_params=pltpu.CompilerParams(vmem_limit_bytes=60 * 2**20),
         cost_estimate=pl.CostEstimate(flops=2**24, bytes_accessed=24 * 2**20, transcendentals=0),

time: 137 us -> 136 us (level)
  transfers between devices with their start and end apart: 4 -> 4, of which waited for: 3 -> 3; matrix products, arithmetic and copies ran while one was open for 0% -> 0% of each run, Pallas kernels for 12% -> 11%
where the time goes in v13:
time: 136 us; the launch traced here: 134 us
  waiting for transfers between devices  56 us (41%)
  blocking collectives  25.4 us (19%)
  starting transfers between devices  20.9 us (15%)
  Pallas kernels  17.7 us (13%)
  between operations  13.4 us (10%)
    all_gather x1, waiting for transfers between devices, body(): lax.all_gather(with_lines(weight, destinations[0], offsets[0]), ('y', 'co...  45.2 us
    all_to_all x1, blocking collectives, body(): num = lax.all_to_all(num, ('y', 'core'), 0, 0, tiled=True)  25.4 us
    all_to_all x1, starting transfers between devices, body(): slots = lax.all_to_all(slots, ('x', 'z'), 0, 0, tiled=True)  13.7 us
    all_to_all x1, waiting for transfers between devices, body(): den = lax.all_to_all(den, 'z', 0, 0, tiled=True)  9.41 us
    pallas_call x1, Pallas kernels, place_band(): pl.pallas_call(band_kernel, out_shape=jax.ShapeDtypeStruct((patches, BAND...  7.17 us
    all_to_all x1, starting transfers between devices, body(): den = lax.all_to_all(den, 'z', 0, 0, tiled=True)  7.15 us
    pallas_call x1, Pallas kernels, match(): pl.pallas_call(match_kernel, out_shape=jax.ShapeDtypeStruct((owners, 2 *...  5.82 us
  transfers between devices with their start and end apart: 4, of which 3 were waited for; matrix products, arithmetic and copies ran while one was open for 0% of the time, Pallas kernels for 11%

profile of v13, /device:TPU:1, one launch (start us, length us, event | category | flops | bytes accessed | tf_op | source)
XLA Modules:
  0.0 134.3 jit_solution(14880916398267523955)
XLA Ops:
  6.5 0.0 all-gather.3.cloned.1.call-start
  6.5 2.6 %lines.1 = bf16[2064,128]{1,0:T(8,128)(2,1)} custom-call(s32[2,16]{1,0:T(2,128)} %bitcast.25, s32[2,2,16]{2,1,0:T(2,128)} %bitcast.23, bf16[2048,128]{1,0:T(8,128)(2,1)} %bitcast.20), custom_call_target="tpu_custom_call" | custom-call | flops 65536 | bytes 4194304 | tf_op jit(solution)/shard_map/lines/pallas_call | solution.py:144
  9.1 0.0 all-gather.3.cloned.1.call-update
  9.1 5.8 %match.1 = bf16[32,272,128]{2,1,0:T(8,128)(2,1)} custom-call(f32[15,1,16]{2,1,0:T(1,128)} %bitcast.28, s32[2,16]{1,0:T(2,128)} %bitcast.26, s32[2,2,16]{2,1,0:T(2,128)} %bitcast.24, bf16[5,41]{1,0:T(8,128)(2,1)} %rows_ref.1, bf16[5,41]{1,0:T(8,128)(2,1)} %cols_ref.1, bf16[16,128,128]{2,1,0:T(8,128)(2,1)} %bitcast.27, bf16[16,128,128]{2,1,0:T(8,128)(2,1)} %bitcast.21), custom_call_target="tpu_custom_call" | custom-call | flops 1073741824 | bytes 16777216 | tf_op jit(solution)/shard_map/match/pallas_call | solution.py:96
  15.0 13.7 %all-to-all-start = ((bf16[32,272,128]{2,1,0:T(8,128)(2,1)}), bf16[32,272,128]{2,1,0:T(8,128)(2,1)S(1)}, u32[]{:S(2)}, u32[]{:S(2)}) async-start(bf16[32,272,128]{2,1,0:T(8,128)(2,1)} %match.1), calls=%async_computation | async-start | bytes 4456448 | tf_op jit(solution)/shard_map/all_to_all | solution.py:327
  28.7 0.0 reduce-scatter.2.cloned.1.call-start
  28.7 45.2 %all-gather.3.cloned.1.call-done = bf16[33024,128]{1,0:T(8,128)(2,1)} async-done(((bf16[2064,128]{1,0:T(8,128)(2,1)}), bf16[33024,128]{1,0:T(8,128)(2,1)}) %all-gather.3.cloned.1.call-update) | async-done | bytes 8454160 | tf_op jit(solution)/shard_map/all_gather | solution.py:321
  74.0 7.2 %place_band.1 = bf16[32,32,512]{2,1,0:T(8,128)(2,1)} custom-call(s32[1]{0:T(128)} %bitcast.8.where_ref, bf16[16,2064,128]{2,1,0:T(8,128)(2,1)} %bitcast.18), custom_call_target="tpu_custom_call" | custom-call | flops 16777216 | bytes 25165824 | tf_op jit(solution)/shard_map/place_band/pallas_call | solution.py:295
  81.1 0.0 reduce-scatter.2.cloned.1.call-update
  81.1 0.0 all-to-all-done.slots_ref
  81.2 2.1 %place_whole.1 = bf16[512,512]{1,0:T(8,128)(2,1)S(1)} custom-call(bf16[32,272,128]{2,1,0:T(8,128)(2,1)S(1)} %all-to-all-done.slots_ref), custom_call_target="tpu_custom_call" | custom-call | flops 8388608 | bytes 16777216 | tf_op jit(solution)/shard_map/place_whole/pallas_call | solution.py:220
  83.3 25.4 %all_to_all.15 = bf16[16,32,512]{2,1,0:T(8,128)(2,1)S(1)} all-to-all(bf16[16,32,512]{2,1,0:T(8,128)(2,1)S(1)} %bitcast.17), channel_id=1, replica_groups=mesh['y'=8,'core'=2,'x'=4,'z'=8] {'y','core'}, dimensions={0} | all-to-all | bytes 1048576 | tf_op jit(solution)/shard_map/all_to_all | solution.py:329
  108.8 1.4 %reduce-scatter.2.cloned.1.call-done = bf16[1,8,32,512]{3,2,1,0:T(8,128)(2,1)} async-done(((bf16[4,8,32,512]{3,2,1,0:T(8,128)(2,1)}), bf16[1,8,32,512]{3,2,1,0:T(8,128)(2,1)}) %reduce-scatter.2.cloned.1.call-update) | async-done | bytes 262160 | tf_op jit(solution)/shard_map/reduce_scatter | solution.py:323
  110.1 7.2 %all-to-all-start.2 = ((bf16[8,32,512]{2,1,0:T(8,128)(2,1)}), bf16[8,32,512]{2,1,0:T(8,128)(2,1)S(1)}, u32[]{:S(2)}, u32[]{:S(2)}) async-start(bf16[8,32,512]{2,1,0:T(8,128)(2,1)} %bitcast.22), calls=%async_computation.3 | async-start | bytes 524288 | tf_op jit(solution)/shard_map/all_to_all | solution.py:324
  117.3 0.1 convert_reduce_fusion
  117.4 9.4 %all-to-all-done.2 = bf16[8,32,512]{2,1,0:T(8,128)(2,1)S(1)} async-done(((bf16[8,32,512]{2,1,0:T(8,128)(2,1)}), bf16[8,32,512]{2,1,0:T(8,128)(2,1)S(1)}, u32[]{:S(2)}, u32[]{:S(2)}) %all-to-all-start.2) | async-done | bytes 262176 | tf_op jit(solution)/shard_map/all_to_all | solution.py:324
  126.8 0.6 divide_bitcast_fusion
  (1 shorter events, 0.0 us)
Async XLA Ops:
  6.5 67.4 %all-gather.3.cloned.1.call-start = ((), (), s32[]{:S(2)}) async-start(), calls=%async_computation.5 | async-start | bytes 8982528 | tf_op jit(solution)/shard_map/all_gather | solution.py:321
  15.0 66.2 %all-to-all-start = ((bf16[32,272,128]{2,1,0:T(8,128)(2,1)}), bf16[32,272,128]{2,1,0:T(8,128)(2,1)S(1)}, u32[]{:S(2)}, u32[]{:S(2)}) async-start(bf16[32,272,128]{2,1,0:T(8,128)(2,1)} %match.1), calls=%async_computation | async-start | bytes 4456448 | tf_op jit(solution)/shard_map/all_to_all | solution.py:327
  28.7 81.4 %reduce-scatter.2.cloned.1.call-start = ((), (), s32[]{:S(2)}) async-start(), calls=%async_computation.4 | async-start | bytes 1310720 | tf_op jit(solution)/shard_map/reduce_scatter | solution.py:323
  110.1 16.6 %all-to-all-start.2 = ((bf16[8,32,512]{2,1,0:T(8,128)(2,1)}), bf16[8,32,512]{2,1,0:T(8,128)(2,1)S(1)}, u32[]{:S(2)}, u32[]{:S(2)}) async-start(bf16[8,32,512]{2,1,0:T(8,128)(2,1)} %bitcast.22), calls=%async_computation.3 | async-start | bytes 524288 | tf_op jit(solution)/shard_map/all_to_all | solution.py:324
Sparse Core Ops, SparseCore 0:
  9.5 64.4 all-gather.2
  81.3 28.8 reduce-scatter.1
